TPU v7x, 32 devices: a whole 2x2x4 slice. The times are simulated.
32 devices in a mesh: dp: 8 (over y, x, core), tensor: 4 (over z).
Axes of the slice: x: 2, y: 2, z: 4, core: 2. Of those that a mesh axis runs over, the one named last changes fastest.
Arguments:
- block_input: float32 [16, 680, 1024], P('dp', 'tensor'), may hold values from -6 to 6
- cotangent: float32 [16, 680, 1024], P('dp', 'tensor'), may hold values from -6 to 6
- class_ids: int32 [16], replicated, may hold values from 0 to 1023
- scale_ids: int32 [16, 680], P('dp'), may hold values from 0 to 9, never falling along the last dimension, each value on 1 to 256 neighbouring positions
- class_table: bfloat16 [1024, 1024], P('dp', 'tensor'), may hold values from -6 to 6
- w_ada: bfloat16 [1024, 6, 1024], P('tensor', None, 'dp'), may hold values from -0.1875 to 0.1875
- b_ada: bfloat16 [6, 1024], P(None, 'dp'), may hold values from -4 to 4
- query_key_value_weight: bfloat16 [3, 1024, 1024], P(None, 'dp', 'tensor'), may hold values from -0.1875 to 0.1875
- qv_bias: bfloat16 [2, 16, 64], P(None, 'tensor', 'dp'), may hold values from -6 to 6
- q_gain: bfloat16 [16, 64], P('tensor', 'dp'), may hold values from 8 to 24
- output_projection: bfloat16 [1024, 1024], P('tensor', 'dp'), may hold values from -0.75 to 0.75
- up_weight: bfloat16 [1024, 4096], P('dp', 'tensor'), may hold values from -0.1875 to 0.1875
- hidden_bias: bfloat16 [64, 64], P('tensor', 'dp'), may hold values from -6 to 6
- down_weight: bfloat16 [4096, 1024], P('tensor', 'dp'), may hold values from -0.09375 to 0.09375
- projection_bias: bfloat16 [2, 1024], P(None, 'dp'), may hold values from -6 to 6
Outputs:
- block_output: float32 [16, 680, 1024], P('dp', 'tensor')
- input_grad: float32 [16, 680, 1024], P('dp', 'tensor')
- table_grad: float32 [1024, 1024], P('dp', 'tensor')
- w_ada_grad: float32 [1024, 6, 1024], P('tensor', None, 'dp')
- b_ada_grad: float32 [6, 1024], P(None, 'dp')
- w_qkv_grad: float32 [3, 1024, 1024], P(None, 'dp', 'tensor')
- qv_bias_grad: float32 [2, 16, 64], P(None, 'tensor', 'dp')
- q_gain_grad: float32 [16, 64], P('tensor', 'dp')
- w_proj_grad: float32 [1024, 1024], P('tensor', 'dp')
- w_fc1_grad: float32 [1024, 4096], P('dp', 'tensor')
- b_fc1_grad: float32 [64, 64], P('tensor', 'dp')
- w_fc2_grad: float32 [4096, 1024], P('tensor', 'dp')
- b_out_grad: float32 [2, 1024], P(None, 'dp')
Inputs may be any that keep to these rules, and one draw needn't show every extreme that they name: `scale_ids`: in each sequence the scale ids never fall, every one of the 10 scales holds 1 to 256 tokens, and some scale holds exactly 256.
All inputs are finite; a program needn't handle non-finite values.
Results may differ from a plain program's by a relative error of at most 0.015.
Values may be sent and summed in bfloat16 or wider, within the bound.
A program may use at most 192 MiB of HBM per device.

v0:
```python
import jax
import jax.numpy as jnp
from jax import lax
from jax.sharding import PartitionSpec as P

MICRO = 2


highest_precision = lax.Precision.HIGHEST


def modulate(tokens, scale_in, shift_in):
    centred = tokens - jnp.mean(tokens, axis=-1, keepdims=True)
    spread = jnp.mean(centred * centred, axis=-1, keepdims=True)
    return centred * lax.rsqrt(spread + 1e-06) * (1.0 + scale_in) + shift_in


def gelu_tanh(values):
    return jax.nn.gelu(values, approximate=True)


def qk_norm(queries, key_rows, q_scales):
    q_hat = queries * lax.rsqrt(jnp.sum(queries * queries, axis=-1, keepdims=True) + 1e-06)
    k_hat = key_rows * lax.rsqrt(jnp.sum(key_rows * key_rows, axis=-1, keepdims=True) + 1e-06)
    return (q_hat * q_scales, k_hat)


def attend(operands, allowed):
    q_head, k_head, v_head = operands
    scores = jnp.einsum("sqd,skd->sqk", q_head, k_head, preferred_element_type=jnp.float32)
    scores = jnp.where(allowed, scores, -1e30)
    peak = jnp.max(scores, axis=-1, keepdims=True)
    expo_vals = jnp.exp(scores - peak)
    row_totals = jnp.sum(expo_vals, axis=-1, keepdims=True)
    weights = (expo_vals / row_totals).astype(jnp.bfloat16)
    mixed = jnp.einsum("sqk,skd->sqd", weights, v_head, preferred_element_type=jnp.float32)
    return (mixed, peak + jnp.log(row_totals))


def attend_back(operands, allowed):
    q_head, k_head, v_head, d_mixed, log_total = operands
    scores = jnp.einsum("sqd,skd->sqk", q_head, k_head, preferred_element_type=jnp.float32)
    weights = jnp.where(allowed, jnp.exp(jnp.where(allowed, scores, -1e30) - log_total), 0.0)
    d_weights = jnp.einsum("sqd,skd->sqk", d_mixed, v_head, preferred_element_type=jnp.float32)
    d_values = jnp.einsum(
        "sqk,sqd->skd", weights.astype(jnp.bfloat16), d_mixed, preferred_element_type=jnp.float32
    )
    d_scores = (
        weights * (d_weights - jnp.sum(weights * d_weights, axis=-1, keepdims=True))
    ).astype(jnp.bfloat16)
    d_query = jnp.einsum("sqk,skd->sqd", d_scores, k_head, preferred_element_type=jnp.float32)
    d_keys = jnp.einsum("sqk,sqd->skd", d_scores, q_head, preferred_element_type=jnp.float32)
    return (d_query, d_keys, d_values)


def local(
    block_input,
    cotangent,
    class_ids,
    scale_ids,
    class_table,
    w_ada,
    b_ada,
    query_key_value_weight,
    qv_bias,
    q_gain,
    output_projection,
    up_weight,
    hidden_bias,
    down_weight,
    projection_bias,
):
    local_seqs = block_input.shape[0]
    per_micro = local_seqs // MICRO
    length = scale_ids.shape[1]
    my_classes = lax.dynamic_slice_in_dim(class_ids, lax.axis_index("dp") * local_seqs, local_seqs)
    single_float = jnp.float32
    b16 = jnp.bfloat16
    gathered = None
    accum = None
    outputs = []
    input_grads = []
    for micro_step in range(MICRO):
        gathered = (
            lax.all_gather(class_table, "dp", axis=0, tiled=True),
            lax.all_gather(w_ada, "dp", axis=2, tiled=True),
            lax.all_gather(b_ada, "dp", axis=1, tiled=True),
            lax.all_gather(query_key_value_weight, "dp", axis=1, tiled=True),
            lax.all_gather(qv_bias, "dp", axis=2, tiled=True),
            lax.all_gather(q_gain, "dp", axis=1, tiled=True),
            lax.all_gather(output_projection, "dp", axis=1, tiled=True),
            lax.all_gather(up_weight, "dp", axis=0, tiled=True),
            lax.all_gather(hidden_bias, "dp", axis=1, tiled=True),
            lax.all_gather(down_weight, "dp", axis=1, tiled=True),
            lax.all_gather(projection_bias, "dp", axis=1, tiled=True),
        )
        (
            table_all,
            ada_all,
            ada_bias,
            query_key_value_total,
            qv_all,
            gain_all,
            projection_total,
            up_weight_total,
            fc1_bias,
            down_weight_total,
            out_bias,
        ) = gathered
        lower = micro_step * per_micro
        rows_in = block_input[lower : lower + per_micro]
        grad_in = cotangent[lower : lower + per_micro]
        labels = my_classes[lower : lower + per_micro]
        scale_rows = scale_ids[lower : lower + per_micro]
        allowed = scale_rows[:, :, None] >= scale_rows[:, None, :]
        cond = jnp.take(table_all, labels, axis=0).astype(single_float)
        silu_vals, silu_back = jax.vjp(jax.nn.silu, cond)
        silu_low = silu_vals.astype(b16)
        partial_mod = jnp.einsum(
            "sc,cjd->sjd", silu_low, ada_all, preferred_element_type=single_float
        )
        modulation = lax.psum(partial_mod, "tensor") + ada_bias.astype(single_float)
        gamma_one = modulation[:, 0][:, None, :]
        gamma_two = modulation[:, 1][:, None, :]
        scale_one = modulation[:, 2][:, None, :]
        scale_two = modulation[:, 3][:, None, :]
        shift_one = modulation[:, 4][:, None, :]
        shift_two = modulation[:, 5][:, None, :]
        normed_one, norm_one_back = jax.vjp(modulate, rows_in, scale_one, shift_one)
        first_residual = lax.all_gather(normed_one.astype(b16), "tensor", axis=1, tiled=True)
        query_key_value_rows = jnp.einsum(
            "zug,hgn->hzun",
            first_residual,
            query_key_value_total,
            preferred_element_type=single_float,
        )
        head_count, head_size = gain_all.shape
        shaped = (per_micro, length, head_count, head_size)
        qv_rows = qv_all.astype(single_float).reshape(2, -1)
        queries = (query_key_value_rows[0] + qv_rows[0]).reshape(shaped)
        key_rows = query_key_value_rows[1].reshape(shaped)
        value_rows = (query_key_value_rows[2] + qv_rows[1]).reshape(shaped)
        (q_scaled, k_hat), norm_back = jax.vjp(
            qk_norm, queries, key_rows, gain_all.astype(single_float)
        )
        q_heads = jnp.moveaxis(q_scaled.astype(b16), 2, 0)
        k_heads = jnp.moveaxis(k_hat.astype(b16), 2, 0)
        v_heads = jnp.moveaxis(value_rows.astype(b16), 2, 0)
        head_out, log_total = lax.map(
            lambda operands: attend(operands, allowed), (q_heads, k_heads, v_heads)
        )
        attention_result = jnp.moveaxis(head_out, 0, 2).reshape(per_micro, length, -1).astype(b16)
        branch_partials = jnp.einsum(
            "yxi,it->yxt", attention_result, projection_total, preferred_element_type=single_float
        )
        branch_output = lax.psum_scatter(
            branch_partials.astype(jnp.bfloat16), "tensor", scatter_dimension=1, tiled=True
        ).astype(jnp.float32) + out_bias[0].astype(single_float)
        middle = rows_in + gamma_one * branch_output
        normed_two, norm_two_back = jax.vjp(modulate, middle, scale_two, shift_two)
        second_residual = lax.all_gather(normed_two.astype(b16), "tensor", axis=1, tiled=True)
        hidden_units = jnp.einsum(
            "ahi,ir->ahr", second_residual, up_weight_total, preferred_element_type=single_float
        ) + fc1_bias.astype(single_float).reshape(-1)
        act_vals, gelu_back = jax.vjp(gelu_tanh, hidden_units)
        activation_lowprec = act_vals.astype(b16)
        feedforward_partials = jnp.einsum(
            "xmt,ti->xmi",
            activation_lowprec,
            down_weight_total,
            preferred_element_type=single_float,
        )
        feedforward_output = lax.psum_scatter(
            feedforward_partials.astype(jnp.bfloat16), "tensor", scatter_dimension=1, tiled=True
        ).astype(jnp.float32) + out_bias[1].astype(single_float)
        outputs.append(middle + gamma_two * feedforward_output)
        gathered = (
            lax.all_gather(class_table, "dp", axis=0, tiled=True),
            lax.all_gather(w_ada, "dp", axis=2, tiled=True),
            lax.all_gather(b_ada, "dp", axis=1, tiled=True),
            lax.all_gather(query_key_value_weight, "dp", axis=1, tiled=True),
            lax.all_gather(qv_bias, "dp", axis=2, tiled=True),
            lax.all_gather(q_gain, "dp", axis=1, tiled=True),
            lax.all_gather(output_projection, "dp", axis=1, tiled=True),
            lax.all_gather(up_weight, "dp", axis=0, tiled=True),
            lax.all_gather(hidden_bias, "dp", axis=1, tiled=True),
            lax.all_gather(down_weight, "dp", axis=1, tiled=True),
            lax.all_gather(projection_bias, "dp", axis=1, tiled=True),
        )
        (
            table_all,
            ada_all,
            ada_bias,
            query_key_value_total,
            qv_all,
            gain_all,
            projection_total,
            up_weight_total,
            fc1_bias,
            down_weight_total,
            out_bias,
        ) = gathered
        d_gamma_two = jnp.sum(grad_in * feedforward_output, axis=1)
        d_ffn = (gamma_two * grad_in).astype(b16)
        d_out_two = jnp.sum(d_ffn.astype(single_float), axis=1)
        feedforward_grad_total = lax.all_gather(d_ffn, "tensor", axis=1, tiled=True)
        down_weight_grad = jnp.einsum(
            "bci,bcw->iw",
            activation_lowprec,
            feedforward_grad_total,
            preferred_element_type=single_float,
        )
        activation_grad = jnp.einsum(
            "oyz,qz->oyq",
            feedforward_grad_total,
            down_weight_total,
            preferred_element_type=single_float,
        )
        (d_hidden_full,) = gelu_back(activation_grad)
        hidden_grad = d_hidden_full.astype(b16)
        g_fc1_bias = jnp.sum(hidden_grad.astype(single_float), axis=(0, 1)).reshape(fc1_bias.shape)
        up_weight_grad = jnp.einsum(
            "jtw,jtp->wp", second_residual, hidden_grad, preferred_element_type=single_float
        )
        second_grad_partials = jnp.einsum(
            "wnh,xh->wnx", hidden_grad, up_weight_total, preferred_element_type=single_float
        )
        d_two = lax.psum_scatter(
            second_grad_partials.astype(jnp.bfloat16), "tensor", scatter_dimension=1, tiled=True
        ).astype(jnp.float32)
        d_mid_norm, d_scale_two, d_shift_two = norm_two_back(d_two)
        d_middle = grad_in + d_mid_norm
        d_gamma_one = jnp.sum(d_middle * branch_output, axis=1)
        d_branch = (gamma_one * d_middle).astype(b16)
        d_out_one = jnp.sum(d_branch.astype(single_float), axis=1)
        branch_grad_total = lax.all_gather(d_branch, "tensor", axis=1, tiled=True)
        projection_grad = jnp.einsum(
            "mxk,mxb->kb", attention_result, branch_grad_total, preferred_element_type=single_float
        )
        d_attended = (
            jnp.einsum(
                "cir,or->cio",
                branch_grad_total,
                projection_total,
                preferred_element_type=single_float,
            )
            .astype(b16)
            .reshape(shaped)
        )
        d_q_heads, d_k_heads, d_v_heads = lax.map(
            lambda operands: attend_back(operands, allowed),
            (q_heads, k_heads, v_heads, jnp.moveaxis(d_attended, 2, 0), log_total),
        )
        d_queries, d_keys, g_gain = norm_back(
            (jnp.moveaxis(d_q_heads, 0, 2), jnp.moveaxis(d_k_heads, 0, 2))
        )
        query_key_value_grad = (
            jnp.stack([d_queries, d_keys, jnp.moveaxis(d_v_heads, 0, 2)])
            .reshape(3, per_micro, length, -1)
            .astype(b16)
        )
        g_qv = jnp.sum(query_key_value_grad[::2].astype(single_float), axis=(1, 2)).reshape(
            qv_all.shape
        )
        query_key_value_weight_grad = jnp.einsum(
            "gty,zgta->zya",
            first_residual,
            query_key_value_grad,
            preferred_element_type=single_float,
        )
        first_grad_partials = jnp.einsum(
            "mypa,mka->ypk",
            query_key_value_grad,
            query_key_value_total,
            preferred_element_type=single_float,
        )
        d_one = lax.psum_scatter(
            first_grad_partials.astype(jnp.bfloat16), "tensor", scatter_dimension=1, tiled=True
        ).astype(jnp.float32)
        d_rows_norm, d_scale_one, d_shift_one = norm_one_back(d_one)
        input_grads.append(d_middle + d_rows_norm)
        per_sequence = jnp.stack(
            [
                d_gamma_one,
                d_gamma_two,
                d_scale_one[:, 0],
                d_scale_two[:, 0],
                d_shift_one[:, 0],
                d_shift_two[:, 0],
                d_out_one,
                d_out_two,
            ],
            axis=1,
        )
        seq_totals = lax.psum(per_sequence.astype(jnp.bfloat16), "tensor").astype(jnp.float32)
        d_mod = seq_totals[:, :6].astype(b16)
        g_ada_bias = jnp.sum(d_mod.astype(single_float), axis=0)
        g_out_bias = jnp.sum(seq_totals[:, 6:], axis=0)
        g_ada = jnp.einsum("sc,sjd->cjd", silu_low, d_mod, preferred_element_type=single_float)
        d_silu = jnp.einsum("sjd,cjd->sc", d_mod, ada_all, preferred_element_type=single_float)
        (d_cond,) = silu_back(d_silu)
        one_hot = (
            labels[:, None] == jnp.arange(table_all.shape[0], dtype=jnp.int32)[None, :]
        ).astype(single_float)
        g_table = jnp.dot(
            one_hot.T, d_cond, precision=highest_precision, preferred_element_type=single_float
        )
        terms = (
            g_table,
            g_ada,
            g_ada_bias,
            query_key_value_weight_grad,
            g_qv,
            g_gain,
            projection_grad,
            up_weight_grad,
            g_fc1_bias,
            down_weight_grad,
            g_out_bias,
        )
        if accum is None:
            accum = terms
        else:
            accum = tuple((older + newer for older, newer in zip(accum, terms)))
    block_output = jnp.concatenate(outputs, axis=0)
    input_grad = jnp.concatenate(input_grads, axis=0)
    reduced = (
        lax.psum_scatter(accum[0], "dp", scatter_dimension=0, tiled=True),
        lax.psum_scatter(accum[1], "dp", scatter_dimension=2, tiled=True),
        lax.psum_scatter(accum[2], "dp", scatter_dimension=1, tiled=True),
        lax.psum_scatter(accum[3], "dp", scatter_dimension=1, tiled=True),
        lax.psum_scatter(accum[4], "dp", scatter_dimension=2, tiled=True),
        lax.psum_scatter(accum[5], "dp", scatter_dimension=1, tiled=True),
        lax.psum_scatter(accum[6], "dp", scatter_dimension=1, tiled=True),
        lax.psum_scatter(accum[7], "dp", scatter_dimension=0, tiled=True),
        lax.psum_scatter(accum[8], "dp", scatter_dimension=1, tiled=True),
        lax.psum_scatter(accum[9], "dp", scatter_dimension=1, tiled=True),
        lax.psum_scatter(accum[10], "dp", scatter_dimension=1, tiled=True),
    )
    return (
        block_output,
        input_grad,
        reduced[0],
        reduced[1],
        reduced[2],
        reduced[3],
        reduced[4],
        reduced[5],
        reduced[6],
        reduced[7],
        reduced[8],
        reduced[9],
        reduced[10],
    )


def solution(mesh):
    return jax.shard_map(
        local,
        mesh=mesh,
        in_specs=(
            P("dp", "tensor", None),
            P("dp", "tensor", None),
            P(),
            P("dp", None),
            P("dp", "tensor"),
            P("tensor", None, "dp"),
            P(None, "dp"),
            P(None, "dp", "tensor"),
            P(None, "tensor", "dp"),
            P("tensor", "dp"),
            P("tensor", "dp"),
            P("dp", "tensor"),
            P("tensor", "dp"),
            P("tensor", "dp"),
            P(None, "dp"),
        ),
        out_specs=(
            P("dp", "tensor", None),
            P("dp", "tensor", None),
            P("dp", "tensor"),
            P("tensor", None, "dp"),
            P(None, "dp"),
            P(None, "dp", "tensor"),
            P(None, "tensor", "dp"),
            P("tensor", "dp"),
            P("tensor", "dp"),
            P("dp", "tensor"),
            P("tensor", "dp"),
            P("tensor", "dp"),
            P(None, "dp"),
        ),
        check_vma=False,
    )
```

profile of v0, /device:TPU:24, one launch (start us, length us, event | category | flops | bytes accessed | tf_op | source)
XLA Modules:
  0.0 1435.7 jit_solution(411415383068108795)
XLA Ops:
  14.2 9.0 all_gather.80
  23.3 10.7 all_gather.38
  37.6 4.7 multiply_reduce_fusion.23
  47.8 16.1 %all-reduce.20 = (f32[1,6,1024]{2,1,0:T(8,128)S(1)}, f32[1,6,1024]{2,1,0:T(8,128)S(1)}) all-reduce(f32[1,6,1024]{2,1,0:T(8,128)S(1)} %copy.292, f32[1,6,1024]{2,1,0:T(8,128)S(1)} %copy.291), channel_id=1, replica_groups=mesh['dp'=8,'tensor'=4] {'tensor'}, use_global_device_ids=true, to_apply=%region_13.15 | all-reduce | flops 12288 | bytes 98304 | tf_op jit(solution)/shard_map/psum | solution.py:122
  71.2 9.4 all_gather.86
  80.5 8.2 all-gather
  89.4 9.0 all_gather.83
  99.8 10.3 all_gather.85
  110.1 18.4 %all-gather.16.cloned.1.call-done = bf16[1,680,1024]{2,0,1:T(2,128)(2,1)} async-done(((bf16[1,170,1024]{2,0,1:T(2,128)(2,1)}), bf16[1,680,1024]{2,0,1:T(2,128)(2,1)}) %all-gather.16.cloned.1.call-update) | async-done | bytes 1392656 | tf_op jit(solution)/shard_map/all_gather | solution.py:130
  134.5 52.4 %all-gather.26.cloned.1.call-done = bf16[1,680,1024]{2,0,1:T(2,128)(2,1)} async-done(((bf16[1,170,1024]{2,0,1:T(2,128)(2,1)}), bf16[1,680,1024]{2,0,1:T(2,128)(2,1)}) %all-gather.26.cloned.1.call-update) | async-done | bytes 1392656 | tf_op jit(solution)/shard_map/all_gather | solution.py:130
  186.9 3.6 convolution_bitcast_fusion.8
  208.9 17.9 %while.57 = (s32[]{:T(128)}, bf16[4,1,680,64]{2,3,1,0:T(8,128)(2,1)}, f32[4,1,680,1]{2,3,1,0:T(1,128)}, bf16[4,1,680,64]{3,2,1,0:T(8,128)(2,1)}, bf16[4,1,680,64...) while((s32[]{:T(128)}, ...), condition=%wide.region_8.10_spmd.clone, body=%wide.region_5.0_spmd.clone.sunk | while | flops 123922520 | bytes 9343897 | solution.py:149
  229.6 17.9 %while.58 = (s32[]{:T(128)}, bf16[4,1,680,64]{2,3,1,0:T(8,128)(2,1)}, f32[4,1,680,1]{2,3,1,0:T(1,128)}, bf16[4,1,680,64]{3,2,1,0:T(8,128)(2,1)}, bf16[4,1,680,64...) while((s32[]{:T(128)}, ...), condition=%wide.region_21.23_spmd.clone, body=%wide.region_18.22_spmd.clone.sunk | while | flops 123922520 | bytes 9343897 | solution.py:149
  252.0 53.1 %fusion.222 = (bf16[176,1024]{1,0:T(8,128)(2,1)}, bf16[176,1024]{1,0:T(8,128)(2,1)}) fusion(bf16[1,680,1024]{2,1,0:T(8,128)(2,1)} %fusion.105, bf16[1,680,1024]{2,1,0:T(8,128)(2,1)} %fusion.104), kind=kCustom, calls=%all-reduce-scatter.10 | all-reduce-scatter fusion | flops 1441793 | bytes 3506688
  314.6 4.6 concatenate.51
  319.2 4.6 concatenate.53
  326.3 5.5 fusion.235
  338.3 4.7 fusion.223
  350.5 10.2 all_gather.89
  363.7 32.3 %all-gather.20.cloned.1.call-done = bf16[1,680,1024]{2,0,1:T(2,128)(2,1)} async-done(((bf16[1,170,1024]{2,0,1:T(2,128)(2,1)}), bf16[1,680,1024]{2,0,1:T(2,128)(2,1)}) %all-gather.20.cloned.1.call-update) | async-done | bytes 1392656 | tf_op jit(solution)/shard_map/all_gather | solution.py:161
  396.0 5.7 fusion.132
  401.6 25.7 %all-gather.24.cloned.1.call-done = bf16[1024,1024]{1,0:T(8,128)(2,1)} async-done(((bf16[1024,128]{1,0:T(8,128)(2,1)}), bf16[1024,1024]{1,0:T(8,128)(2,1)}) %all-gather.24.cloned.1.call-update) | async-done | bytes 2097168 | tf_op jit(solution)/shard_map/all_gather | solution.py:94
  427.3 57.2 %all-gather.30.cloned.1.call-done = bf16[1,680,1024]{2,0,1:T(2,128)(2,1)} async-done(((bf16[1,170,1024]{2,0,1:T(2,128)(2,1)}), bf16[1,680,1024]{2,0,1:T(2,128)(2,1)}) %all-gather.30.cloned.1.call-update) | async-done | bytes 1392656 | tf_op jit(solution)/shard_map/all_gather | solution.py:206
  484.5 7.3 convert_reduce_fusion.1
  495.6 47.3 %all-gather.28.cloned.1.call-done = bf16[1,680,1024]{2,0,1:T(2,128)(2,1)} async-done(((bf16[1,170,1024]{2,0,1:T(2,128)(2,1)}), bf16[1,680,1024]{2,0,1:T(2,128)(2,1)}) %all-gather.28.cloned.1.call-update) | async-done | bytes 1392656 | tf_op jit(solution)/shard_map/all_gather | solution.py:161
  542.9 5.7 fusion.117
  548.6 52.0 %all-gather.34.cloned.1.call-done = bf16[1,680,1024]{2,0,1:T(2,128)(2,1)} async-done(((bf16[1,170,1024]{2,0,1:T(2,128)(2,1)}), bf16[1,680,1024]{2,0,1:T(2,128)(2,1)}) %all-gather.34.cloned.1.call-update) | async-done | bytes 1392656 | tf_op jit(solution)/shard_map/all_gather | solution.py:206
  600.6 7.3 convert_reduce_fusion
  611.8 53.3 %fusion.221 = (bf16[176,1024]{1,0:T(8,128)(2,1)}, bf16[176,1024]{1,0:T(8,128)(2,1)}) fusion(bf16[1,680,1024]{2,1,0:T(8,128)(2,1)} %fusion.111, bf16[1,680,1024]{2,1,0:T(8,128)(2,1)} %fusion.110), kind=kCustom, calls=%all-reduce-scatter.9 | all-reduce-scatter fusion | flops 1441793 | bytes 3506688
  672.0 4.6 concatenate.55
  678.4 4.4 multiply_reduce_fusion.12
  683.5 4.1 fusion.233
  688.2 4.6 concatenate.57
  694.7 4.5 multiply_reduce_fusion.8
  699.8 3.9 fusion.234
  703.7 4.6 fusion.224
  710.5 5.6 fusion.108
  723.3 41.8 %all-gather.32.cloned.1.call-done = bf16[1,680,1024]{2,0,1:T(2,128)(2,1)} async-done(((bf16[1,170,1024]{2,0,1:T(2,128)(2,1)}), bf16[1,680,1024]{2,0,1:T(2,128)(2,1)}) %all-gather.32.cloned.1.call-update) | async-done | bytes 1392656 | tf_op jit(solution)/shard_map/all_gather | solution.py:236
  772.1 30.3 %while.59 = (s32[]{:T(128)}, f32[4,1,680,64]{2,3,1,0:T(8,128)}, f32[4,1,680,64]{2,3,1,0:T(8,128)}, bf16[4,1,680,64]{2,3,1,0:T(8,128)(2,1)}, bf16[4,1,680,64]{3,2...) while((s32[]{:T(128)}, f32[4,1,680,64]{2,3,1,0:T(8,128)}, ...), condition=%wide.region_31.33_spmd.clone, body=%wide.region_29.32_spmd.clone.sunk | while | flops 300559328 | bytes 21845992 | solution.py:250
  806.0 16.8 %all-gather.36.cloned.1.call-done = bf16[1,680,1024]{2,0,1:T(2,128)(2,1)} async-done(((bf16[1,170,1024]{2,0,1:T(2,128)(2,1)}), bf16[1,680,1024]{2,0,1:T(2,128)(2,1)}) %all-gather.36.cloned.1.call-update) | async-done | bytes 1392656 | tf_op jit(solution)/shard_map/all_gather | solution.py:236
  829.8 27.7 %while.60 = (s32[]{:T(128)}, f32[4,1,680,64]{2,3,1,0:T(8,128)}, f32[4,1,680,64]{2,3,1,0:T(8,128)}, bf16[4,1,680,64]{2,3,1,0:T(8,128)(2,1)S(1)}, bf16[4,1,680,64]...) while((s32[]{:T(128)}, f32[4,1,680,64]{2,3,1,0:T(8,128)}, ...), condition=%wide.region_42.44_spmd.clone, body=%wide.region_40.43_spmd.clone.sunk | while | flops 300559328 | bytes 17667988 | solution.py:250
  863.6 3.9 fusion.107
  870.0 100.1 %fusion.220 = (bf16[176,1024]{1,0:T(8,128)(2,1)S(1)}, bf16[176,1024]{1,0:T(8,128)(2,1)S(1)}, bf16[176,1024]{1,0:T(8,128)(2,1)S(1)}, bf16[176,1024]{1,0:T(8,128)(2,1)S(1)}) fusion(bf16[1,680,1024]{2,1,0:T(8,128)(2,1)} %fusion.109, bf16[1,680,1024]{2,1,0:T(8,128)(2,1)} %fusion.108, bf16[1,680,1024]{2,1,0:T(8,128)(2,1)} %fusion.107, ...), kind=kCustom, calls=%all-reduce-scatter.8 | all-reduce-scatter fusion | flops 2883585 | bytes 7012864
  977.1 5.0 fusion.134
  992.3 5.2 fusion.231
  997.6 5.3 multiply_reduce_fusion.15
  1003.0 4.8 concatenate.52
  1017.2 4.2 concatenate.54
  1022.6 4.5 multiply_reduce_fusion.14
  1028.7 21.8 %all-reduce.21 = (bf16[1,8,1024]{2,1,0:T(8,128)(2,1)S(1)}, bf16[1,8,1024]{2,1,0:T(8,128)(2,1)S(1)}) all-reduce(bf16[1,8,1024]{2,1,0:T(8,128)(2,1)S(1)} %stack.111, bf16[1,8,1024]{2,1,0:T(8,128)(2,1)S(1)} %stack.102), channel_id=1, replica_groups=mesh['dp'=8,'tensor'=4] {'tensor'}, use_global_device_ids=true, to_apply=%region_65.67 | all-reduce | flops 16384 | bytes 65536 | tf_op jit(solution)/shard_map/psum | solution.py:295
  1051.7 6.2 add_bitcast_fusion
  1063.0 4.0 fusion.143
  1075.0 4.4 fusion.130
  1079.4 4.0 convolution_add_fusion.1
  1085.3 4.3 fusion.137
  1089.6 4.4 convolution_add_fusion
  1101.5 22.8 %all-reduce.19 = (f32[2,4,64]{2,1,0:T(4,128)S(1)}, f32[4,64]{1,0:T(4,128)S(1)}, f32[16,64]{1,0:T(8,128)S(1)}) all-reduce(f32[2,4,64]{2,1,0:T(4,128)S(1)} %add.562, f32[4,64]{1,0:T(4,128)S(1)} %add.563, f32[16,64]{1,0:T(8,128)S(1)} %add.567), channel_id=14, replica_groups=mesh['dp'=8,'tensor'=4] {'dp'}, use_global_device_ids=true, to_apply=%region_72.74.clone | all-reduce | flops 1792 | bytes 14336
  1132.5 4.5 reduce-scatter.44.cloned.1.call-done
  1138.9 32.8 %reduce-scatter.42.cloned.1.call-done = f32[6,128]{1,0:T(8,128)} async-done(((f32[6,1024]{1,0:T(8,128)}), f32[6,128]{1,0:T(8,128)}) %reduce-scatter.42.cloned.1.call-update) | async-done | bytes 3088 | tf_op jit(solution)/shard_map/reduce_scatter | solution.py:330
  1171.7 40.0 %reduce-scatter.46.cloned.1.call-done = f32[256,128]{1,0:T(8,128)} async-done(((f32[256,1024]{1,0:T(8,128)}), f32[256,128]{1,0:T(8,128)}) %reduce-scatter.46.cloned.1.call-update) | async-done | bytes 131088 | tf_op jit(solution)/shard_map/reduce_scatter | solution.py:334
  1211.7 40.0 %reduce-scatter.38.cloned.1.call-done = f32[128,256]{1,0:T(8,128)} async-done(((f32[1024,256]{1,0:T(8,128)}), f32[128,256]{1,0:T(8,128)}) %reduce-scatter.38.cloned.1.call-update) | async-done | bytes 131088 | tf_op jit(solution)/shard_map/reduce_scatter | solution.py:328
  1251.7 55.5 %reduce-scatter.48.cloned.1.call-done = f32[128,1024]{1,0:T(8,128)} async-done(((f32[1024,1024]{1,0:T(8,128)}), f32[128,1024]{1,0:T(8,128)}) %reduce-scatter.48.cloned.1.call-update) | async-done | bytes 524304 | tf_op jit(solution)/shard_map/reduce_scatter | solution.py:335
  1307.2 55.3 %reduce-scatter.50.cloned.1.call-done = f32[1024,128]{1,0:T(8,128)} async-done(((f32[1024,1024]{1,0:T(8,128)}), f32[1024,128]{1,0:T(8,128)}) %reduce-scatter.50.cloned.1.call-update) | async-done | bytes 524304 | tf_op jit(solution)/shard_map/reduce_scatter | solution.py:337
  1362.5 66.0 %reduce-scatter.40.cloned.1.call-done = f32[256,6,128]{2,0,1:T(8,128)} async-done(((f32[256,6,1024]{2,0,1:T(8,128)}), f32[256,6,128]{2,0,1:T(8,128)}) %reduce-scatter.40.cloned.1.call-update) | async-done | bytes 786448 | tf_op jit(solution)/shard_map/reduce_scatter | solution.py:329
  (671 shorter events, 290.7 us)
Async XLA Ops:
  7.2 30.4 %copy-start.4 = (f32[2,170,1024]{2,0,1:T(2,128)S(1)}, f32[2,170,1024]{2,0,1:T(2,128)}, u32[]{:S(2)}) copy-start(f32[2,170,1024]{2,0,1:T(2,128)} %param.25) | copy-start | bytes 4177924
  7.2 36.6 %all-gather.14.cloned.1.call-start = ((), (), s32[]{:S(2)}) async-start(), calls=%async_computation.8 | async-start | bytes 3538944 | tf_op jit(solution)/shard_map/all_gather | solution.py:86
  7.9 102.2 %all-gather.18.cloned.1.call-start = ((), (), s32[]{:S(2)}) async-start(), calls=%async_computation.10 | async-start | bytes 1769472 | tf_op jit(solution)/shard_map/all_gather | solution.py:88
  8.7 119.9 %all-gather.16.cloned.1.call-start = ((), (), s32[]{:S(2)}) async-start(), calls=%async_computation.9 | async-start | bytes 3481600 | tf_op jit(solution)/shard_map/all_gather | solution.py:130
  42.3 22.3 %copy-start.6 = (f32[1,170,1024]{2,0,1:T(1,128)}, f32[1,170,1024]{2,0,1:T(1,128)S(1)}, u32[]{:S(2)}) copy-start(f32[1,170,1024]{2,0,1:T(1,128)S(1)} %get-tuple-element.733) | copy-start | bytes 2088964
  42.3 24.1 %copy-start.106 = (f32[170]{0:T(256)}, f32[170]{0:T(256)S(1)}, u32[]{:S(2)}) copy-start(f32[170]{0:T(256)S(1)} %get-tuple-element.757) | copy-start | bytes 2044
  42.3 24.7 %copy-start.8 = (f32[1,170,1024]{2,0,1:T(1,128)}, f32[1,170,1024]{2,0,1:T(1,128)S(1)}, u32[]{:S(2)}) copy-start(f32[1,170,1024]{2,0,1:T(1,128)S(1)} %get-tuple-element.758) | copy-start | bytes 2088964
  42.3 22.3 %copy-start.102 = (f32[170]{0:T(256)}, f32[170]{0:T(256)S(1)}, u32[]{:S(2)}) copy-start(f32[170]{0:T(256)S(1)} %fusion.208) | copy-start | bytes 2044
  66.3 120.5 %all-gather.26.cloned.1.call-start = ((), (), s32[]{:S(2)}) async-start(), calls=%async_computation.14 | async-start | bytes 3481600 | tf_op jit(solution)/shard_map/all_gather | solution.py:130
  67.1 13.5 copy-start.128
  67.1 22.3 %copy-start.121 = (s32[2,680]{1,0:T(2,128)S(1)}, s32[2,680]{1,0:T(2,128)}, u32[]{:S(2)}) copy-start(s32[2,680]{1,0:T(2,128)} %param.28) | copy-start | bytes 16324
  67.1 32.8 %copy-start.83 = (bf16[256,128]{1,0:T(8,128)(2,1)S(1)}, bf16[256,128]{1,0:T(8,128)(2,1)}, u32[]{:S(2)}) copy-start(bf16[256,128]{1,0:T(8,128)(2,1)} %param.35) | copy-start | bytes 196612
  68.9 294.8 %all-gather.22.cloned.1.call-start = ((), (), s32[]{:S(2)}) async-start(), calls=%async_computation.12 | async-start | bytes 2359296 | tf_op jit(solution)/shard_map/all_gather | solution.py:92
  69.4 326.5 %all-gather.20.cloned.1.call-start = ((), (), s32[]{:S(2)}) async-start(), calls=%async_computation.11 | async-start | bytes 3481600 | tf_op jit(solution)/shard_map/all_gather | solution.py:161
  132.9 57.5 %copy-start.81 = (f32[680,4]{0,1:T(4,128)}, f32[680,4]{0,1:T(4,128)S(1)}, u32[]{:S(2)}) copy-start(f32[680,4]{0,1:T(4,128)S(1)} %multiply_reduce_fusion.6) | copy-start | bytes 32644
  133.0 57.5 %copy-start.74 = (f32[680,4]{0,1:T(4,128)}, f32[680,4]{0,1:T(4,128)S(1)}, u32[]{:S(2)}) copy-start(f32[680,4]{0,1:T(4,128)S(1)} %add_rsqrt_fusion.2) | copy-start | bytes 32644
  307.9 6.7 collective-permute-start
  309.2 10.0 collective-permute-start.2
  337.5 89.8 %all-gather.24.cloned.1.call-start = ((), (), s32[]{:S(2)}) async-start(), calls=%async_computation.13 | async-start | bytes 2359296 | tf_op jit(solution)/shard_map/all_gather | solution.py:94
  338.3 146.2 %all-gather.30.cloned.1.call-start = ((), (), s32[]{:S(2)}) async-start(), calls=%async_computation.16 | async-start | bytes 3481600 | tf_op jit(solution)/shard_map/all_gather | solution.py:206
  343.1 199.9 %all-gather.28.cloned.1.call-start = ((), (), s32[]{:S(2)}) async-start(), calls=%async_computation.15 | async-start | bytes 3481600 | tf_op jit(solution)/shard_map/all_gather | solution.py:161
  350.4 250.2 %all-gather.34.cloned.1.call-start = ((), (), s32[]{:S(2)}) async-start(), calls=%async_computation.18 | async-start | bytes 3481600 | tf_op jit(solution)/shard_map/all_gather | solution.py:206
  363.4 401.7 %all-gather.32.cloned.1.call-start = ((), (), s32[]{:S(2)}) async-start(), calls=%async_computation.17 | async-start | bytes 3481600 | tf_op jit(solution)/shard_map/all_gather | solution.py:236
  665.9 6.1 collective-permute-start.4
  668.6 19.5 %collective-permute-start.6 = (bf16[18,1024]{1,0:T(8,128)(2,1)}, bf16[18,1024]{1,0:T(8,128)(2,1)}, u32[]{:S(2)}, u32[]{:S(2)}) collective-permute-start(bf16[18,1024]{1,0:T(8,128)(2,1)} %slice.211), channel_id=1, source_target_pairs={{0,1},{1,2},{2,3},{4,5},{5,6},{6,7},{8,9},{9,10},{10,11},{12,13},{... | collective-permute-start | bytes 110600
  688.2 15.5 %copy-start.91 = (f32[1,1,1024]{2,1,0:T(1,128)S(1)}, f32[1,1,1024]{2,1,0:T(1,128)}, u32[]{:S(2)}) copy-start(f32[1,1,1024]{2,1,0:T(1,128)} %get-tuple-element.772) | copy-start | bytes 12292
  692.8 10.9 copy-start.2
  692.8 10.9 copy-start.51
  692.8 10.9 copy-start.92
  692.8 10.9 copy-start.122
  708.4 114.4 %all-gather.36.cloned.1.call-start = ((), (), s32[]{:S(2)}) async-start(), calls=%async_computation.19 | async-start | bytes 3481600 | tf_op jit(solution)/shard_map/all_gather | solution.py:236
  722.8 408.3 %reduce-scatter.52.cloned.1.call-start = ((), (), s32[]{:S(2)}) async-start(), calls=%async_computation.27 | async-start | bytes 589824
  806.0 23.9 %copy-start.13 = (bf16[4,1,680,64]{3,2,1,0:T(8,128)(2,1)S(1)}, bf16[4,1,680,64]{3,2,1,0:T(8,128)(2,1)}, u32[]{:S(2)}) copy-start(bf16[4,1,680,64]{3,2,1,0:T(8,128)(2,1)} %get-tuple-element.1166) | copy-start | bytes 1044484
  829.8 29.1 %copy-start.80 = (f32[680,4]{0,1:T(4,128)S(1)}, f32[680,4]{0,1:T(4,128)}, u32[]{:S(2)}) copy-start(f32[680,4]{0,1:T(4,128)} %copy-done.79) | copy-start | bytes 32644
  829.8 29.1 %copy-start.73 = (f32[680,4]{0,1:T(4,128)S(1)}, f32[680,4]{0,1:T(4,128)}, u32[]{:S(2)}) copy-start(f32[680,4]{0,1:T(4,128)} %copy-done.72) | copy-start | bytes 32644
  870.0 107.1 %copy-start.61 = (bf16[1,680,256]{2,1,0:T(8,128)(2,1)S(1)}, bf16[1,680,256]{2,1,0:T(8,128)(2,1)}, u32[]{:S(2)}) copy-start(bf16[1,680,256]{2,1,0:T(8,128)(2,1)} %copy-done.60) | copy-start | bytes 1044484
  870.0 107.1 %copy-start.63 = (bf16[1,680,256]{2,1,0:T(8,128)(2,1)S(1)}, bf16[1,680,256]{2,1,0:T(8,128)(2,1)}, u32[]{:S(2)}) copy-start(bf16[1,680,256]{2,1,0:T(8,128)(2,1)} %copy.274) | copy-start | bytes 1044484
  870.0 107.1 %copy-start.65 = (bf16[1,680,256]{2,1,0:T(8,128)(2,1)S(1)}, bf16[1,680,256]{2,1,0:T(8,128)(2,1)}, u32[]{:S(2)}) copy-start(bf16[1,680,256]{2,1,0:T(8,128)(2,1)} %copy-done.64) | copy-start | bytes 1044484
  971.6 12.1 copy-start.7
  971.6 12.1 copy-start.85
  971.6 12.1 copy-start.103
  971.6 10.6 collective-permute-start.5
  973.0 14.2 collective-permute-start.7
  974.3 28.7 %collective-permute-start.1 = (bf16[18,1024]{1,0:T(8,128)(2,1)}, bf16[18,1024]{1,0:T(8,128)(2,1)}, u32[]{:S(2)}, u32[]{:S(2)}) collective-permute-start(bf16[18,1024]{1,0:T(8,128)(2,1)} %slice.206), channel_id=1, source_target_pairs={{0,1},{1,2},{2,3},{4,5},{5,6},{6,7},{8,9},{9,10},{10,11},{12,13},{... | collective-permute-start | bytes 110600
  975.6 41.6 %collective-permute-start.3 = (bf16[18,1024]{1,0:T(8,128)(2,1)}, bf16[18,1024]{1,0:T(8,128)(2,1)}, u32[]{:S(2)}, u32[]{:S(2)}) collective-permute-start(bf16[18,1024]{1,0:T(8,128)(2,1)} %slice.208), channel_id=1, source_target_pairs={{0,1},{1,2},{2,3},{4,5},{5,6},{6,7},{8,9},{9,10},{10,11},{12,13},{... | collective-permute-start | bytes 110600
  1002.9 19.5 %copy-start.3 = (f32[2,170,1024]{2,0,1:T(2,128)S(1)}, f32[2,170,1024]{2,0,1:T(2,128)}, u32[]{:S(2)}) copy-start(f32[2,170,1024]{2,0,1:T(2,128)} %param.26) | copy-start | bytes 4177924
  1002.9 19.5 %copy-start.22 = (f32[1,170,1024]{2,0,1:T(1,128)S(1)}, f32[1,170,1024]{2,0,1:T(1,128)}, u32[]{:S(2)}) copy-start(f32[1,170,1024]{2,0,1:T(1,128)} %copy-done.21) | copy-start | bytes 2088964
  1002.9 19.6 %copy-start.23 = (f32[1,170,1024]{2,0,1:T(1,128)S(1)}, f32[1,170,1024]{2,0,1:T(1,128)}, u32[]{:S(2)}) copy-start(f32[1,170,1024]{2,0,1:T(1,128)} %get-tuple-element.751) | copy-start | bytes 2088964
  1002.9 19.6 %copy-start.89 = (f32[1,1,1024]{2,1,0:T(1,128)S(1)}, f32[1,1,1024]{2,1,0:T(1,128)}, u32[]{:S(2)}) copy-start(f32[1,1,1024]{2,1,0:T(1,128)} %get-tuple-element.767) | copy-start | bytes 12292
  1002.9 19.6 %copy-start.90 = (f32[1,1,1024]{2,1,0:T(1,128)S(1)}, f32[1,1,1024]{2,1,0:T(1,128)}, u32[]{:S(2)}) copy-start(f32[1,1,1024]{2,1,0:T(1,128)} %get-tuple-element.775) | copy-start | bytes 12292
  1003.0 19.6 %copy-start.96 = (f32[1,1024]{1,0:T(1,128)S(1)}, f32[1,1024]{1,0:T(1,128)}, u32[]{:S(2)}) copy-start(f32[1,1024]{1,0:T(1,128)} %get-tuple-element.789) | copy-start | bytes 12292
  1022.6 29.1 %copy-start.57 = (bf16[1,680,256]{2,1,0:T(8,128)(2,1)S(1)}, bf16[1,680,256]{2,1,0:T(8,128)(2,1)}, u32[]{:S(2)}) copy-start(bf16[1,680,256]{2,1,0:T(8,128)(2,1)} %copy-done.56) | copy-start | bytes 1044484
  1050.5 11.8 copy-start.82
  1051.6 85.4 %reduce-scatter.44.cloned.1.call-start = ((), (), s32[]{:S(2)}) async-start(), calls=%async_computation.23 | async-start | bytes 3538944 | tf_op jit(solution)/shard_map/reduce_scatter | solution.py:331
  1057.9 113.9 %reduce-scatter.42.cloned.1.call-start = ((), (), s32[]{:S(2)}) async-start(), calls=%async_computation.22 | async-start | bytes 36864 | tf_op jit(solution)/shard_map/reduce_scatter | solution.py:330
  1062.9 148.8 %reduce-scatter.46.cloned.1.call-start = ((), (), s32[]{:S(2)}) async-start(), calls=%async_computation.24 | async-start | bytes 1179648 | tf_op jit(solution)/shard_map/reduce_scatter | solution.py:334
  1067.0 184.7 %reduce-scatter.38.cloned.1.call-start = ((), (), s32[]{:S(2)}) async-start(), calls=%async_computation.20 | async-start | bytes 1179648 | tf_op jit(solution)/shard_map/reduce_scatter | solution.py:328
  1075.0 232.2 %reduce-scatter.48.cloned.1.call-start = ((), (), s32[]{:S(2)}) async-start(), calls=%async_computation.25 | async-start | bytes 4718592 | tf_op jit(solution)/shard_map/reduce_scatter | solution.py:335
  1083.5 279.0 %reduce-scatter.50.cloned.1.call-start = ((), (), s32[]{:S(2)}) async-start(), calls=%async_computation.26 | async-start | bytes 4718592 | tf_op jit(solution)/shard_map/reduce_scatter | solution.py:337
  1094.1 334.4 %reduce-scatter.40.cloned.1.call-start = ((), (), s32[]{:S(2)}) async-start(), calls=%async_computation.21 | async-start | bytes 7077888 | tf_op jit(solution)/shard_map/reduce_scatter | solution.py:329
  1100.9 25.5 %copy-start.46 = (f32[1,170,1024]{2,0,1:T(1,128)S(1)}, f32[1,170,1024]{2,0,1:T(1,128)}, u32[]{:S(2)}) copy-start(f32[1,170,1024]{2,0,1:T(1,128)} %get-tuple-element.765) | copy-start | bytes 2088964
  1100.9 25.5 %copy-start.47 = (f32[1,170,1024]{2,0,1:T(1,128)S(1)}, f32[1,170,1024]{2,0,1:T(1,128)}, u32[]{:S(2)}) copy-start(f32[1,170,1024]{2,0,1:T(1,128)} %get-tuple-element.766) | copy-start | bytes 2088964
  1101.1 27.6 %copy-start.44 = (f32[1,170,1024]{2,0,1:T(1,128)S(1)}, f32[1,170,1024]{2,0,1:T(1,128)}, u32[]{:S(2)}) copy-start(f32[1,170,1024]{2,0,1:T(1,128)} %get-tuple-element.763) | copy-start | bytes 2088964
  1101.1 27.6 %copy-start.45 = (f32[1,170,1024]{2,0,1:T(1,128)S(1)}, f32[1,170,1024]{2,0,1:T(1,128)}, u32[]{:S(2)}) copy-start(f32[1,170,1024]{2,0,1:T(1,128)} %get-tuple-element.764) | copy-start | bytes 2088964
  (134 other events, 415.6 us)
Sparse Core Ops, SparseCore 0:
  9.9 33.8 all-gather.13
  45.7 25.6 all-gather.17
  73.5 54.9 all-gather.15
  130.6 56.2 all-gather.25
  188.6 29.1 all-gather.21
  337.6 58.2 all-gather.19
  397.8 29.4 all-gather.23
  429.5 54.9 all-gather.29
  486.6 56.2 all-gather.27
  544.3 56.2 all-gather.33
  708.5 56.5 all-gather.31
  766.5 56.2 all-gather.35
  1051.7 35.1 reduce-scatter.51
  1090.5 46.4 reduce-scatter.43
  1140.4 31.2 reduce-scatter.41
  1175.6 36.0 reduce-scatter.45
  1215.6 36.0 reduce-scatter.37
  1255.9 51.2 reduce-scatter.47
  1311.1 51.3 reduce-scatter.49
  1366.7 61.7 reduce-scatter.39
where the time goes:
time: 1450 us; the launch traced here: 1440 us
  waiting for transfers between devices  645 us (44%)
  blocking collectives  334 us (23%)
  matrix products  178 us (12%)
  local copies, waits for them, and re-layouts  124 us (9%)
  other arithmetic  119 us (8%)
  between operations  22 us (2%)
    unnamed x4, blocking collectives  229 us
    all_gather x2, waiting for transfers between devices, local(): feedforward_grad_total = lax.all_gather(d_ffn, 'tensor', axis=1, tiled=True)  109 us
    all_gather x2, waiting for transfers between devices, local(): lax.all_gather(normed_two.astype(b16), 'tensor', axis=1, tiled=True)  79.6 us
    unnamed x307, local copies, waits for them, and re-layouts  73.3 us
    all_gather x2, waiting for transfers between devices, local(): lax.all_gather(normed_one.astype(b16), 'tensor', axis=1, tiled=True)  70.8 us
    reduce_scatter x1, waiting for transfers between devices, local(): lax.psum_scatter(accum[1], 'dp', scatter_dimension=2, tiled=True)  66 us
    all_gather x2, waiting for transfers between devices, local(): branch_grad_total = lax.all_gather(d_branch, 'tensor', axis=1, tiled=True)  58.6 us
    reduce_scatter x1, waiting for transfers between devices, local(): lax.psum_scatter(accum[7], 'dp', scatter_dimension=0, tiled=True)  55.5 us
  transfers between devices with their start and end apart: 28, of which 19 were waited for; matrix products, arithmetic and copies ran while one was open for 26% of the time, Pallas kernels for 0%

commit v1 on v0

v1 whole, which is shorter than its diff:
```python
import functools

import jax
import jax.numpy as jnp
from jax import lax
from jax.experimental import pallas as pl
from jax.experimental.pallas import tpu as pltpu
from jax.sharding import PartitionSpec as P

MESH = pl.DeviceIdType.MESH
F32, B16 = jnp.float32, jnp.bfloat16
GROUPS = 3
CHUNK = 256
EPS = 1e-06
FAR = 256.0


def dot(a, b):
    return lax.dot_general(a, b, (((1,), (0,)), ((), ())), preferred_element_type=F32)


def dot_nt(a, b):
    return lax.dot_general(a, b, (((1,), (1,)), ((), ())), preferred_element_type=F32)


def dot_tn(a, b):
    return lax.dot_general(a, b, (((0,), (0,)), ((), ())), preferred_element_type=F32)


def split_dot(a, b):
    high = a.astype(B16)
    low = (a - high.astype(F32)).astype(B16)
    return dot(high, b) + dot(low, b)


def row_sum(a):
    return jnp.sum(a, axis=0, keepdims=True)


class Dims:
    def __init__(self, dp, tensor, rows, width, head, hidden):
        self.T = tensor
        self.NC = dp // 2
        self.bits = self.NC.bit_length() - 1
        self.Q = rows
        self.M = rows * tensor
        self.D = width
        self.hd = head
        self.hq = width // tensor // 2
        self.fu = hidden // tensor // 2
        self.R = width // dp
        self.C = 4 * self.hq + 2 * self.fu
        self.off = (0, 4 * self.hq, 4 * self.hq + self.fu)
        self.wide = (4 * self.hq, self.fu, self.fu)
        self.NCH = width // CHUNK
        assert 1 << self.bits == self.NC


def block_kernel(
    dm,
    ws, xb, dyb, mods, hp, hb, psi, phi,
    fin, outd, gind, sums, hsum, fsum,
    wall, xs, dys, h1, h2, qs, ks, vs, rq, rk, linv, o, ol, ab, n2, r2, g, gp,
    send, recv, df, xt, do, dqkv, od, rb0, rb1, zb, fbuf,
    c_s, c_r, c_l, z_s, z_r, p_s, p_r, x_s, x_r, x_l, x_f,
    e_s, e_r, rs_s, rs_r, rz_s, rz_r, f_s, f_r, o_s, o_r, o_l,
):
    T, NB, Q, M, D, R, C = dm.T, dm.bits, dm.Q, dm.M, dm.D, dm.R, dm.C
    hq, fu, NCH = dm.hq, dm.fu, dm.NCH
    TH = T // 2
    dpi = lax.axis_index("dp")
    me_z = lax.axis_index("tensor")
    core = lax.rem(dpi, 2)
    chip = dpi // 2
    mybit = [lax.rem(chip // (1 << b), 2) for b in range(NB)]
    partner = (dpi + 1 - 2 * core, me_z)

    def z_dev(off):
        return (dpi, lax.rem(me_z + off, T))

    def bit_dev(b):
        return (dpi + (1 - 2 * mybit[b]) * (2 << b), me_z)

    bar = pltpu.get_barrier_semaphore()
    friends = [partner] + [z_dev(k) for k in range(1, T)] + [bit_dev(b) for b in range(NB)]
    for dev in friends:
        pl.semaphore_signal(bar, inc=1, device_id=dev, device_id_type=MESH)
    pl.semaphore_wait(bar, len(friends))

    def rdma(src, dst, ss, rs, dev):
        return pltpu.make_async_remote_copy(
            src_ref=src, dst_ref=dst, send_sem=ss, recv_sem=rs, device_id=dev, device_id_type=MESH
        )

    every = slice(None)

    def place(fixed):
        return tuple(fixed.get(b, every) for b in reversed(range(NB)))

    mine = place({b: mybit[b] for b in range(NB)})

    def cols(grp):
        return pl.ds(dm.off[grp], dm.wide[grp])

    def core_copy(grp):
        src = ws.at[1 - core, :, cols(grp)]
        dst = wall.at[(me_z,) + mine + (pl.ds(pl.multiple_of(core * R, R), R), cols(grp))]
        return rdma(src, dst, c_s.at[grp], c_r.at[grp], partner)

    def core_local(grp):
        src = ws.at[core, :, cols(grp)]
        dst = wall.at[(me_z,) + mine + (pl.ds(pl.multiple_of(core * R, R), R), cols(grp))]
        return pltpu.make_async_copy(src, dst, c_l.at[grp])

    def core_wait(grp):
        core_local(grp).wait()
        other = wall.at[(me_z,) + mine + (pl.ds(pl.multiple_of((1 - core) * R, R), R), cols(grp))]
        rdma(other, other, c_s.at[grp], c_r.at[grp], partner).wait_recv()

    def z_copy(grp, off):
        part = wall.at[(me_z,) + mine + (every, cols(grp))]
        return rdma(part, part, z_s.at[grp, off - 1], z_r.at[grp, off - 1], z_dev(off))

    def z_start(grp):
        for off in range(1, T):
            z_copy(grp, off).start()

    def z_wait(grp):
        for off in range(1, T):
            part = wall.at[(lax.rem(me_z - off + T, T),) + mine + (every, cols(grp))]
            rdma(part, part, z_s.at[grp, off - 1], z_r.at[grp, off - 1], z_dev(off)).wait_recv()

    order = [list(range(NB)), list(reversed(range(NB)))]

    def half_z(h):
        return pl.ds(h * TH, TH)

    def p_copy(grp, step, h, landing):
        b = order[h][step]
        fixed = {k: mybit[k] for k in order[h][step:]}
        if landing:
            fixed[b] = 1 - mybit[b]
        part = wall.at[(half_z(h),) + place(fixed) + (every, cols(grp))]
        return rdma(part, part, p_s.at[grp, step, h], p_r.at[grp, step, h], bit_dev(b))

    def p_start(grp, step):
        for h in range(2):
            p_copy(grp, step, h, False).start()

    def p_wait(grp, step):
        for h in range(2):
            p_copy(grp, step, h, True).wait_recv()

    def gather_sent(grp):
        core_copy(grp).wait_send()
        for off in range(1, T):
            z_copy(grp, off).wait_send()
        for step in range(NB):
            for h in range(2):
                p_copy(grp, step, h, False).wait_send()

    owner = me_z // 2 == core

    def tok_copy(which, src, dst, i):
        zt = 2 * core + i
        return rdma(src.at[i], dst.at[me_z], x_s.at[which, i], x_r.at[which, me_z], (dpi, zt))

    def tok_start(which, src, dst):
        for i in range(2):
            @pl.when(2 * core + i != me_z)
            def _():
                tok_copy(which, src, dst, i).start()

            @pl.when(2 * core + i == me_z)
            def _():
                pltpu.make_async_copy(src.at[i], dst.at[me_z], x_l.at[which]).start()

    def tok_forward(which, dst):
        return rdma(dst, dst, x_f.at[which, 0], x_f.at[which, 1], partner)

    def tok_wait(which, src, dst):
        @pl.when(owner)
        def _():
            for off in range(1, T):
                zq = lax.rem(me_z + off, T)
                rdma(dst.at[zq], dst.at[zq], x_s.at[which, 0], x_r.at[which, zq], (dpi, zq)).wait_recv()
            pltpu.make_async_copy(src.at[0], dst.at[me_z], x_l.at[which]).wait()
            tok_forward(which, dst).start()

        @pl.when(jnp.logical_not(owner))
        def _():
            tok_forward(which, dst).wait_recv()

    def tok_sent(which, src, dst):
        for i in range(2):
            @pl.when(2 * core + i != me_z)
            def _():
                tok_copy(which, src, dst, i).wait_send()

        @pl.when(owner)
        def _():
            tok_forward(which, dst).wait_send()

    back_from = (od, h2)

    def back_copy(which, dst, zq):
        return rdma(back_from[which].at[zq], dst.at[lax.rem(me_z, 2)], o_s.at[which, zq], o_r.at[which, lax.rem(me_z, 2)], (dpi, zq))

    def back_start(which, dst):
        @pl.when(owner)
        def _():
            for off in range(1, T):
                back_copy(which, dst, lax.rem(me_z + off, T)).start()
            pltpu.make_async_copy(back_from[which].at[me_z], dst.at[lax.rem(me_z, 2)], o_l.at[which]).start()

    def back_wait(which, dst):
        @pl.when(owner)
        def _():
            for off in range(1, T):
                back_copy(which, dst, lax.rem(me_z + off, T)).wait_send()
            pltpu.make_async_copy(back_from[which].at[me_z], dst.at[lax.rem(me_z, 2)], o_l.at[which]).wait()

        for i in range(2):
            @pl.when(2 * core + i != me_z)
            def _():
                rdma(dst.at[i], dst.at[i], o_s.at[which, 0], o_r.at[which, i], (dpi, 2 * core + i)).wait_recv()

    def x_copy(k, n):
        return rdma(send.at[n], recv.at[k % 2, n], e_s.at[k, n], e_r.at[k, n], partner)

    def exchange(k, n, value):
        send[n] = value.astype(B16).reshape(T, Q, CHUNK)
        x_copy(k, n).start()

    def exchange_wait(k):
        for n in range(NCH):
            x_copy(k, n).wait_recv()

    def exchange_sent(k):
        for n in range(NCH):
            x_copy(k, n).wait_send()

    def both(k, t):
        parts = [send[n, t].astype(F32) + recv[k % 2, n, t].astype(F32) for n in range(NCH)]
        return jnp.concatenate(parts, axis=-1)

    def wz(z, lo, n):
        return wall[(z,) + (every,) * NB + (every, pl.ds(lo, n))].reshape(D, n)

    def wrows(z, n, lo, width):
        per = CHUNK // (2 * R)
        low = per.bit_length() - 1
        top = n * per
        fixed = {b: (top >> b) & 1 for b in range(low, NB)}
        return wall[(z,) + place(fixed) + (every, pl.ds(lo, width))].reshape(CHUNK, width)

    def wstore(z, lo, n, value):
        wall[(z,) + (every,) * NB + (every, pl.ds(lo, n))] = value.astype(B16).reshape(
            (2,) * NB + (2 * R, n)
        )

    def all_z(ref):
        return jnp.concatenate([ref[z] for z in range(T)], axis=-1)

    def mod(r):
        return mods[r : r + 1, :]

    def transpose_into(ref):
        for n in range(D // 128):
            block = ref[:, :, n * 128 : (n + 1) * 128].reshape(M, 128)
            xt[n * 128 : (n + 1) * 128, :] = block.T

    def rs_region(grp, step, h, away):
        order_r = order[h][::-1]
        fixed = {k: mybit[k] for k in order_r[: step + 1]}
        b = order_r[step]
        if away:
            fixed[b] = 1 - mybit[b]
        return b, fixed

    slot = {2: 0, 1: 1, 0: 0}

    def rs_buf(grp, step, h):
        return rb0.at[slot[grp], h] if step == 0 else rb1[step - 1].at[grp, h]

    def rs_copy(grp, step, h):
        b, fixed = rs_region(grp, step, h, True)
        part = wall.at[(half_z(h),) + place(fixed) + (every, cols(grp))]
        return rdma(part, rs_buf(grp, step, h), rs_s.at[grp, step, h], rs_r.at[grp, step, h], bit_dev(b))

    def rs_start(grp, step, h):
        rs_copy(grp, step, h).start()

    def rs_add(grp, step, h):
        rs_copy(grp, step, h).wait_recv()
        b, fixed = rs_region(grp, step, h, False)
        rest = [k for k in reversed(range(NB)) if k not in fixed]
        buf = rs_buf(grp, step, h)

        def one(i, carry):
            zz, j = i // (1 << len(rest)), lax.rem(i, 1 << len(rest))
            at = dict(fixed)
            inner = ()
            for pos, k in enumerate(rest):
                v = lax.rem(j // (1 << (len(rest) - 1 - pos)), 2)
                at[k] = v
                inner += (v,)
            where = (h * TH + zz,) + place(at) + (every, cols(grp))
            wall[where] = (wall[where].astype(F32) + buf[(zz,) + inner].astype(F32)).astype(B16)
            return carry

        lax.fori_loop(0, TH << len(rest), one, 0)

    def rz_copy(grp, off):
        part = wall.at[(lax.rem(me_z + off, T),) + mine + (every, cols(grp))]
        return rdma(part, zb.at[off - 1, :, cols(grp)], rz_s.at[grp, off - 1], rz_r.at[grp, off - 1], z_dev(off))

    def rz_start(grp):
        for off in range(1, T):
            rz_copy(grp, off).start()

    def fin_copy(grp):
        rows = pl.ds(pl.multiple_of((1 - core) * R, R), R)
        return rdma(fbuf.at[rows, cols(grp)], fin.at[core, :, cols(grp)], f_s.at[grp], f_r.at[grp], partner)

    def rz_add(grp):
        for off in range(1, T):
            rz_copy(grp, off).wait_recv()
        total = wall[(me_z,) + mine + (every, cols(grp))].astype(F32)
        for off in range(1, T):
            total = total + zb[off - 1, :, cols(grp)].astype(F32)
        fbuf[:, cols(grp)] = total
        fin_copy(grp).start()
        fin[core, :, cols(grp)] = fbuf[pl.ds(pl.multiple_of(core * R, R), R), cols(grp)]

    def rs_end(grp):
        for step in range(NB):
            for h in range(2):
                rs_copy(grp, step, h).wait_send()
        for off in range(1, T):
            rz_copy(grp, off).wait_send()
        fin_copy(grp).wait()

    tok_start(0, xb, xs)
    for grp in range(GROUPS):
        core_copy(grp).start()
        core_local(grp).start()
    for grp in range(GROUPS):
        core_wait(grp)
        if grp == 0:
            z_start(0)
    sums[...] = jnp.zeros_like(sums)
    tok_wait(0, xb, xs)

    def ln(rows):
        centred = rows - jnp.mean(rows, axis=-1, keepdims=True)
        inv = lax.rsqrt(jnp.mean(centred * centred, axis=-1, keepdims=True) + EPS)
        return centred * inv, inv

    def first_norm(t, carry):
        normed, _ = ln(xs[t].astype(F32))
        h1[t] = (normed * (1.0 + mod(2)) + mod(4)).astype(B16)
        return carry

    lax.fori_loop(0, T, first_norm, 0)
    z_wait(0)
    p_start(0, 0)
    z_start(1)
    tok_start(1, dyb, dys)
    for step in range(NB):
        p_wait(0, step)
        if step + 1 < NB:
            p_start(0, step + 1)
    z_wait(1)
    p_start(1, 0)
    z_start(2)

    lane = lax.broadcasted_iota(jnp.int32, (1, hq), 1)
    halves = [(lane // dm.hd) == k for k in range(hq // dm.hd)]
    bi = lax.broadcasted_iota(jnp.int32, (hq, hq), 0) // dm.hd
    bj = lax.broadcasted_iota(jnp.int32, (hq, hq), 1) // dm.hd
    same_head = (bi == bj).astype(B16)

    def qkv(z, carry):
        t = dot(h1[...].reshape(M, D), wz(z, 0, 3 * hq))
        q = t[:, :hq] + hp[z, 0:1, :]
        k = t[:, hq : 2 * hq]
        v = t[:, 2 * hq :] + hp[z, 1:2, :]
        qi = lax.rsqrt(split_dot(q * q, same_head) + EPS)
        ki = lax.rsqrt(split_dot(k * k, same_head) + EPS)
        qs[z] = (q * qi * hp[z, 2:3, :]).astype(B16)
        ks[z] = (k * ki).astype(B16)
        vs[z] = v.astype(B16)
        rq[z] = qi.astype(B16)
        rk[z] = ki.astype(B16)
        return carry

    lax.fori_loop(0, T, qkv, 0)
    zero16 = jnp.zeros((), B16)

    def expo(z, k, q_all, k_all):
        q_one = jnp.where(halves[k], q_all, zero16)
        left = jnp.concatenate([q_one, psi[...]], axis=1)
        right = jnp.concatenate([k_all, phi[...]], axis=1)
        return q_one, jnp.exp(dot_nt(left, right)).astype(B16)

    def attend(z, carry):
        q_all, k_all, v_all = qs[z], ks[z], vs[z]
        v_ones = jnp.concatenate([v_all, jnp.ones((M, hq), B16)], axis=1)
        mixed = inverse = None
        for k in range(hq // dm.hd):
            _, e = expo(z, k, q_all, k_all)
            both_ = dot(e, v_ones)
            inv = 1.0 / both_[:, hq:]
            one = both_[:, :hq] * inv
            mixed = one if mixed is None else jnp.where(halves[k], one, mixed)
            inverse = inv if inverse is None else jnp.where(halves[k], inv, inverse)
        o[z] = mixed.astype(B16)
        ol[z] = (mixed - mixed.astype(B16).astype(F32)).astype(B16)
        linv[z] = inverse
        return carry

    for z0 in range(0, T, 2):
        lax.fori_loop(z0, z0 + 2, attend, 0)
        if z0 == 0:
            p_wait(1, 0)
            if NB > 1:
                p_start(1, 1)
            z_wait(2)
            p_start(2, 0)

    o_all = all_z(o)
    for n in range(NCH):
        w = jnp.concatenate([wrows(z, n, 3 * hq, hq) for z in range(T)], axis=-1)
        exchange(0, n, dot_nt(o_all, w))
    exchange_wait(0)

    def middle(t):
        return xs[t].astype(F32) + mod(0) * ab[t].astype(F32)

    def second_norm(t, carry):
        ab[t] = (both(0, t) + mod(6)).astype(B16)
        normed, inv = ln(middle(t))
        h2[t] = (normed * (1.0 + mod(3)) + mod(5)).astype(B16)
        n2[t] = normed.astype(B16)
        r2[t] = jnp.broadcast_to(inv, (Q, 128))
        return carry

    lax.fori_loop(0, T, second_norm, 0)
    exchange_sent(0)
    for step in range(1, NB):
        p_wait(1, step)
        if step + 1 < NB:
            p_start(1, step + 1)
    p_wait(2, 0)
    if NB > 1:
        p_start(2, 1)

    root = 0.7978845608028654

    def up(z, carry):
        u = dot(h2[...].reshape(M, D), wz(z, dm.off[1], fu)) + hb[z, 0:1, :]
        uu = u * u
        th = jnp.tanh(root * u * (1.0 + 0.044715 * uu))
        g[z] = (0.5 * u * (1.0 + th)).astype(B16)
        gp[z] = (0.5 * (1.0 + th) + (0.5 * root) * u * (1.0 - th * th) * (1.0 + 0.134145 * uu)).astype(B16)
        return carry

    lax.fori_loop(0, T, up, 0)
    for step in range(1, NB):
        p_wait(2, step)
        if step + 1 < NB:
            p_start(2, step + 1)

    g_all = all_z(g)
    for n in range(NCH):
        w = jnp.concatenate([wrows(z, n, dm.off[2], fu) for z in range(T)], axis=-1)
        exchange(1, n, dot_nt(g_all, w))
    tok_wait(1, dyb, dys)
    exchange_wait(1)

    def last(t, carry):
        f = both(1, t) + mod(7)
        dy = dys[t].astype(F32)
        gamma = mod(1)
        od[t] = (mod(0) * ab[t].astype(F32) + gamma * f).astype(B16)
        sums[1:2, :] += row_sum(dy * f)
        d = (gamma * dy).astype(B16)
        df[t] = d
        sums[7:8, :] += row_sum(d.astype(F32))
        return carry

    lax.fori_loop(0, T, last, 0)
    exchange_sent(1)
    back_start(0, outd)
    for grp in range(GROUPS):
        gather_sent(grp)

    transpose_into(df)

    def down_back(z, carry):
        dg = dot(df[...].reshape(M, D), wz(z, dm.off[2], fu))
        du = (dg * gp[z].astype(F32)).astype(B16)
        gp[z] = du
        fsum[z] = jnp.broadcast_to(row_sum(du.astype(F32)), (8, fu))
        wstore(z, dm.off[2], fu, dot(xt[...], g[z]))
        return carry

    for h in range(2):
        lax.fori_loop(h * TH, (h + 1) * TH, down_back, 0)
        rs_start(2, 0, h)

    du_all = all_z(gp)
    for n in range(NCH):
        w = jnp.concatenate([wrows(z, n, dm.off[1], fu) for z in range(T)], axis=-1)
        exchange(2, n, dot_nt(du_all, w))
    transpose_into(h2)

    def up_back(z, carry):
        wstore(z, dm.off[1], fu, dot(xt[...], gp[z]))
        return carry

    lax.fori_loop(0, TH, up_back, 0)
    exchange_wait(2)

    def ln_back(e, normed, inv):
        return (e - jnp.mean(e, axis=-1, keepdims=True) - normed * jnp.mean(e * normed, axis=-1, keepdims=True)) * inv

    def mid_back(t, carry):
        dh = both(2, t)
        normed = n2[t].astype(F32)
        sums[3:4, :] += row_sum(dh * normed)
        sums[5:6, :] += row_sum(dh)
        step_back = ln_back(dh * (1.0 + mod(3)), normed, r2[t, :, 0:1])
        dx1 = dys[t].astype(F32) + step_back
        dys[t] = step_back.astype(B16)
        sums[0:1, :] += row_sum(dx1 * ab[t].astype(F32))
        da = (mod(0) * dx1).astype(B16)
        df[t] = da
        sums[6:7, :] += row_sum(da.astype(F32))
        return carry

    tok_sent(1, dyb, dys)
    lax.fori_loop(0, T, mid_back, 0)
    exchange_sent(2)
    for h in range(2):
        rs_add(2, 0, h)
        if NB > 1:
            rs_start(2, 1, h)
    rs_start(1, 0, 0)
    lax.fori_loop(TH, T, up_back, 0)
    rs_start(1, 0, 1)

    w_proj = jnp.concatenate([wz(z, 3 * hq, hq) for z in range(T)], axis=-1)
    do_all = dot(df[...].reshape(M, D), w_proj).astype(B16)
    for z in range(T):
        do[z] = do_all[:, z * hq : (z + 1) * hq]
    transpose_into(df)
    dw = dot(xt[...], all_z(o))
    for z in range(T):
        wstore(z, 3 * hq, hq, dw[:, z * hq : (z + 1) * hq])

    lane2 = lax.broadcasted_iota(jnp.int32, (1, hq), 1)
    ends = jnp.where(lane2 < 2, -1.0, 0.0).astype(B16)

    def attend_back(z, carry):
        q_all, k_all, v_all = qs[z], ks[z], vs[z]
        scaled = do[z].astype(F32) * linv[z]
        dob = scaled.astype(B16)
        prod = dob.astype(F32) * (o[z].astype(F32) + ol[z].astype(F32))
        v_ends = jnp.concatenate([v_all, jnp.broadcast_to(ends, (M, hq))], axis=1)
        dq = dk = dv = 0.0
        for k in range(hq // dm.hd):
            q_one, e = expo(z, k, q_all, k_all)
            to_all = (bi == k).astype(B16)
            total = split_dot(prod, to_all)
            high = total.astype(B16)
            low = (total - high.astype(F32)).astype(B16)
            extra = jnp.where(lane2 == 0, high, jnp.where(lane2 == 1, low, zero16))
            d_one = jnp.where(halves[k], dob, zero16)
            dp = dot_nt(jnp.concatenate([d_one, extra], axis=1), v_ends)
            ds = (e.astype(F32) * dp).astype(B16)
            dq = dq + dot(ds, jnp.where(halves[k], k_all, zero16))
            dk = dk + dot_tn(ds, q_one)
            dv = dv + dot_tn(e, d_one)
        gain = hp[z, 2:3, :]
        q_hat = q_all.astype(F32) * hp[z, 3:4, :]
        k_hat = k_all.astype(F32)
        hsum[z, 2:3, :] = row_sum(dq * q_hat)
        eq = dq * gain
        dq = ((eq - q_hat * split_dot(eq * q_hat, same_head)) * rq[z].astype(F32)).astype(B16)
        dk = ((dk - k_hat * split_dot(dk * k_hat, same_head)) * rk[z].astype(F32)).astype(B16)
        dv = dv.astype(B16)
        hsum[z, 0:1, :] = row_sum(dq.astype(F32))
        hsum[z, 1:2, :] = row_sum(dv.astype(F32))
        dqkv[z] = jnp.concatenate([dq, dk, dv], axis=1)
        return carry

    hsum[...] = jnp.zeros_like(hsum)
    lax.fori_loop(0, TH, attend_back, 0)
    for h in range(2):
        for step in range(1, NB):
            rs_add(2, step, h)
            if step + 1 < NB:
                rs_start(2, step + 1, h)
    rz_start(2)
    for h in range(2):
        rs_add(1, 0, h)
        if NB > 1:
            rs_start(1, 1, h)
    lax.fori_loop(TH, T, attend_back, 0)

    d_all = all_z(dqkv)
    for n in range(NCH):
        w = jnp.concatenate([wrows(z, n, 0, 3 * hq) for z in range(T)], axis=-1)
        exchange(3, n, dot_nt(d_all, w))
    transpose_into(h1)

    def qkv_back(z, carry):
        wstore(z, 0, 3 * hq, dot(xt[...], dqkv[z]))
        return carry

    for h in range(2):
        lax.fori_loop(h * TH, (h + 1) * TH, qkv_back, 0)
        rs_start(0, 0, h)
    exchange_wait(3)

    def first_back(t, carry):
        dh = both(3, t)
        normed, inv = ln(xs[t].astype(F32))
        sums[2:3, :] += row_sum(dh * normed)
        sums[4:5, :] += row_sum(dh)
        h2[t] = (dys[t].astype(F32) + ln_back(dh * (1.0 + mod(2)), normed, inv)).astype(B16)
        return carry

    lax.fori_loop(0, T, first_back, 0)
    exchange_sent(3)
    back_start(1, gind)
    for h in range(2):
        for step in range(1, NB):
            rs_add(1, step, h)
            if step + 1 < NB:
                rs_start(1, step + 1, h)
    rz_start(1)
    rz_add(2)
    for step in range(NB):
        for h in range(2):
            rs_add(0, step, h)
            if step + 1 < NB:
                rs_start(0, step + 1, h)
    rz_start(0)
    rz_add(1)
    rz_add(0)
    for grp in range(GROUPS):
        rs_end(grp)
    tok_sent(0, xb, xs)
    back_wait(0, outd)
    back_wait(1, gind)


def block_call(dm, ws, xb, dyb, mods, hp, hb, psi, phi):
    T, NB, Q, M, D, R, C = dm.T, dm.bits, dm.Q, dm.M, dm.D, dm.R, dm.C
    hq, fu, NCH, gw = dm.hq, dm.fu, dm.NCH, dm.fu
    TH = T // 2
    two = (2,) * NB
    v = pltpu.VMEM
    dma = pltpu.SemaphoreType.DMA
    any_, vm = pl.BlockSpec(memory_space=pl.ANY), pl.BlockSpec(memory_space=pltpu.VMEM)
    s = jax.ShapeDtypeStruct
    tok = (T, Q, D)
    scratch = [
        v((T,) + two + (2 * R, C), B16),
        v(tok, B16), v(tok, B16), v(tok, B16), v(tok, B16),
        v((T, M, hq), B16), v((T, M, hq), B16), v((T, M, hq), B16),
        v((T, M, hq), B16), v((T, M, hq), B16), v((T, M, hq), F32),
        v((T, M, hq), B16), v((T, M, hq), B16), v(tok, B16), v(tok, B16), v((T, Q, 128), F32),
        v((T, M, fu), B16), v((T, M, fu), B16),
        v((NCH, T, Q, CHUNK), B16), v((2, NCH, T, Q, CHUNK), B16),
        v(tok, B16), v((D, M), B16),
        v((T, M, hq), B16), v((T, M, 3 * hq), B16), v(tok, B16),
        v((2, 2, TH) + (2,) * (NB - 1) + (2 * R, gw), B16),
        [v((GROUPS, 2, TH) + (2,) * (NB - 1 - k) + (2 * R, gw), B16) for k in range(1, NB)],
        v((T - 1, 2 * R, C), B16), v((2 * R, C), F32),
        dma((GROUPS,)), dma((GROUPS,)), dma((GROUPS,)),
        dma((GROUPS, T - 1)), dma((GROUPS, T - 1)),
        dma((GROUPS, NB, 2)), dma((GROUPS, NB, 2)),
        dma((2, 2)), dma((2, T)), dma((2,)), dma((2, 2)),
        dma((4, NCH)), dma((4, NCH)),
        dma((GROUPS, NB, 2)), dma((GROUPS, NB, 2)),
        dma((GROUPS, T - 1)), dma((GROUPS, T - 1)),
        dma((GROUPS,)), dma((GROUPS,)),
        dma((2, T)), dma((2, 2)), dma((2,)),
    ]
    return pl.pallas_call(
        functools.partial(block_kernel, dm),
        out_shape=(
            s((2, R, C), F32), s((2, Q, D), B16), s((2, Q, D), B16),
            s((8, D), F32), s((T, 8, hq), F32), s((T, 8, fu), F32),
        ),
        in_specs=[any_] * 3 + [vm] * 5,
        out_specs=(vm, any_, any_, vm, vm, vm),
        scratch_shapes=scratch,
        compiler_params=pltpu.CompilerParams(
            collective_id=0, has_side_effects=True, vmem_limit_bytes=66 * 1024 * 1024
        ),
        cost_estimate=pl.CostEstimate(flops=30 * 10**9, bytes_accessed=10**7, transcendentals=10**7),
    )(ws, xb, dyb, mods, hp, hb, psi, phi)


def local(
    dp, tensor,
    block_input, cotangent, class_ids, scale_ids, class_table, w_ada, b_ada, query_key_value_weight,
    qv_bias, q_gain, output_projection, up_weight, hidden_bias, down_weight, projection_bias,
):
    seqs, quarter, width = block_input.shape
    length = scale_ids.shape[1]
    assert seqs == 2 and tensor == 4
    rows = -(-quarter // 16) * 16
    head = q_gain.shape[1] * dp
    hidden = up_weight.shape[1] * tensor
    dm = Dims(dp, tensor, rows, width, head, hidden)
    T, R, hq, fu, NC, M = dm.T, dm.R, dm.hq, dm.fu, dm.NC, dm.M
    total = class_ids.shape[0]
    di, zi = lax.axis_index("dp"), lax.axis_index("tensor")
    core = di % 2

    my_rows = class_table.shape[0]
    hot = (class_ids[:, None] == (di * my_rows + jnp.arange(my_rows, dtype=jnp.int32))[None, :]).astype(B16)
    cond = lax.psum(jnp.dot(hot, class_table, preferred_element_type=F32), "dp")
    silu, silu_back = jax.vjp(jax.nn.silu, cond)
    silu_low = silu.astype(B16)
    parts = jnp.einsum("sc,cjd->sjd", silu_low, w_ada, preferred_element_type=F32)
    parts = parts.reshape((NC, T) + parts.shape[1:])
    mine = lax.psum_scatter(parts, "tensor", scatter_dimension=1, tiled=True)[:, 0] + b_ada.astype(F32)
    spread = lax.all_to_all(jnp.repeat(mine, 2, axis=0), "dp", 0, 0, tiled=True)
    modulation = jnp.moveaxis(spread, 0, 1).reshape(6, width)

    pieces = [qv_bias, q_gain, hidden_bias, projection_bias]
    flat = jnp.concatenate([p.reshape(-1) for p in pieces])
    everyone = lax.all_gather(lax.all_gather(flat, "tensor"), "dp")
    cut, at = [], 0
    for p in pieces:
        cut.append(everyone[:, :, at : at + p.size].reshape((dp, T) + p.shape).astype(F32))
        at += p.size
    qv_all = cut[0].transpose(2, 1, 3, 0, 4).reshape(2, T, 2, hq)[:, :, core]
    gain_all = cut[1].transpose(1, 2, 0, 3).reshape(T, 2, hq)[:, core]
    hidden_all = cut[2].transpose(1, 2, 0, 3).reshape(T, 2, fu)[:, core]
    out_bias = cut[3][:, 0].transpose(1, 0, 2).reshape(2, width)
    mods = jnp.concatenate([modulation, out_bias], axis=0)
    hp = jnp.stack([qv_all[0], qv_all[1], gain_all, 1.0 / gain_all], axis=1)
    hp = jnp.concatenate([hp, jnp.zeros_like(hp)], axis=1)
    hb = jnp.broadcast_to(hidden_all[:, None], (T, 8, fu))

    swap = [(d, d + 1 - 2 * (d % 2)) for d in range(dp)]
    other = lax.ppermute(scale_ids, "dp", swap)
    ids = jnp.where(zi // 2 == core, scale_ids, other)
    ids = lax.dynamic_index_in_dim(ids, zi % 2, 0, keepdims=False)
    ids = jnp.pad(ids.reshape(T, quarter), ((0, 0), (0, rows - quarter)), constant_values=127).reshape(M, 1)
    lanes = jnp.arange(128, dtype=jnp.int32)[None, :]
    psi = jnp.where(lanes > ids, FAR, 0.0).astype(B16)
    phi = jnp.where(lanes == ids, -1.0, 0.0).astype(B16)

    def halves(w):
        return jnp.moveaxis(w.reshape(w.shape[:-1] + (2, w.shape[-1] // 2)), -2, 0)

    qkv_half = halves(query_key_value_weight)
    ws = jnp.concatenate(
        [qkv_half[:, 0], qkv_half[:, 1], qkv_half[:, 2], halves(output_projection.T), halves(up_weight), halves(down_weight.T)],
        axis=-1,
    )
    pad = ((0, 0), (0, rows - quarter), (0, 0))
    xb = jnp.pad(block_input.astype(B16), pad)
    dyb = jnp.pad(cotangent.astype(B16), pad)

    fin, outd, gind, sums, hsum, fsum = block_call(dm, ws, xb, dyb, mods, hp, hb, psi, phi)

    block_output = block_input + outd[:, :quarter].astype(F32)
    input_grad = cotangent + gind[:, :quarter].astype(F32)

    def joined(lo, n):
        return jnp.moveaxis(fin[:, :, lo : lo + n], 0, 1).reshape(R, 2 * n)

    w_qkv_grad = jnp.stack([joined(k * hq, hq) for k in range(3)])
    w_proj_grad = joined(3 * hq, hq).T
    w_fc1_grad = joined(dm.off[1], fu)
    w_fc2_grad = joined(dm.off[2], fu).T

    dmod = sums[:6].reshape(6, dp, R).astype(B16)
    dmod = lax.all_to_all(jnp.moveaxis(dmod, 1, 0), "dp", 0, 0, tiled=True)
    dmod = lax.all_gather(dmod[::2], "tensor", axis=1)
    dmod = dmod.reshape((total, 6, R))
    b_ada_grad = jnp.sum(dmod.astype(F32), axis=0)
    w_ada_grad = jnp.einsum("sc,sjd->cjd", silu_low, dmod, preferred_element_type=F32)
    d_silu = lax.psum(jnp.einsum("sjd,cjd->sc", dmod, w_ada, preferred_element_type=F32), "dp")
    (d_cond,) = silu_back(d_silu)
    table_grad = jnp.dot(hot.astype(F32).T, d_cond, precision=lax.Precision.HIGHEST, preferred_element_type=F32)

    vec = jnp.concatenate([hsum[:, :3].reshape(-1), fsum[:, 0].reshape(-1), sums[6:].reshape(-1) * 0.5])
    nh, nf = T * 3 * hq, T * fu
    place_ = jnp.arange(2, dtype=jnp.int32) == core
    by_core = jnp.where(place_[:, None], vec[None, : nh + nf], 0.0).reshape(-1)
    vec = lax.psum(jnp.concatenate([by_core, vec[nh + nf :]]), ("dp", "tensor"))
    by_core = vec[: 2 * (nh + nf)].reshape(2, nh + nf)
    heads = by_core[:, :nh].reshape(2, T, 3, hq)
    heads = lax.dynamic_index_in_dim(heads, zi, 1, keepdims=False)
    heads = jnp.moveaxis(heads, 0, 1).reshape(3, -1, head)
    step = head // dp
    heads = lax.dynamic_slice_in_dim(heads, di * step, step, 2)
    qv_bias_grad, q_gain_grad = heads[:2], heads[2]
    fc1 = lax.dynamic_index_in_dim(by_core[:, nh:].reshape(2, T, fu), zi, 1, keepdims=False)
    fc1 = fc1.reshape(-1, hidden_bias.shape[1] * dp)
    step = hidden_bias.shape[1]
    b_fc1_grad = lax.dynamic_slice_in_dim(fc1, di * step, step, 1)
    b_out_grad = lax.dynamic_slice_in_dim(vec[2 * (nh + nf) :].reshape(2, width), di * R, R, 1)

    return (
        block_output, input_grad, table_grad, w_ada_grad, b_ada_grad, w_qkv_grad, qv_bias_grad, q_gain_grad,
        w_proj_grad, w_fc1_grad, b_fc1_grad, w_fc2_grad, b_out_grad,
    )


def solution(mesh):
    dp, tensor = mesh.shape["dp"], mesh.shape["tensor"]
    return jax.shard_map(
        functools.partial(local, dp, tensor),
        mesh=mesh,
        in_specs=(
            P("dp", "tensor", None),
            P("dp", "tensor", None),
            P(),
            P("dp", None),
            P("dp", "tensor"),
            P("tensor", None, "dp"),
            P(None, "dp"),
            P(None, "dp", "tensor"),
            P(None, "tensor", "dp"),
            P("tensor", "dp"),
            P("tensor", "dp"),
            P("dp", "tensor"),
            P("tensor", "dp"),
            P("tensor", "dp"),
            P(None, "dp"),
        ),
        out_specs=(
            P("dp", "tensor", None),
            P("dp", "tensor", None),
            P("dp", "tensor"),
            P("tensor", None, "dp"),
            P(None, "dp"),
            P(None, "dp", "tensor"),
            P(None, "tensor", "dp"),
            P("tensor", "dp"),
            P("tensor", "dp"),
            P("dp", "tensor"),
            P("tensor", "dp"),
            P("tensor", "dp"),
            P(None, "dp"),
        ),
        check_vma=False,
    )
```

time: 1450 us -> 512 us (0.35)
  waiting for transfers between devices: 645 us -> 0.01 us
  Pallas kernels: 0 us -> 312 us
  blocking collectives: 334 us -> 134 us
  matrix products: 178 us -> 4.59 us
  other arithmetic: 119 us -> 11.4 us
  local copies, waits for them, and re-layouts: 124 us -> 32.5 us
  between operations: 22 us -> 2.13 us
    all_gather x12 -> x0, waiting for transfers between devices: 345 us -> none  [the longest x2 109 us: local(): feedforward_grad_total = lax.all_gather(d_ffn, 'tensor', axis=1, tiled=True)]
    pallas_call x0 -> x1, Pallas kernels: none -> 312 us  [block_call(): pl.pallas_call(functools.partial(block_kernel, dm), out_shape=(s((2, R, C...]
    reduce_scatter x7 -> x0, waiting for transfers between devices: 294 us -> none  [the longest x1 66 us: local(): lax.psum_scatter(accum[1], 'dp', scatter_dimension=2, tiled=True)]
    unnamed x4 -> x2, blocking collectives: 229 us -> 26.4 us
    dot_general x84 -> x5, matrix products: 178 us -> 4.59 us  [the longest x1 1.2 us: local(): jnp.einsum('sc,cjd->sjd', silu_low, w_ada, preferred_element_type=F32)]
    reduce_sum x35 -> x2, other arithmetic: 81.4 us -> 0.71 us  [local(): b_ada_grad = jnp.sum(dmod.astype(F32), axis=0)]
    unnamed x307 -> x59, local copies, waits for them, and re-layouts: 73.3 us -> 12.1 us
    psum x2 -> x3, blocking collectives: 38 us -> 84.5 us  [the longest x1 37.2 us: local(): vec = lax.psum(jnp.concatenate([by_core, vec[nh + nf:]]), ('dp', 'tensor'))]
  transfers between devices with their start and end apart: 28 -> 3, of which waited for: 19 -> 0; matrix products, arithmetic and copies ran while one was open for 26% -> 6% of each run, Pallas kernels for 0% -> 0%
where the time goes in v1:
time: 512 us; the launch traced here: 504 us
  Pallas kernels  312 us (61%)
  blocking collectives  134 us (26%)
  local copies, waits for them, and re-layouts  32.5 us (6%)
  other arithmetic  11.4 us (2%)
  starting transfers between devices  6.97 us (1%)
    pallas_call x1, Pallas kernels, block_call(): pl.pallas_call(functools.partial(block_kernel, dm), out_shape=(s((2, R, C...  312 us
    psum x1, blocking collectives, local(): vec = lax.psum(jnp.concatenate([by_core, vec[nh + nf:]]), ('dp', 'tensor'))  37.2 us
    unnamed x2, blocking collectives  26.4 us
    psum x1, blocking collectives, local(): cond = lax.psum(jnp.dot(hot, class_table, preferred_element_type=F32), 'dp')  24.7 us
    psum x1, blocking collectives, local(): lax.psum(jnp.einsum('sjd,cjd->sc', dmod, w_ada, preferred_element_type=F3...  22.6 us
    all_gather x1, blocking collectives, local(): dmod = lax.all_gather(dmod[::2], 'tensor', axis=1)  13.7 us
    unnamed x59, local copies, waits for them, and re-layouts  12.1 us
  transfers between devices with their start and end apart: 3, of which 0 were waited for; matrix products, arithmetic and copies ran while one was open for 6% of the time, Pallas kernels for 0%

profile of v1, /device:TPU:24, one launch (start us, length us, event | category | flops | bytes accessed | tf_op | source)
XLA Modules:
  0.0 503.8 jit_solution(6526544190415411843)
XLA Ops:
  0.8 1.0 fusion.15
  1.8 24.7 %psum.21 = f32[16,256]{1,0:T(8,128)S(1)} all-reduce(f32[16,256]{1,0:T(8,128)S(1)} %fusion.15), channel_id=1, replica_groups=mesh['dp'=8,'tensor'=4] {'dp'}, use_global_device_ids=true, to_apply=%region_0.1 | all-reduce | flops 4096 | bytes 32768 | tf_op jit(solution)/shard_map/psum | solution.py:729
  26.5 1.2 fusion.18
  27.7 15.8 %all-reduce.4 = f32[4,4,6,128]{3,0,2,1:T(4,128)S(1)} all-reduce(f32[4,4,6,128]{3,0,2,1:T(4,128)S(1)} %copy.179), channel_id=5, replica_groups=mesh['dp'=8,'tensor'=4] {'tensor'}, use_global_device_ids=true, to_apply=%region_1.2.clone | all-reduce | flops 12288 | bytes 98304
  43.5 0.7 convert_element_type.56
  44.2 1.3 fusion.30
  45.5 0.7 fusion.13
  46.2 0.6 broadcast_in_dim.51
  46.8 3.3 all-to-all-start
  50.2 0.8 copy.181
  51.1 0.8 reshape.173
  51.8 0.8 reshape.174
  53.2 0.7 pad_maximum_fusion.4
  54.0 0.2 dynamic-update-slice
  54.2 10.6 %all-reduce.3 = bf16[1920]{0:T(1024)(128)(2,1)S(1)} all-reduce(bf16[1920]{0:T(1024)(128)(2,1)S(1)} %dynamic-update-slice), channel_id=2, replica_groups=mesh['dp'=8,'tensor'=4] {'tensor'}, use_global_device_ids=true, to_apply=%add.3 | all-reduce | flops 1920 | bytes 7680
  64.9 9.4 %all-gather.3 = bf16[8,4,480]{2,1,0:T(4,128)(2,1)S(1)} all-gather(bf16[1,4,480]{2,1,0:T(4,128)(2,1)S(1)} %reshape.225), channel_id=3, replica_groups=mesh['dp'=8,'tensor'=4] {'dp'}, dimensions={0}, use_global_device_ids=true | all-gather | bytes 34560 | tf_op jit(solution)/shard_map/all_gather | solution.py:740
  75.9 0.2 copy.172
  76.3 0.2 copy.174
  76.9 0.6 iota_compare_fusion.2
  77.5 0.2 copy-done.1
  77.7 0.5 convert_element_type.53
  78.2 0.2 copy.177
  78.4 0.9 pad.11.xb
  79.3 0.5 copy-done
  79.8 0.5 convert_element_type.54
  80.3 0.2 copy.178
  80.4 0.9 pad.12.dyb
  81.4 0.6 concatenate.21.hp
  82.2 0.9 select_convert_fusion
  83.1 0.6 pad_maximum_fusion.2.mods
  83.7 0.6 broadcast_in_dim.54.hb
  84.4 312.1 %shard_map.246 = (f32[2,128,1536]{2,1,0:T(8,128)}, bf16[2,176,1024]{2,1,0:T(8,128)(2,1)}, bf16[2,176,1024]{2,1,0:T(8,128)(2,1)}, f32[8,1024]{1,0:T(8,128)}, f32[4,8,128]{2,1,0:T(8,128)}, /*index=5*/f32[4,8,512]{2,1,0:T(8,128)}) custom-call(bf16[2,128,1536]{2,1,0:T(8,128)(2,1)} %copy-done.15, bf16[2,176,1024]{2,1,0:T(8,128)(2,1)} %pad.11.xb, ...), custom_call_target="tpu_custom_call" | custom-call | flops 30000001024 | bytes 10000000 | tf_op jit(solution)/shard_map/pallas_call | solution.py:694
  396.5 0.8 slice.118
  397.3 0.8 slice.119
  398.2 0.7 broadcast_select_fusion
  399.0 0.8 multiply_bitcast_fusion
  399.7 37.2 %psum.23 = f32[9216]{0:T(1024)S(1)} all-reduce(f32[9216]{0:T(1024)S(1)} %pad_maximum_fusion.1), channel_id=1, replica_groups=mesh['dp'=8,'tensor'=4] {'dp','tensor'}, use_global_device_ids=true, to_apply=%region_4.5 | all-reduce | flops 9216 | bytes 73728 | tf_op jit(solution)/shard_map/psum | solution.py:802
  437.1 1.8 slice_bitcast_fusion.2
  438.9 0.9 slice_bitcast_fusion
  439.7 0.6 fusion.10
  440.5 0.7 constant_dynamic-slice_fusion.3
  441.2 0.7 constant_dynamic-slice_fusion
  441.9 0.6 fusion.27
  442.5 0.6 slice.130
  443.2 0.8 copy.198
  444.0 0.8 copy.199
  444.7 3.6 all-to-all-start.1
  448.3 3.2 copy_add_fusion
  451.5 0.8 pad_maximum_fusion
  452.3 1.2 constant_dynamic-slice_fusion.2
  453.5 1.4 copy.207
  454.9 1.9 copy.205
  456.8 2.2 copy.203
  459.0 2.2 copy.204
  461.1 0.2 copy.201
  461.3 1.0 copy.206
  462.3 1.0 copy.202
  463.3 0.8 copy.200
  464.1 13.7 %all-gather.2 = bf16[4,24,128]{2,0,1:T(4,128)(2,1)S(1)} all-gather(bf16[4,6,128]{2,0,1:T(4,128)(2,1)S(1)} %copy.193), channel_id=4, replica_groups=mesh['dp'=8,'tensor'=4] {'tensor'}, dimensions={1}, use_global_device_ids=true | all-gather | bytes 30720 | tf_op jit(solution)/shard_map/all_gather | solution.py:790
  477.9 1.2 fusion.3
  479.1 0.2 convolution_bitcast_fusion
  479.4 22.6 %psum.22 = f32[16,256]{1,0:T(8,128)S(1)} all-reduce(f32[16,256]{1,0:T(8,128)S(1)} %convolution_bitcast_fusion), channel_id=1, replica_groups=mesh['dp'=8,'tensor'=4] {'dp'}, use_global_device_ids=true, to_apply=%region_2.3 | all-reduce | flops 4096 | bytes 32768 | tf_op jit(solution)/shard_map/psum | solution.py:794
  502.0 1.0 fusion.8
  503.0 0.6 reduce_sum.9
  (105 shorter events, 3.0 us)
Async XLA Ops:
  0.6 81.3 %collective-permute-start = (s32[2,680]{1,0:T(2,128)}, s32[2,680]{1,0:T(2,128)S(1)}, u32[]{:S(2)}, u32[]{:S(2)}) collective-permute-start(s32[2,680]{1,0:T(2,128)} %param.18), channel_id=1, source_target_pairs={{0,4},{4,0},{8,12},{12,8},{16,20},{20,16},{24,28},{28,24},{1,5},{5... | collective-permute-start | bytes 16328 | tf_op jit(solution)/shard_map/ppermute | solution.py:755
  0.7 26.9 %copy-start.18 = (s32[128]{0:T(128)}, s32[128]{0:T(128)S(1)}, u32[]{:S(2)}) copy-start(s32[128]{0:T(128)S(1)} %iota_add_fusion) | copy-start | bytes 1540
  26.5 48.0 %copy-start.8 = (f32[16,256]{1,0:T(8,128)}, f32[16,256]{1,0:T(8,128)S(1)}, u32[]{:S(2)}) copy-start(f32[16,256]{1,0:T(8,128)S(1)} %psum.21) | copy-start | bytes 49156
  26.5 49.2 %copy-start.12 = (bf16[3,128,256]{2,1,0:T(8,128)(2,1)S(1)}, bf16[3,128,256]{2,1,0:T(8,128)(2,1)}, u32[]{:S(2)}) copy-start(bf16[3,128,256]{2,1,0:T(8,128)(2,1)} %param.22) | copy-start | bytes 589828
  46.8 36.3 %all-to-all-start = ((f32[8,6,128]{2,1,0:T(8,128)}), f32[8,6,128]{2,1,0:T(8,128)S(1)}, u32[]{:S(2)}, u32[]{:S(2)}) async-start(f32[8,6,128]{2,1,0:T(8,128)} %bitcast.16), calls=%async_computation | async-start | bytes 65536 | tf_op jit(solution)/shard_map/all_to_all | solution.py:735
  74.8 1.3 copy-start.13
  74.9 1.4 copy-start.10
  75.5 1.2 copy-start.11
  76.3 1.4 copy-start.1
  76.9 1.4 copy-start.15
  78.1 1.6 copy-start
  80.2 1.8 copy-start.16
  396.5 42.4 %copy-start.4 = (f32[2,128,1536]{2,1,0:T(8,128)S(1)}, f32[2,128,1536]{2,1,0:T(8,128)}, u32[]{:S(2)}) copy-start(f32[2,128,1536]{2,1,0:T(8,128)} %get-tuple-element.22) | copy-start | bytes 4718596
  437.1 2.7 copy-start.14
  444.7 19.4 %all-to-all-start.1 = ((bf16[8,6,128]{2,1,0:T(8,128)(2,1)}), bf16[8,6,128]{2,1,0:T(8,128)(2,1)S(1)}, u32[]{:S(2)}, u32[]{:S(2)}) async-start(bf16[8,6,128]{2,1,0:T(8,128)(2,1)} %fusion.10), calls=%async_computation.1 | async-start | bytes 32768 | tf_op jit(solution)/shard_map/all_to_all | solution.py:789
  448.3 3.2 copy-start.5
  448.3 3.2 copy-start.6
  459.0 2.2 copy-start.2
  461.1 2.2 copy-start.7
  461.3 16.6 %copy-start.9 = (f32[16,256]{1,0:T(8,128)S(1)}, f32[16,256]{1,0:T(8,128)}, u32[]{:S(2)}) copy-start(f32[16,256]{1,0:T(8,128)} %copy-done.8) | copy-start | bytes 49156
  461.3 17.7 %copy-start.3 = (bf16[256,6,128]{2,0,1:T(8,128)(2,1)S(1)}, bf16[256,6,128]{2,0,1:T(8,128)(2,1)}, u32[]{:S(2)}) copy-start(bf16[256,6,128]{2,0,1:T(8,128)(2,1)} %param.20) | copy-start | bytes 1179652
  462.3 39.6 %copy-start.17 = (s32[16]{0:T(128)S(1)}, s32[16]{0:T(128)}, u32[]{:S(2)}) copy-start(s32[16]{0:T(128)} %param.17) | copy-start | bytes 196
  462.3 39.6 %copy-start.19 = (s32[128]{0:T(128)S(1)}, s32[128]{0:T(128)}, u32[]{:S(2)}) copy-start(s32[128]{0:T(128)} %copy-done.18) | copy-start | bytes 1540

commit v2 on v1

v2 whole, which is shorter than its diff:
```python
import functools

import jax
import jax.numpy as jnp
from jax import lax
from jax.experimental import pallas as pl
from jax.experimental.pallas import tpu as pltpu
from jax.sharding import PartitionSpec as P

MESH = pl.DeviceIdType.MESH
F32, B16 = jnp.float32, jnp.bfloat16
SLOTS = 3
CHUNK = 256
EPS = 1e-06
FAR = 256.0


def dot(a, b):
    return lax.dot_general(a, b, (((1,), (0,)), ((), ())), preferred_element_type=F32)


def dot_nt(a, b):
    return lax.dot_general(a, b, (((1,), (1,)), ((), ())), preferred_element_type=F32)


def dot_tn(a, b):
    return lax.dot_general(a, b, (((0,), (0,)), ((), ())), preferred_element_type=F32)


def split_dot(a, b):
    high = a.astype(B16)
    low = (a - high.astype(F32)).astype(B16)
    return dot(high, b) + dot(low, b)


def row_sum(a):
    return jnp.sum(a, axis=0, keepdims=True)


class Dims:
    def __init__(self, dp, tensor, rows, width, head, hidden):
        self.T = tensor
        self.NC = dp // 2
        self.bits = self.NC.bit_length() - 1
        self.Q = rows
        self.M = rows * tensor
        self.D = width
        self.hd = head
        self.hq = width // tensor // 2
        self.fu = hidden // tensor // 2
        self.R = width // dp
        self.C = 4 * self.hq + 2 * self.fu
        self.NCH = width // CHUNK
        self.inside = self.R % 128 == 0 and self.NC <= 8 and hidden // tensor <= width
        self.W = self.hq + self.fu + width
        hq, fu, half = self.hq, self.fu, self.fu // 2
        up, down = 4 * hq, 4 * hq + fu
        self.up, self.down, self.half = up, down, half
        self.pieces = ((0, hq), (hq, hq), (2 * hq, hq), (3 * hq, hq), (up, half), (down, half), (up + half, half), (down + half, half))
        self.sums_order = (5, 4, 7, 6, 3, 2, 1, 0)
        assert 1 << self.bits == self.NC


class Refs:
    pass


def block_kernel(dm, names, *refs):
    m = Refs()
    for name, ref in zip(names, refs):
        if name.startswith("rb"):
            m.rb = getattr(m, "rb", []) + [ref]
        else:
            setattr(m, name, ref)
    T, NC, NB, Q, M, D, R, C = dm.T, dm.NC, dm.bits, dm.Q, dm.M, dm.D, dm.R, dm.C
    hq, fu, NCH, half = dm.hq, dm.fu, dm.NCH, dm.half
    TH = T // 2
    NP = len(dm.pieces)
    wall, xs, dys, h1, h2 = m.wall, m.xs, m.dys, m.h1, m.h2
    mods, hp, hb, sums, hsum, fsum = m.mods, m.hp, m.hb, m.sums, m.hsum, m.fsum
    dpi = lax.axis_index("dp")
    me_z = lax.axis_index("tensor")
    core = lax.rem(dpi, 2)
    chip = dpi // 2
    mybit = [lax.rem(chip // (1 << b), 2) for b in range(NB)]
    partner = (dpi + 1 - 2 * core, me_z)

    def z_dev(off):
        return (dpi, lax.rem(me_z + off, T))

    def bit_dev(b):
        return (dpi + (1 - 2 * mybit[b]) * (2 << b), me_z)

    def chip_dev(k):
        return (lax.rem(chip + k, NC) * 2 + core, me_z)

    bar = pltpu.get_barrier_semaphore()
    friends = [partner] + [z_dev(k) for k in range(1, T)]
    friends += [chip_dev(k) for k in range(1, NC)] if dm.inside else [bit_dev(b) for b in range(NB)]
    for dev in friends:
        pl.semaphore_signal(bar, inc=1, device_id=dev, device_id_type=MESH)
    pl.semaphore_wait(bar, len(friends))

    def rdma(src, dst, ss, rs, dev):
        return pltpu.make_async_remote_copy(
            src_ref=src, dst_ref=dst, send_sem=ss, recv_sem=rs, device_id=dev, device_id_type=MESH
        )

    every = slice(None)

    def place(fixed):
        return tuple(fixed.get(b, every) for b in reversed(range(NB)))

    mine = place({b: mybit[b] for b in range(NB)})

    def cols(pc):
        return pl.ds(*dm.pieces[pc])

    def core_rows(c):
        return pl.ds(pl.multiple_of(c * R, R), R)

    def core_copy(pc):
        dst = wall.at[(me_z,) + mine + (core_rows(core), cols(pc))]
        return rdma(m.ws.at[1 - core, :, cols(pc)], dst, m.c_s.at[pc], m.c_r.at[pc], partner)

    def core_local(pc):
        dst = wall.at[(me_z,) + mine + (core_rows(core), cols(pc))]
        return pltpu.make_async_copy(m.ws.at[core, :, cols(pc)], dst, m.c_l.at[pc])

    def z_copy(pc, off):
        part = wall.at[(me_z,) + mine + (every, cols(pc))]
        return rdma(part, part, m.z_s.at[pc, off - 1], m.z_r.at[pc, off - 1], z_dev(off))

    order = [list(range(NB)), list(reversed(range(NB)))]

    def half_z(h):
        return pl.ds(h * TH, TH)

    def p_copy(pc, step, h, landing):
        b = order[h][step]
        fixed = {k: mybit[k] for k in order[h][step:]}
        if landing:
            fixed[b] = 1 - mybit[b]
        part = wall.at[(half_z(h),) + place(fixed) + (every, cols(pc))]
        return rdma(part, part, m.p_s.at[pc, step, h], m.p_r.at[pc, step, h], bit_dev(b))

    def gather_stage(pc, s):
        if not 0 <= pc < NP:
            return
        if s == 0:
            core_local(pc).wait()
            other = wall.at[(me_z,) + mine + (core_rows(1 - core), cols(pc))]
            rdma(other, other, m.c_s.at[pc], m.c_r.at[pc], partner).wait_recv()
            for off in range(1, T):
                z_copy(pc, off).start()
            return
        if s == 1:
            for off in range(1, T):
                part = wall.at[(lax.rem(me_z - off + T, T),) + mine + (every, cols(pc))]
                rdma(part, part, m.z_s.at[pc, off - 1], m.z_r.at[pc, off - 1], z_dev(off)).wait_recv()
        for h in range(2):
            if s > 1:
                p_copy(pc, s - 2, h, True).wait_recv()
            if s <= NB:
                p_copy(pc, s - 1, h, False).start()

    ticks = [0]

    def gather_tick():
        t = ticks[0]
        ticks[0] += 1
        for s in range(NB, -1, -1):
            gather_stage(t - s, s)
        gather_stage(t - NB - 1, NB + 1)

    def gather_until(pc):
        while ticks[0] <= pc + NB + 1:
            gather_tick()

    def gather_sent(which):
        for pc in which:
            core_copy(pc).wait_send()
            for off in range(1, T):
                z_copy(pc, off).wait_send()
            for step in range(NB):
                for h in range(2):
                    p_copy(pc, step, h, False).wait_send()

    owner = me_z // 2 == core

    def tok_copy(which, src, dst, i):
        zt = 2 * core + i
        return rdma(src.at[i], dst.at[me_z], m.x_s.at[which, i], m.x_r.at[which, me_z], (dpi, zt))

    def tok_start(which, src, dst):
        for i in range(2):
            @pl.when(2 * core + i != me_z)
            def _():
                tok_copy(which, src, dst, i).start()

            @pl.when(2 * core + i == me_z)
            def _():
                pltpu.make_async_copy(src.at[i], dst.at[me_z], m.x_l.at[which]).start()

    def tok_forward(which, dst):
        return rdma(dst, dst, m.x_f.at[which, 0], m.x_f.at[which, 1], partner)

    def tok_wait(which, src, dst):
        @pl.when(owner)
        def _():
            for off in range(1, T):
                zq = lax.rem(me_z + off, T)
                rdma(dst.at[zq], dst.at[zq], m.x_s.at[which, 0], m.x_r.at[which, zq], (dpi, zq)).wait_recv()
            pltpu.make_async_copy(src.at[0], dst.at[me_z], m.x_l.at[which]).wait()
            tok_forward(which, dst).start()

        @pl.when(jnp.logical_not(owner))
        def _():
            tok_forward(which, dst).wait_recv()

    def tok_sent(which, src, dst):
        for i in range(2):
            @pl.when(2 * core + i != me_z)
            def _():
                tok_copy(which, src, dst, i).wait_send()

        @pl.when(owner)
        def _():
            tok_forward(which, dst).wait_send()

    back_from = (m.n2, m.ab)

    def back_copy(which, dst, zq):
        i = lax.rem(me_z, 2)
        return rdma(back_from[which].at[zq], dst.at[i], m.o_s.at[which, zq], m.o_r.at[which, i], (dpi, zq))

    def back_start(which, dst):
        @pl.when(owner)
        def _():
            for off in range(1, T):
                back_copy(which, dst, lax.rem(me_z + off, T)).start()
            pltpu.make_async_copy(back_from[which].at[me_z], dst.at[lax.rem(me_z, 2)], m.o_l.at[which]).start()

    def back_wait(which, dst):
        @pl.when(owner)
        def _():
            for off in range(1, T):
                back_copy(which, dst, lax.rem(me_z + off, T)).wait_send()
            pltpu.make_async_copy(back_from[which].at[me_z], dst.at[lax.rem(me_z, 2)], m.o_l.at[which]).wait()

        for i in range(2):
            @pl.when(2 * core + i != me_z)
            def _():
                rdma(dst.at[i], dst.at[i], m.o_s.at[which, 0], m.o_r.at[which, i], (dpi, 2 * core + i)).wait_recv()

    def x_copy(k, n):
        return rdma(m.send.at[n], m.recv.at[k % 2, n], m.e_s.at[k, n], m.e_r.at[k, n], partner)

    def exchange(k, n, value):
        m.send[n] = value.astype(B16).reshape(T, Q, CHUNK)
        x_copy(k, n).start()

    def exchange_wait(k):
        for n in range(NCH):
            x_copy(k, n).wait_recv()

    def exchange_sent(k):
        for n in range(NCH):
            x_copy(k, n).wait_send()

    def both(k, t):
        parts = [m.send[n, t].astype(F32) + m.recv[k % 2, n, t].astype(F32) for n in range(NCH)]
        return jnp.concatenate(parts, axis=-1)

    def wz(z, lo, n):
        return wall[(z,) + (every,) * NB + (every, pl.ds(lo, n))].reshape(D, n)

    def wrows(z, n, lo, width):
        per = CHUNK // (2 * R)
        low = per.bit_length() - 1
        top = n * per
        fixed = {b: (top >> b) & 1 for b in range(low, NB)}
        return wall[(z,) + place(fixed) + (every, pl.ds(lo, width))].reshape(CHUNK, width)

    def wrows_all(n, lo, width):
        return jnp.concatenate([wrows(z, n, lo, width) for z in range(T)], axis=-1)

    def wstore(z, lo, n, value):
        wall[(z,) + (every,) * NB + (every, pl.ds(lo, n))] = value.astype(B16).reshape(
            (2,) * NB + (2 * R, n)
        )

    def all_z(ref):
        return jnp.concatenate([ref[z] for z in range(T)], axis=-1)

    def whole(ref):
        return ref[...].reshape(M, D)

    def mod(r):
        return mods[r : r + 1, :]

    def transpose_into(dst, ref):
        for n in range(D // 128):
            block = ref[:, :, n * 128 : (n + 1) * 128].reshape(M, 128)
            dst[n * 128 : (n + 1) * 128, :] = block.T

    place_of = {pc: j for j, pc in enumerate(dm.sums_order)}

    def rs_fixed(step, h, away):
        order_r = order[h][::-1]
        fixed = {k: mybit[k] for k in order_r[: step + 1]}
        b = order_r[step]
        if away:
            fixed[b] = 1 - mybit[b]
        return b, fixed

    def rs_copy(j, step, h):
        pc = dm.sums_order[j]
        b, fixed = rs_fixed(step, h, True)
        part = wall.at[(half_z(h),) + place(fixed) + (every, cols(pc))]
        buf = m.rb[step].at[(j % SLOTS, h) + (every,) * (NB - step) + (every, pl.ds(0, dm.pieces[pc][1]))]
        return rdma(part, buf, m.rs_s.at[j, step, h], m.rs_r.at[j, step, h], bit_dev(b))

    def rs_start(j, step, h):
        if j >= SLOTS:
            pl.semaphore_wait(m.free.at[step, h], 1)
        rs_copy(j, step, h).start()

    def rs_add(j, step, h):
        pc = dm.sums_order[j]
        rs_copy(j, step, h).wait_recv()
        b, fixed = rs_fixed(step, h, False)
        rest = [k for k in reversed(range(NB)) if k not in fixed]
        slot, width = j % SLOTS, dm.pieces[pc][1]

        def one(i, carry):
            zz, r = i // (1 << len(rest)), lax.rem(i, 1 << len(rest))
            at = dict(fixed)
            inner = ()
            for pos, k in enumerate(rest):
                v = lax.rem(r // (1 << (len(rest) - 1 - pos)), 2)
                at[k] = v
                inner += (v,)
            where = (h * TH + zz,) + place(at) + (every, cols(pc))
            got = m.rb[step][(slot, h, zz) + inner + (every, pl.ds(0, width))]
            wall[where] = (wall[where].astype(F32) + got.astype(F32)).astype(B16)
            return carry

        lax.fori_loop(0, TH << len(rest), one, 0)
        if j + SLOTS < NP:
            pl.semaphore_signal(m.free.at[step, h], inc=1, device_id=bit_dev(b), device_id_type=MESH)

    def rz_copy(j, off):
        pc = dm.sums_order[j]
        part = wall.at[(lax.rem(me_z + off, T),) + mine + (every, cols(pc))]
        return rdma(part, m.zb.at[off - 1, :, cols(pc)], m.rz_s.at[j, off - 1], m.rz_r.at[j, off - 1], z_dev(off))

    def fin_copy(j):
        pc = dm.sums_order[j]
        return rdma(m.fbuf.at[:, cols(pc)], m.fin.at[core, :, cols(pc)], m.f_s.at[j], m.f_r.at[j], partner)

    def rs_event(j, s):
        pc = dm.sums_order[j]
        if s <= NB:
            for h in range(2):
                rs_add(j, s - 1, h)
                if s < NB:
                    rs_start(j, s, h)
            if s == NB:
                for off in range(1, T):
                    rz_copy(j, off).start()
            return
        for off in range(1, T):
            rz_copy(j, off).wait_recv()

        def total(rows):
            acc = wall[(me_z,) + mine + (rows, cols(pc))].astype(F32)
            for off in range(1, T):
                acc = acc + m.zb[off - 1, rows, cols(pc)].astype(F32)
            return acc

        m.fbuf[:, cols(pc)] = total(core_rows(1 - core))
        fin_copy(j).start()
        m.fin[core, :, cols(pc)] = total(core_rows(core))

    events = sorted(((j, s) for j in range(NP) for s in range(1, NB + 2)), key=lambda e: (e[0] + 1.5 * e[1], e[0]))
    begun = set()

    def pump(count):
        while count and events and (events[0][0], 1) in begun:
            rs_event(*events.pop(0))
            count -= 1

    def rs_begin(pc, h):
        j = place_of[pc]
        while (j - SLOTS, 1) in events:
            pump(1)
        rs_start(j, 0, h)
        begun.add((j, h))

    def rs_end():
        for j in range(NP):
            for step in range(NB):
                for h in range(2):
                    rs_copy(j, step, h).wait_send()
            for off in range(1, T):
                rz_copy(j, off).wait_send()
            fin_copy(j).wait()

    def small(src, dst, k, dev):
        return rdma(src, dst, m.s_s.at[k], m.s_r.at[k], dev)

    def sum_step(acc, got, i, base, sign):
        dev = partner if i < sign else bit_dev(i - sign)
        return small(acc.at[i], got.at[i], base + i, dev)

    def sum_finish(acc, got, i, base, sign):
        sum_step(acc, got, i, base, sign).wait_recv()
        acc[i + 1] = acc[i] + got[i]

    S_SID = 0
    S_M1 = 1
    S_M2 = S_M1 + NB + 1
    S_SM = S_M2 + T - 1
    S_M3 = S_SM + T - 1
    S_M4 = S_M3 + NC - 1
    S_B1 = S_M4 + 1
    S_B2 = S_B1 + NC - 1
    S_B3 = S_B2 + T - 1
    S_PZ = S_B3 + NB + 1
    S_PB = S_PZ + T - 1
    S_PC = S_PB + NB

    sid_copy = small(m.sid, m.sidr, S_SID, partner)
    sid_copy.start()
    if dm.inside:
        m.macc[0] = m.m1[...]
        sum_step(m.macc, m.mrec, 0, S_M1, 1).start()
    core_copy(0).start()
    core_local(0).start()
    tok_start(0, m.xb, xs)
    for pc in range(1, NP):
        core_copy(pc).start()
        core_local(pc).start()
    gather_tick()
    sums[...] = jnp.zeros_like(sums)
    hsum[...] = jnp.zeros_like(hsum)
    fsum[...] = jnp.zeros_like(fsum)

    if dm.inside:
        for i in range(NB + 1):
            sum_finish(m.macc, m.mrec, i, S_M1, 1)
            if i < NB:
                sum_step(m.macc, m.mrec, i + 1, S_M1, 1).start()
        m.sm[me_z] = m.macc[NB + 1, 8:16, :]
        for off in range(1, T):
            small(m.sm.at[me_z], m.sm.at[me_z], S_SM + off - 1, z_dev(off)).start()
        m.cond[...] = m.macc[NB + 1, 0:8, :]
        width = D // T
        for zz in range(T):
            c = m.cond[:, zz * width : (zz + 1) * width]
            low = (c / (1.0 + jnp.exp(-c))).astype(B16)
            rows = [dot(low, m.wada[j]) for j in range(6)] + [jnp.zeros((8, 2 * R), F32)]
            m.m2s[zz] = jnp.concatenate(rows, axis=-1)
        for off in range(1, T):
            small(m.m2s.at[lax.rem(me_z + off, T)], m.m2r.at[off - 1], S_M2 + off - 1, z_dev(off)).start()

    gather_tick()

    if dm.inside:
        for off in range(1, T):
            small(m.m2s.at[0], m.m2r.at[off - 1], S_M2 + off - 1, z_dev(off)).wait_recv()
        m.m3c[core, chip] = m.m2s[me_z] + sum(m.m2r[k] for k in range(T - 1)) + m.badd[...]
        own = m.m3c.at[core, chip]
        for k in range(1, NC):
            small(own, own, S_M3 + k - 1, chip_dev(k)).start()
        for k in range(1, NC):
            got = m.m3c.at[core, lax.rem(chip - k + NC, NC)]
            small(got, got, S_M3 + k - 1, chip_dev(k)).wait_recv()
        small(m.m3c.at[core], m.m3c.at[core], S_M4, partner).start()
        for off in range(1, T):
            got = m.sm.at[lax.rem(me_z - off + T, T)]
            small(got, got, S_SM + off - 1, z_dev(off)).wait_recv()
        head_cols = pl.ds(pl.multiple_of(core * hq, hq), hq)
        for z in range(T):
            for r in range(3):
                hp[z, r : r + 1, :] = m.sm[z, r + 1 : r + 2, head_cols]
            hp[z, 3:4, :] = 1.0 / hp[z, 2:3, :]
            hb[z, 0:1, :] = m.sm[z, 0:1, pl.ds(pl.multiple_of(core * fu, fu), fu)]
        got = m.m3c.at[1 - core]
        small(got, got, S_M4, partner).wait_recv()
        for c in range(2):
            for p in range(NC):
                row = m.m3c[c, p, pl.ds(chip, 1), :]
                d = 2 * p + c
                for j in range(8):
                    mods[j : j + 1, d * R : (d + 1) * R] = row[:, j * R : (j + 1) * R]

    got = small(m.sidr, m.sidr, S_SID, partner)
    got.wait_recv()
    pick = lax.rem(me_z, 2)
    ids = jnp.where(owner, m.sid[pl.ds(pick, 1), :], m.sidr[pl.ds(pick, 1), :])
    lanes = lax.broadcasted_iota(jnp.int32, (128, 1), 0).astype(F32)
    m.psi[...] = jnp.where(lanes > ids, FAR, 0.0).astype(B16).T
    m.phi[...] = jnp.where(lanes == ids, -1.0, 0.0).astype(B16).T
    tok_wait(0, m.xb, xs)

    def ln(rows):
        centred = rows - jnp.mean(rows, axis=-1, keepdims=True)
        inv = lax.rsqrt(jnp.mean(centred * centred, axis=-1, keepdims=True) + EPS)
        return centred * inv, inv

    def first_norm(t, carry):
        normed, _ = ln(xs[t].astype(F32))
        h1[t] = (normed * (1.0 + mod(2)) + mod(4)).astype(B16)
        return carry

    lax.fori_loop(0, T, first_norm, 0)
    tok_start(1, m.dyb, dys)
    gather_until(2)

    lane = lax.broadcasted_iota(jnp.int32, (1, hq), 1)
    halves = [(lane // dm.hd) == k for k in range(hq // dm.hd)]
    bi = lax.broadcasted_iota(jnp.int32, (hq, hq), 0) // dm.hd
    bj = lax.broadcasted_iota(jnp.int32, (hq, hq), 1) // dm.hd
    same_head = (bi == bj).astype(B16)

    def qkv(z, carry):
        t = dot(whole(h1), wz(z, 0, 3 * hq))
        q = t[:, :hq] + hp[z, 0:1, :]
        k = t[:, hq : 2 * hq]
        v = t[:, 2 * hq :] + hp[z, 1:2, :]
        qi = lax.rsqrt(split_dot(q * q, same_head) + EPS)
        ki = lax.rsqrt(split_dot(k * k, same_head) + EPS)
        m.qs[z] = (q * qi * hp[z, 2:3, :]).astype(B16)
        m.ks[z] = (k * ki).astype(B16)
        m.vs[z] = v.astype(B16)
        m.rq[z] = qi.astype(B16)
        m.rk[z] = ki.astype(B16)
        return carry

    lax.fori_loop(0, T, qkv, 0)
    zero16 = jnp.zeros((), B16)

    def expo(z, k, q_all, k_all):
        q_one = jnp.where(halves[k], q_all, zero16)
        left = jnp.concatenate([q_one, m.psi[...]], axis=1)
        right = jnp.concatenate([k_all, m.phi[...]], axis=1)
        return q_one, jnp.exp(dot_nt(left, right)).astype(B16)

    def attend(z, carry):
        q_all, k_all, v_all = m.qs[z], m.ks[z], m.vs[z]
        v_ones = jnp.concatenate([v_all, jnp.ones((M, hq), B16)], axis=1)
        mixed = inverse = None
        for k in range(hq // dm.hd):
            _, e = expo(z, k, q_all, k_all)
            both_ = dot(e, v_ones)
            inv = 1.0 / both_[:, hq:]
            one = both_[:, :hq] * inv
            mixed = one if mixed is None else jnp.where(halves[k], one, mixed)
            inverse = inv if inverse is None else jnp.where(halves[k], inv, inverse)
        m.o[z] = mixed.astype(B16)
        m.ol[z] = (mixed - mixed.astype(B16).astype(F32)).astype(B16)
        m.linv[z] = inverse
        return carry

    lax.fori_loop(0, TH, attend, 0)
    gather_until(3)
    lax.fori_loop(TH, T, attend, 0)

    o_all = all_z(m.o)
    for n in range(NCH):
        exchange(0, n, dot_nt(o_all, wrows_all(n, 3 * hq, hq)))
    tok_wait(1, m.dyb, dys)

    def out_grad(t, carry):
        d = (mod(1) * dys[t].astype(F32)).astype(B16)
        m.df[t] = d
        sums[7:8, :] += row_sum(d.astype(F32))
        return carry

    lax.fori_loop(0, T, out_grad, 0)
    exchange_wait(0)

    def second_norm(t, carry):
        a = both(0, t) + mod(6)
        m.ab[t] = a.astype(B16)
        normed, inv = ln(xs[t].astype(F32) + mod(0) * a)
        h2[t] = (normed * (1.0 + mod(3)) + mod(5)).astype(B16)
        m.n2[t] = normed.astype(B16)
        m.r2[t] = jnp.broadcast_to(inv, (Q, 128))
        return carry

    lax.fori_loop(0, T, second_norm, 0)
    exchange_sent(0)
    gather_until(4)
    transpose_into(m.xt, h2)
    transpose_into(m.xt2, m.df)

    root = 0.7978845608028654

    def hidden(k):
        lo_u, lo_d = dm.up + k * half, dm.down + k * half

        def up(z, carry):
            u = dot(whole(h2), wz(z, lo_u, half)) + hb[z, 0:1, k * half : (k + 1) * half]
            uu = u * u
            th = jnp.tanh(root * u * (1.0 + 0.044715 * uu))
            m.gk[z] = (0.5 * u * (1.0 + th)).astype(B16)
            m.duk[z] = (0.5 * (1.0 + th) + (0.5 * root) * u * (1.0 - th * th) * (1.0 + 0.134145 * uu)).astype(B16)
            return carry

        def down(z, carry):
            dg = dot(whole(m.df), wz(z, lo_d, half))
            du = (dg * m.duk[z].astype(F32)).astype(B16)
            m.duk[z] = du
            fsum[z, 0:1, k * half : (k + 1) * half] = row_sum(du.astype(F32))
            return carry

        lax.fori_loop(0, T, up, 0)
        gather_until(5 + 2 * k)
        lax.fori_loop(0, T, down, 0)

    def grads(k, begin):
        lo_u, lo_d = dm.up + k * half, dm.down + k * half

        def down_grad(z, carry):
            wstore(z, lo_d, half, dot(m.xt2[...], m.gk[z]))
            return carry

        def up_grad(z, carry):
            wstore(z, lo_u, half, dot(m.xt[...], m.duk[z]))
            return carry

        for pc, body in ((5 + 2 * k, down_grad), (4 + 2 * k, up_grad)):
            for h in range(2):
                lax.fori_loop(h * TH, (h + 1) * TH, body, 0)
                if begin:
                    rs_begin(pc, h)

    hidden(0)
    du_all, g_all = all_z(m.duk), all_z(m.gk)
    for n in range(NCH):
        m.dacc[n] = dot_nt(du_all, wrows_all(n, dm.up, half))
        m.facc[n] = dot_nt(g_all, wrows_all(n, dm.down, half))
    gather_sent((4, 5))
    grads(0, False)
    gather_until(6)
    for pc in (5, 4):
        for h in range(2):
            rs_begin(pc, h)
    hidden(1)
    du_all, g_all = all_z(m.duk), all_z(m.gk)
    for n in range(NCH):
        exchange(1, n, m.dacc[n] + dot_nt(du_all, wrows_all(n, dm.up + half, half)))
    for n in range(NCH):
        m.facc[n] = m.facc[n] + dot_nt(g_all, wrows_all(n, dm.down + half, half))
    gather_sent((0, 1, 2, 3, 6, 7))
    grads(1, True)
    transpose_into(m.xt, h1)
    tok_sent(1, m.dyb, dys)
    exchange_wait(1)

    def ln_back(e, normed, inv):
        return (e - jnp.mean(e, axis=-1, keepdims=True) - normed * jnp.mean(e * normed, axis=-1, keepdims=True)) * inv

    def mid_back(t, carry):
        dh = both(1, t)
        normed = m.n2[t].astype(F32)
        sums[3:4, :] += row_sum(dh * normed)
        sums[5:6, :] += row_sum(dh)
        step_back = ln_back(dh * (1.0 + mod(3)), normed, m.r2[t, :, 0:1])
        h2[t] = step_back.astype(B16)
        dx1 = dys[t].astype(F32) + step_back
        sums[0:1, :] += row_sum(dx1 * m.ab[t].astype(F32))
        da = (mod(0) * dx1).astype(B16)
        m.df[t] = da
        sums[6:7, :] += row_sum(da.astype(F32))
        return carry

    lax.fori_loop(0, T, mid_back, 0)
    exchange_sent(1)
    for n in range(NCH):
        exchange(2, n, m.facc[n])

    w_proj = jnp.concatenate([wz(z, 3 * hq, hq) for z in range(T)], axis=-1)
    do_all = dot(whole(m.df), w_proj).astype(B16)
    for z in range(T):
        m.do[z] = do_all[:, z * hq : (z + 1) * hq]
    transpose_into(m.xt2, m.df)
    dw = dot(m.xt2[...], all_z(m.o))
    for z in range(T):
        wstore(z, 3 * hq, hq, dw[:, z * hq : (z + 1) * hq])
    for h in range(2):
        rs_begin(3, h)
    pump(1)
    exchange_wait(2)

    def last(t, carry):
        f = both(2, t) + mod(7)
        m.n2[t] = (mod(0) * m.ab[t].astype(F32) + mod(1) * f).astype(B16)
        sums[1:2, :] += row_sum(dys[t].astype(F32) * f)
        return carry

    lax.fori_loop(0, T, last, 0)
    exchange_sent(2)
    back_start(0, m.outd)

    ends = jnp.where(lane < 2, -1.0, 0.0).astype(B16)

    def attend_back(z, carry):
        q_all, k_all, v_all = m.qs[z], m.ks[z], m.vs[z]
        dob = (m.do[z].astype(F32) * m.linv[z]).astype(B16)
        prod = dob.astype(F32) * (m.o[z].astype(F32) + m.ol[z].astype(F32))
        v_ends = jnp.concatenate([v_all, jnp.broadcast_to(ends, (M, hq))], axis=1)
        dq = dk = dv = 0.0
        for k in range(hq // dm.hd):
            q_one, e = expo(z, k, q_all, k_all)
            to_all = (bi == k).astype(B16)
            total = split_dot(prod, to_all)
            high = total.astype(B16)
            low = (total - high.astype(F32)).astype(B16)
            extra = jnp.where(lane == 0, high, jnp.where(lane == 1, low, zero16))
            d_one = jnp.where(halves[k], dob, zero16)
            dp = dot_nt(jnp.concatenate([d_one, extra], axis=1), v_ends)
            ds = (e.astype(F32) * dp).astype(B16)
            dq = dq + dot(ds, jnp.where(halves[k], k_all, zero16))
            dk = dk + dot_tn(ds, q_one)
            dv = dv + dot_tn(e, d_one)
        gain = hp[z, 2:3, :]
        q_hat = q_all.astype(F32) * hp[z, 3:4, :]
        k_hat = k_all.astype(F32)
        hsum[z, 2:3, :] = row_sum(dq * q_hat)
        eq = dq * gain
        dq = ((eq - q_hat * split_dot(eq * q_hat, same_head)) * m.rq[z].astype(F32)).astype(B16)
        dk = ((dk - k_hat * split_dot(dk * k_hat, same_head)) * m.rk[z].astype(F32)).astype(B16)
        dv = dv.astype(B16)
        hsum[z, 0:1, :] = row_sum(dq.astype(F32))
        hsum[z, 1:2, :] = row_sum(dv.astype(F32))
        m.dqkv[...] = jnp.concatenate([dq, dk, dv], axis=1)
        return carry

    for z in range(T):
        lax.fori_loop(z, z + 1, attend_back, 0)
        d_one_z = m.dqkv[...]
        for n in range(NCH):
            part = dot_nt(d_one_z, wrows(z, n, 0, 3 * hq))
            if z == T - 1:
                exchange(3, n, m.facc[n] + part)
            else:
                m.facc[n] = part if z == 0 else m.facc[n] + part
        wstore(z, 0, 3 * hq, dot(m.xt[...], d_one_z))
        if z % TH == TH - 1:
            for pc in (2, 1, 0):
                rs_begin(pc, z // TH)
        else:
            pump(2)

    if dm.inside:
        for z in range(T):
            m.pks[z] = jnp.concatenate([hsum[z], fsum[z], sums[...]], axis=-1)
        for off in range(1, T):
            small(m.pks.at[lax.rem(me_z + off, T)], m.pkr.at[off - 1], S_PZ + off - 1, z_dev(off)).start()
    pump(2)
    exchange_wait(3)

    def first_back(t, carry):
        dh = both(3, t)
        normed, inv = ln(xs[t].astype(F32))
        sums[2:3, :] += row_sum(dh * normed)
        sums[4:5, :] += row_sum(dh)
        m.ab[t] = (h2[t].astype(F32) + ln_back(dh * (1.0 + mod(2)), normed, inv)).astype(B16)
        return carry

    lax.fori_loop(0, T, first_back, 0)
    exchange_sent(3)
    back_start(1, m.gind)

    if dm.inside:
        for p in range(NC):
            d = pl.multiple_of((2 * p + core) * R, R)
            rows = [sums[j : j + 1, pl.ds(d, R)] for j in range(8)]
            m.b1s[p] = jnp.broadcast_to(jnp.concatenate(rows, axis=-1), (8, 8 * R))
        for k in range(1, NC):
            small(m.b1s.at[lax.rem(chip + k, NC)], m.b1r.at[k - 1], S_B1 + k - 1, chip_dev(k)).start()
        for off in range(1, T):
            small(m.pks.at[0], m.pkr.at[off - 1], S_PZ + off - 1, z_dev(off)).wait_recv()
        m.pka[0] = m.pks[me_z] + sum(m.pkr[k] for k in range(T - 1))
        if NB:
            sum_step(m.pka, m.pkb, 0, S_PB, 0).start()
        for k in range(1, NC):
            small(m.b1s.at[0], m.b1r.at[k - 1], S_B1 + k - 1, chip_dev(k)).wait_recv()
        row8 = lax.broadcasted_iota(jnp.int32, (8, 1), 0)
        packed = jnp.where(row8 == chip, m.b1s[chip], 0.0)
        for k in range(1, NC):
            packed = jnp.where(row8 == lax.rem(chip - k + NC, NC), m.b1r[k - 1], packed)
        m.dmodf[me_z] = packed
        for off in range(1, T):
            small(m.dmodf.at[me_z], m.dmodf.at[me_z], S_B2 + off - 1, z_dev(off)).start()
        pump(1)
        for off in range(1, T):
            got = m.dmodf.at[lax.rem(me_z - off + T, T)]
            small(got, got, S_B2 + off - 1, z_dev(off)).wait_recv()
        width = D // T
        for zz in range(T):
            acc = 0.0
            for j in range(6):
                acc = acc + dot_nt(m.dmodf[zz, :, j * R : (j + 1) * R].astype(B16), m.wada[j])
            m.bacc[0, :, zz * width : (zz + 1) * width] = acc
        sum_step(m.bacc, m.brec, 0, S_B3, 1).start()
        for i in range(NB + 1):
            if i < NB:
                sum_finish(m.pka, m.pkb, i, S_PB, 0)
                if i + 1 < NB:
                    sum_step(m.pka, m.pkb, i + 1, S_PB, 0).start()
            if i == NB:
                m.pk[core] = m.pka[NB]
                small(m.pka.at[NB], m.pk.at[core], S_PC, partner).start()
            sum_finish(m.bacc, m.brec, i, S_B3, 1)
            if i < NB:
                sum_step(m.bacc, m.brec, i + 1, S_B3, 1).start()
            pump(1)
        m.dsil[...] = m.bacc[NB + 1]
    pump(len(events))
    assert not events
    rs_end()
    tok_sent(0, m.xb, xs)
    back_wait(0, m.outd)
    back_wait(1, m.gind)
    sid_copy.wait_send()
    if dm.inside:
        for i in range(NB + 1):
            sum_step(m.macc, m.mrec, i, S_M1, 1).wait_send()
            sum_step(m.bacc, m.brec, i, S_B3, 1).wait_send()
        for i in range(NB):
            sum_step(m.pka, m.pkb, i, S_PB, 0).wait_send()
        for off in range(1, T):
            zt = lax.rem(me_z + off, T)
            small(m.sm.at[me_z], m.sm.at[me_z], S_SM + off - 1, z_dev(off)).wait_send()
            small(m.m2s.at[zt], m.m2r.at[off - 1], S_M2 + off - 1, z_dev(off)).wait_send()
            small(m.pks.at[zt], m.pkr.at[off - 1], S_PZ + off - 1, z_dev(off)).wait_send()
            small(m.dmodf.at[me_z], m.dmodf.at[me_z], S_B2 + off - 1, z_dev(off)).wait_send()
        for k in range(1, NC):
            small(m.m3c.at[core, chip], m.m3c.at[core, chip], S_M3 + k - 1, chip_dev(k)).wait_send()
            small(m.b1s.at[lax.rem(chip + k, NC)], m.b1r.at[k - 1], S_B1 + k - 1, chip_dev(k)).wait_send()
        small(m.m3c.at[core], m.m3c.at[core], S_M4, partner).wait_send()
        small(m.pka.at[NB], m.pk.at[core], S_PC, partner).wait_send()
        got = m.pk.at[1 - core]
        small(got, got, S_PC, partner).wait_recv()


def block_call(dm, ws, xb, dyb, sid, extra):
    T, NC, NB, Q, M, D, R, C, W = dm.T, dm.NC, dm.bits, dm.Q, dm.M, dm.D, dm.R, dm.C, dm.W
    hq, fu, NCH, half = dm.hq, dm.fu, dm.NCH, dm.half
    TH, NP = T // 2, len(dm.pieces)
    two = (2,) * NB
    v = pltpu.VMEM
    dma = pltpu.SemaphoreType.DMA
    any_, vm = pl.BlockSpec(memory_space=pl.ANY), pl.BlockSpec(memory_space=pltpu.VMEM)
    s = jax.ShapeDtypeStruct
    tok, heads, acc = (T, Q, D), (T, M, hq), (NCH, M, CHUNK)
    ins = {"ws": ws, "xb": xb, "dyb": dyb, "sid": sid, **extra}
    outs = {"fin": s((2, R, C), F32), "outd": s((2, Q, D), B16), "gind": s((2, Q, D), B16)}
    totals = {"sums": (8, D), "hsum": (T, 8, hq), "fsum": (T, 8, fu)}
    scratch = {"wall": v((T,) + two + (2 * R, C), B16)}
    for name in "xs dys h1 h2 ab n2 df".split():
        scratch[name] = v(tok, B16)
    for name in "qs ks vs rq rk o ol do".split():
        scratch[name] = v(heads, B16)
    scratch.update(
        linv=v(heads, F32), r2=v((T, Q, 128), F32), psi=v((M, 128), B16), phi=v((M, 128), B16), sidr=v((8, M), F32),
        gk=v((T, M, half), B16), duk=v((T, M, half), B16), facc=v(acc, F32), dacc=v(acc, F32),
        send=v((NCH, T, Q, CHUNK), B16), recv=v((2, NCH, T, Q, CHUNK), B16),
        xt=v((D, M), B16), xt2=v((D, M), B16), dqkv=v((M, 3 * hq), B16),
        zb=v((T - 1, 2 * R, C), B16), fbuf=v((R, C), F32),
    )
    for k in range(NB):
        scratch[f"rb{k}"] = v((SLOTS, 2, TH) + (2,) * (NB - 1 - k) + (2 * R, half), B16)
    if dm.inside:
        outs.update(dmodf=s((T, 8, 8 * R), F32), cond=s((8, D), F32), dsil=s((8, D), F32), pk=s((2, 8, W), F32))
        scratch.update({name: v(shape, F32) for name, shape in totals.items()})
        scratch.update(
            mods=v((8, D), F32), hp=v((T, 8, hq), F32), hb=v((T, 8, fu), F32),
            macc=v((NB + 2, 16, D), F32), mrec=v((NB + 1, 16, D), F32), sm=v((T, 8, D), F32),
            m2s=v((T, 8, 8 * R), F32), m2r=v((T - 1, 8, 8 * R), F32), m3c=v((2, NC, 8, 8 * R), F32),
            b1s=v((NC, 8, 8 * R), F32), b1r=v((NC, 8, 8 * R), F32),
            bacc=v((NB + 2, 8, D), F32), brec=v((NB + 1, 8, D), F32),
            pks=v((T, 8, W), F32), pkr=v((T - 1, 8, W), F32), pka=v((NB + 1, 8, W), F32), pkb=v((max(NB, 1), 8, W), F32),
        )
    else:
        outs.update({name: s(shape, F32) for name, shape in totals.items()})
    small = 4 * NB + 6 * T + 2 * NC + 8
    reg = pltpu.SemaphoreType.REGULAR
    scratch.update(
        c_s=dma((NP,)), c_r=dma((NP,)), c_l=dma((NP,)), z_s=dma((NP, T - 1)), z_r=dma((NP, T - 1)),
        p_s=dma((NP, NB, 2)), p_r=dma((NP, NB, 2)), x_s=dma((2, 2)), x_r=dma((2, T)), x_l=dma((2,)), x_f=dma((2, 2)),
        e_s=dma((4, NCH)), e_r=dma((4, NCH)), rs_s=dma((NP, NB, 2)), rs_r=dma((NP, NB, 2)), free=reg((NB, 2)),
        rz_s=dma((NP, T - 1)), rz_r=dma((NP, T - 1)), f_s=dma((NP,)), f_r=dma((NP,)),
        o_s=dma((2, T)), o_r=dma((2, 2)), o_l=dma((2,)), s_s=dma((small,)), s_r=dma((small,)),
    )
    names = tuple(ins) + tuple(outs) + tuple(scratch)
    got = pl.pallas_call(
        functools.partial(block_kernel, dm, names),
        out_shape=tuple(outs.values()),
        in_specs=[any_ if name in ("ws", "xb", "dyb") else vm for name in ins],
        out_specs=tuple(any_ if name in ("outd", "gind") else vm for name in outs),
        scratch_shapes=list(scratch.values()),
        compiler_params=pltpu.CompilerParams(
            collective_id=0, has_side_effects=True, vmem_limit_bytes=66 * 1024 * 1024
        ),
        cost_estimate=pl.CostEstimate(flops=30 * 10**9, bytes_accessed=10**7, transcendentals=10**7),
    )(*ins.values())
    return dict(zip(outs, got))


def local(
    dp, tensor,
    block_input, cotangent, class_ids, scale_ids, class_table, w_ada, b_ada, query_key_value_weight,
    qv_bias, q_gain, output_projection, up_weight, hidden_bias, down_weight, projection_bias,
):
    seqs, quarter, width = block_input.shape
    length = scale_ids.shape[1]
    assert seqs == 2 and tensor == 4
    rows = -(-quarter // 16) * 16
    head = q_gain.shape[1] * dp
    hidden = up_weight.shape[1] * tensor
    dm = Dims(dp, tensor, rows, width, head, hidden)
    T, R, hq, fu, NC, M = dm.T, dm.R, dm.hq, dm.fu, dm.NC, dm.M
    total = class_ids.shape[0]
    di, zi = lax.axis_index("dp"), lax.axis_index("tensor")
    core = di % 2

    pad_rows = ((0, 0), (0, 0), (0, rows - quarter))
    sid = jnp.pad(scale_ids.astype(F32).reshape(2, T, quarter), pad_rows, constant_values=127.0).reshape(2, M)
    sid = jnp.pad(sid, ((0, 6), (0, 0)))
    my_rows = class_table.shape[0]
    my_ids = di * my_rows + jnp.arange(my_rows, dtype=jnp.int32)

    if dm.inside:
        place = jnp.arange(dp, dtype=jnp.int32) == di

        def spread(w):
            return jnp.where(place[:, None], w[..., None, :], 0).reshape(w.shape[:-2] + (-1,)).astype(F32)

        def pad_lanes(w):
            return jnp.pad(w, ((0, 0), (0, width - w.shape[1])))

        hot = (class_ids[:, None] == my_ids[None, :]).astype(B16)
        cond = jnp.dot(hot, class_table, preferred_element_type=F32).reshape(NC, -1)
        tiny = [spread(hidden_bias)[None], spread(qv_bias), spread(q_gain)[None]]
        tiny = jnp.concatenate([pad_lanes(w) for w in tiny], axis=0)
        m1 = jnp.concatenate([jnp.pad(cond, ((0, 8 - NC), (0, 0))), jnp.pad(tiny, ((0, 4), (0, 0)))], axis=0)
        badd = jnp.concatenate([b_ada, projection_bias], axis=0).astype(F32).reshape(1, -1)
        extra = {"m1": m1, "wada": jnp.moveaxis(w_ada, 1, 0), "badd": badd}
    else:
        hot = (class_ids[:, None] == my_ids[None, :]).astype(B16)
        cond = lax.psum(jnp.dot(hot, class_table, preferred_element_type=F32), "dp")
        silu, silu_back = jax.vjp(jax.nn.silu, cond)
        silu_low = silu.astype(B16)
        parts = jnp.einsum("sc,cjd->sjd", silu_low, w_ada, preferred_element_type=F32)
        parts = parts.reshape((NC, T) + parts.shape[1:])
        mine = lax.psum_scatter(parts, "tensor", scatter_dimension=1, tiled=True)[:, 0] + b_ada.astype(F32)
        spread = lax.all_to_all(jnp.repeat(mine, 2, axis=0), "dp", 0, 0, tiled=True)
        modulation = jnp.moveaxis(spread, 0, 1).reshape(6, width)

        pieces = [qv_bias, q_gain, hidden_bias, projection_bias]
        flat = jnp.concatenate([p.reshape(-1) for p in pieces])
        everyone = lax.all_gather(lax.all_gather(flat, "tensor"), "dp")
        cut, at = [], 0
        for p in pieces:
            cut.append(everyone[:, :, at : at + p.size].reshape((dp, T) + p.shape).astype(F32))
            at += p.size
        qv_all = cut[0].transpose(2, 1, 3, 0, 4).reshape(2, T, 2, hq)[:, :, core]
        gain_all = cut[1].transpose(1, 2, 0, 3).reshape(T, 2, hq)[:, core]
        hidden_all = cut[2].transpose(1, 2, 0, 3).reshape(T, 2, fu)[:, core]
        out_bias = cut[3][:, 0].transpose(1, 0, 2).reshape(2, width)
        mods = jnp.concatenate([modulation, out_bias], axis=0)
        hp = jnp.stack([qv_all[0], qv_all[1], gain_all, 1.0 / gain_all], axis=1)
        hp = jnp.concatenate([hp, jnp.zeros_like(hp)], axis=1)
        hb = jnp.broadcast_to(hidden_all[:, None], (T, 8, fu))

        extra = {"mods": mods, "hp": hp, "hb": hb}

    def halves(w):
        return jnp.moveaxis(w.reshape(w.shape[:-1] + (2, w.shape[-1] // 2)), -2, 0)

    qkv_half = halves(query_key_value_weight)
    ws = jnp.concatenate(
        [qkv_half[:, 0], qkv_half[:, 1], qkv_half[:, 2], halves(output_projection.T), halves(up_weight), halves(down_weight.T)],
        axis=-1,
    )
    pad = ((0, 0), (0, rows - quarter), (0, 0))
    xb = jnp.pad(block_input.astype(B16), pad)
    dyb = jnp.pad(cotangent.astype(B16), pad)

    got = block_call(dm, ws, xb, dyb, sid, extra)
    fin, outd, gind = got["fin"], got["outd"], got["gind"]

    block_output = block_input + outd[:, :quarter].astype(F32)
    input_grad = cotangent + gind[:, :quarter].astype(F32)

    def joined(lo, n):
        return jnp.moveaxis(fin[:, :, lo : lo + n], 0, 1).reshape(R, 2 * n)

    w_qkv_grad = jnp.stack([joined(k * hq, hq) for k in range(3)])
    w_proj_grad = joined(3 * hq, hq).T
    w_fc1_grad = joined(dm.up, fu)
    w_fc2_grad = joined(dm.down, fu).T

    if dm.inside:
        cond = got["cond"][:NC].reshape(total, -1)
        silu, silu_back = jax.vjp(jax.nn.silu, cond)
        dmod = jnp.swapaxes(got["dmodf"][:, :NC], 0, 1).reshape(total, 8, R)[:, :6].astype(B16)
        b_ada_grad = jnp.sum(dmod.astype(F32), axis=0)
        w_ada_grad = jnp.einsum("sc,sjd->cjd", silu.astype(B16), dmod, preferred_element_type=F32)
        (d_cond,) = silu_back(got["dsil"][:NC].reshape(total, -1))
        pk = got["pk"]

        def own(w, n):
            return lax.dynamic_slice_in_dim(w, di * n, n, w.ndim - 1)

        heads = own(jnp.swapaxes(pk[:, :3, :hq], 0, 1).reshape(3, -1, head), head // dp)
        qv_bias_grad, q_gain_grad = heads[:2], heads[2]
        b_fc1_grad = own(pk[:, 0, hq : hq + fu].reshape(hidden_bias.shape[0], -1), hidden_bias.shape[1])
        b_out_grad = own(pk[0, 6:8, hq + fu :], R)
    else:
        sums, hsum, fsum = got["sums"], got["hsum"], got["fsum"]
        dmod = sums[:6].reshape(6, dp, R).astype(B16)
        dmod = lax.all_to_all(jnp.moveaxis(dmod, 1, 0), "dp", 0, 0, tiled=True)
        dmod = lax.all_gather(dmod[::2], "tensor", axis=1)
        dmod = dmod.reshape((total, 6, R))
        b_ada_grad = jnp.sum(dmod.astype(F32), axis=0)
        w_ada_grad = jnp.einsum("sc,sjd->cjd", silu_low, dmod, preferred_element_type=F32)
        d_silu = lax.psum(jnp.einsum("sjd,cjd->sc", dmod, w_ada, preferred_element_type=F32), "dp")
        (d_cond,) = silu_back(d_silu)

        vec = jnp.concatenate([hsum[:, :3].reshape(-1), fsum[:, 0].reshape(-1), sums[6:].reshape(-1) * 0.5])
        nh, nf = T * 3 * hq, T * fu
        place_ = jnp.arange(2, dtype=jnp.int32) == core
        by_core = jnp.where(place_[:, None], vec[None, : nh + nf], 0.0).reshape(-1)
        vec = lax.psum(jnp.concatenate([by_core, vec[nh + nf :]]), ("dp", "tensor"))
        by_core = vec[: 2 * (nh + nf)].reshape(2, nh + nf)
        heads = by_core[:, :nh].reshape(2, T, 3, hq)
        heads = lax.dynamic_index_in_dim(heads, zi, 1, keepdims=False)
        heads = jnp.moveaxis(heads, 0, 1).reshape(3, -1, head)
        step = head // dp
        heads = lax.dynamic_slice_in_dim(heads, di * step, step, 2)
        qv_bias_grad, q_gain_grad = heads[:2], heads[2]
        fc1 = lax.dynamic_index_in_dim(by_core[:, nh:].reshape(2, T, fu), zi, 1, keepdims=False)
        fc1 = fc1.reshape(-1, hidden_bias.shape[1] * dp)
        step = hidden_bias.shape[1]
        b_fc1_grad = lax.dynamic_slice_in_dim(fc1, di * step, step, 1)
        b_out_grad = lax.dynamic_slice_in_dim(vec[2 * (nh + nf) :].reshape(2, width), di * R, R, 1)

    table_grad = jnp.dot(hot.astype(F32).T, d_cond, precision=lax.Precision.HIGHEST, preferred_element_type=F32)

    return (
        block_output, input_grad, table_grad, w_ada_grad, b_ada_grad, w_qkv_grad, qv_bias_grad, q_gain_grad,
        w_proj_grad, w_fc1_grad, b_fc1_grad, w_fc2_grad, b_out_grad,
    )


def solution(mesh):
    dp, tensor = mesh.shape["dp"], mesh.shape["tensor"]
    return jax.shard_map(
        functools.partial(local, dp, tensor),
        mesh=mesh,
        in_specs=(
            P("dp", "tensor", None),
            P("dp", "tensor", None),
            P(),
            P("dp", None),
            P("dp", "tensor"),
            P("tensor", None, "dp"),
            P(None, "dp"),
            P(None, "dp", "tensor"),
            P(None, "tensor", "dp"),
            P("tensor", "dp"),
            P("tensor", "dp"),
            P("dp", "tensor"),
            P("tensor", "dp"),
            P("tensor", "dp"),
            P(None, "dp"),
        ),
        out_specs=(
            P("dp", "tensor", None),
            P("dp", "tensor", None),
            P("dp", "tensor"),
            P("tensor", None, "dp"),
            P(None, "dp"),
            P(None, "dp", "tensor"),
            P(None, "tensor", "dp"),
            P("tensor", "dp"),
            P("tensor", "dp"),
            P("dp", "tensor"),
            P("tensor", "dp"),
            P("tensor", "dp"),
            P(None, "dp"),
        ),
        check_vma=False,
    )
```

time: 512 us -> 366 us (0.71)
  blocking collectives: 134 us -> 0 us
  starting transfers between devices: 6.97 us -> 0 us
    psum x3 -> x0, blocking collectives: 84.5 us -> none  [the longest x1 37.2 us: local(): vec = lax.psum(jnp.concatenate([by_core, vec[nh + nf:]]), ('dp', 'tensor'))]
    unnamed x2 -> x0, blocking collectives: 26.4 us -> none
    all_gather x2 -> x0, blocking collectives: 23.2 us -> none  [the longest x1 13.7 us: local(): dmod = lax.all_gather(dmod[::2], 'tensor', axis=1)]
    all_to_all x2 -> x0, starting transfers between devices: 6.89 us -> none  [the longest x1 3.55 us: local(): dmod = lax.all_to_all(jnp.moveaxis(dmod, 1, 0), 'dp', 0, 0, tiled=True)]
    unnamed x59 -> x29, local copies, waits for them, and re-layouts: 12.1 us -> 12.7 us
  transfers between devices with their start and end apart: 3 -> 0, of which waited for: 0 -> 0; matrix products, arithmetic and copies ran while one was open for 6% -> 0% of each run, Pallas kernels for 0% -> 0%
where the time goes in v2:
time: 366 us; the launch traced here: 361 us
  Pallas kernels  317 us (87%)
  local copies, waits for them, and re-layouts  31.5 us (9%)
  other arithmetic  7.45 us (2%)
  matrix products  3.89 us (1%)
    pallas_call x1, Pallas kernels, block_call(): pl.pallas_call(functools.partial(block_kernel, dm, names), out_shape=tupl...  317 us
    unnamed x29, local copies, waits for them, and re-layouts  12.7 us

profile of v2, /device:TPU:24, one launch (start us, length us, event | category | flops | bytes accessed | tf_op | source)
XLA Modules:
  0.0 360.6 jit_solution(13277369453983268219)
XLA Ops:
  0.7 1.4 maximum_convert_fusion
  2.1 0.8 copy.69
  2.9 0.1 broadcast_in_dim.78
  3.0 0.7 convert_element_type.80
  3.7 0.1 reshape.152
  3.8 0.1 reshape.153
  3.9 0.8 broadcast_select_fusion.1
  4.6 0.1 convert_element_type.82
  4.7 1.0 fusion.16
  5.8 0.8 broadcast_in_dim.80
  6.6 0.1 broadcast_in_dim.81
  6.7 0.6 pad.38.refs_3_
  7.3 0.1 broadcast_select_fusion
  7.4 0.1 convert_element_type.81
  7.6 0.6 select_maximum_fusion.refs_4_
  8.2 0.9 copy.63
  9.1 1.1 copy.61
  10.2 0.2 copy.62
  10.4 0.2 copy.64
  10.6 0.1 copy.65
  10.8 0.1 copy.66
  10.9 0.5 convert_element_type.78
  11.4 0.2 copy.67
  11.6 0.9 pad.35.refs_1_
  12.5 0.5 copy-done
  13.0 0.5 convert_element_type.79
  13.5 0.2 copy.68
  13.7 0.9 pad.36.refs_2_
  14.6 0.6 fusion.2
  15.3 0.6 fusion.1
  15.9 0.6 fusion
  16.5 0.6 bitcast_dynamic-update-slice_fusion.2
  17.2 0.7 bitcast_dynamic-update-slice_fusion.1
  17.9 0.7 bitcast_dynamic-update-slice_fusion.refs_0_
  18.6 316.6 %shard_map.246 = (f32[2,128,1536]{2,1,0:T(8,128)}, bf16[2,176,1024]{2,1,0:T(8,128)(2,1)}, bf16[2,176,1024]{2,1,0:T(8,128)(2,1)}, f32[4,8,1024]{2,1,0:T(8,128)}, ...) custom-call(bf16[2,128,1536]{2,1,0:T(8,128)(2,1)} %bitcast_dynamic-update-slice_fusion.refs_0_, ...), custom_call_target="tpu_custom_call" | custom-call | flops 30000001024 | bytes 10000000 | tf_op jit(solution)/shard_map/pallas_call | solution.py:902
  335.2 0.9 slice_reduce_fusion
  336.1 0.1 reshape_squeeze.3
  336.2 0.1 constant_dynamic-slice_fusion.1
  336.3 0.7 copy.87
  336.9 0.7 slice_bitcast_fusion.9
  337.6 0.8 slice.81
  338.4 0.6 dynamic-slice_bitcast_fusion.1
  338.9 0.1 reshape.158
  339.0 0.6 dynamic-slice_bitcast_fusion
  339.7 0.7 constant_dynamic-slice_fusion
  340.4 0.8 slice.67
  341.1 0.8 slice.68
  341.9 0.9 fusion.3
  342.9 0.6 convert_reduce_fusion
  343.5 1.7 fusion.8
  345.1 1.1 slice_bitcast_fusion.2
  346.3 0.9 slice_bitcast_fusion
  347.2 1.0 copy.81
  348.1 0.8 copy.78
  348.9 0.1 copy.76
  349.0 0.1 copy.75
  349.1 0.1 copy.74
  349.2 0.9 copy.84
  350.2 1.4 copy.79
  351.6 1.0 copy.85
  352.6 1.2 fusion.4
  353.7 2.3 copy_add_fusion
  356.0 2.2 copy.83
  358.2 2.2 copy.82
  (29 shorter events, 0.3 us)
Async XLA Ops:
  0.6 10.1 %copy-start.6 = (bf16[1024,128]{1,0:T(8,128)(2,1)S(1)}, bf16[1024,128]{1,0:T(8,128)(2,1)}, u32[]{:S(2)}) copy-start(bf16[1024,128]{1,0:T(8,128)(2,1)} %param.28) | copy-start | bytes 786436
  0.7 9.8 %copy-start.5 = (bf16[128,1024]{1,0:T(8,128)(2,1)S(1)}, bf16[128,1024]{1,0:T(8,128)(2,1)}, u32[]{:S(2)}) copy-start(bf16[128,1024]{1,0:T(8,128)(2,1)} %param.26) | copy-start | bytes 786436
  0.7 6.0 %copy-start.7 = (s32[128]{0:T(128)}, s32[128]{0:T(128)S(1)}, u32[]{:S(2)}) copy-start(s32[128]{0:T(128)S(1)} %iota_add_fusion) | copy-start | bytes 1540
  5.8 5.1 %copy-start.2 = (f32[2,170,1024]{2,0,1:T(2,128)S(1)}, f32[2,170,1024]{2,0,1:T(2,128)}, u32[]{:S(2)}) copy-start(f32[2,170,1024]{2,0,1:T(2,128)} %param.15) | copy-start | bytes 4177924
  11.4 1.6 copy-start
  335.2 11.1 %copy-start.4 = (f32[2,128,1536]{2,1,0:T(8,128)S(1)}, f32[2,128,1536]{2,1,0:T(8,128)}, u32[]{:S(2)}) copy-start(f32[2,128,1536]{2,1,0:T(8,128)} %get-tuple-element.25) | copy-start | bytes 4718596
  350.2 3.6 copy-start.1
  350.2 3.6 copy-start.3

commit v3 on v2

--- a/solution.py
+++ b/solution.py
@@ -9,7 +9,11 @@
 
 MESH = pl.DeviceIdType.MESH
 F32, B16 = jnp.float32, jnp.bfloat16
+FINS = 3
 SLOTS = 3
+PUMPS = (0, 0, 0, 1, 2, 3, 3, 2, 2, 2, 2, 2, 2, 2)
+BEGIN = ((), ((2, 0),), ((1, 0),), ((2, 1), (1, 1), (0, 0), (0, 1)))
+LEAN = 1.5
 CHUNK = 256
 EPS = 1e-06
 FAR = 256.0
@@ -85,6 +89,9 @@
     mybit = [lax.rem(chip // (1 << b), 2) for b in range(NB)]
     partner = (dpi + 1 - 2 * core, me_z)
 
+    def tag_z(dev):
+        return dev
+
     def z_dev(off):
         return (dpi, lax.rem(me_z + off, T))
 
@@ -119,17 +126,47 @@
     def core_rows(c):
         return pl.ds(pl.multiple_of(c * R, R), R)
 
+    def lanes_of(start, n):
+        return pl.ds(pl.multiple_of(start, 128), n)
+
+    def own_weight(pc, c):
+        if pc < 3:
+            return m.wqkv.at[pc, :, lanes_of(c * hq, hq)]
+        if pc == 3:
+            return m.gk.at[0, 128 : 128 + R, lanes_of(c * hq, hq)]
+        k = (pc - 4) // 2
+        if pc % 2 == 0:
+            return m.wup.at[:, lanes_of(c * fu + k * half, half)]
+        return m.gk.at[2 * c + k, 0:R, :]
+
+    def transpose_own():
+        m.gk[0, 128 : 128 + R, :] = m.wproj[...].T
+        for i in range(4):
+            m.gk[i, 0:R, :] = m.wdown[i * half : (i + 1) * half, :].T
+
     def core_copy(pc):
         dst = wall.at[(me_z,) + mine + (core_rows(core), cols(pc))]
-        return rdma(m.ws.at[1 - core, :, cols(pc)], dst, m.c_s.at[pc], m.c_r.at[pc], partner)
+        return rdma(own_weight(pc, 1 - core), dst, m.c_s.at[pc], m.c_r.at[pc], partner)
 
     def core_local(pc):
         dst = wall.at[(me_z,) + mine + (core_rows(core), cols(pc))]
-        return pltpu.make_async_copy(m.ws.at[core, :, cols(pc)], dst, m.c_l.at[pc])
+        return pltpu.make_async_copy(own_weight(pc, core), dst, m.c_l.at[pc])
 
     def z_copy(pc, off):
         part = wall.at[(me_z,) + mine + (every, cols(pc))]
         return rdma(part, part, m.z_s.at[pc, off - 1], m.z_r.at[pc, off - 1], z_dev(off))
+
+    inner = jnp.logical_and(me_z > 0, me_z < T - 1)
+    line_sends = ((2, me_z >= 0), (1, me_z < T - 1), (3, me_z > 0))
+
+    def z_landed(pc, off):
+        part = wall.at[(lax.rem(me_z - off + T, T),) + mine + (every, cols(pc))]
+        rdma(part, part, m.z_s.at[pc, off - 1], m.z_r.at[pc, off - 1], z_dev(off)).wait_recv()
+
+    def z_forward(pc):
+        part = wall.at[(lax.rem(me_z + 2, T),) + mine + (every, cols(pc))]
+        up = lax.rem(me_z + 1, 2)
+        return rdma(part, part, m.z_f.at[pc], m.z_r.at[pc, 2 * up], tag_z((dpi, me_z + 2 * up - 1)))
 
     order = [list(range(NB)), list(reversed(range(NB)))]
 
@@ -151,37 +188,59 @@
             core_local(pc).wait()
             other = wall.at[(me_z,) + mine + (core_rows(1 - core), cols(pc))]
             rdma(other, other, m.c_s.at[pc], m.c_r.at[pc], partner).wait_recv()
-            for off in range(1, T):
-                z_copy(pc, off).start()
+            for off, allowed in line_sends:
+                @pl.when(allowed)
+                def _():
+                    z_copy(pc, off).start()
+            return
+        if s == -1:
+            @pl.when(inner)
+            def _():
+                z_landed(pc, 2)
+                z_forward(pc).start()
             return
         if s == 1:
-            for off in range(1, T):
-                part = wall.at[(lax.rem(me_z - off + T, T),) + mine + (every, cols(pc))]
-                rdma(part, part, m.z_s.at[pc, off - 1], m.z_r.at[pc, off - 1], z_dev(off)).wait_recv()
+            z_landed(pc, 1)
+            z_landed(pc, 3)
+
+            @pl.when(jnp.logical_not(inner))
+            def _():
+                z_landed(pc, 2)
         for h in range(2):
             if s > 1:
                 p_copy(pc, s - 2, h, True).wait_recv()
             if s <= NB:
                 p_copy(pc, s - 1, h, False).start()
 
-    ticks = [0]
-
-    def gather_tick():
-        t = ticks[0]
-        ticks[0] += 1
-        for s in range(NB, -1, -1):
-            gather_stage(t - s, s)
-        gather_stage(t - NB - 1, NB + 1)
+    starts = [(pc - 2.2, pc, 0) for pc in range(NP)] + [(pc - 1.1, pc, -1) for pc in range(NP)]
+    starts += [(pc + 1.1 * (s - 1), pc, s) for pc in range(NP) for s in range(1, NB + 1)]
+    if NB == 2:
+        starts[starts.index((4 + 1.1, 4, 2))] = (4.95, 4, 2)
+    starts.sort()
+
+    here = [0]
+
+    def gather_to(key):
+        while starts and starts[0][0] <= key:
+            gather_stage(*starts.pop(0)[1:])
 
     def gather_until(pc):
-        while ticks[0] <= pc + NB + 1:
-            gather_tick()
+        gather_to(pc + 1.1 * NB)
+        while here[0] <= pc:
+            gather_stage(here[0], NB + 1)
+            here[0] += 1
 
     def gather_sent(which):
         for pc in which:
-            core_copy(pc).wait_send()
-            for off in range(1, T):
-                z_copy(pc, off).wait_send()
+            for off, allowed in line_sends:
+                @pl.when(allowed)
+                def _():
+                    z_copy(pc, off).wait_send()
+
+            @pl.when(inner)
+            def _():
+                z_forward(pc).wait_send()
+
             for step in range(NB):
                 for h in range(2):
                     p_copy(pc, step, h, False).wait_send()
@@ -253,11 +312,14 @@
             def _():
                 rdma(dst.at[i], dst.at[i], m.o_s.at[which, 0], m.o_r.at[which, i], (dpi, 2 * core + i)).wait_recv()
 
+    def sender(k):
+        return m.duk if k == 2 and m.duk.shape == m.send.shape else m.send
+
     def x_copy(k, n):
-        return rdma(m.send.at[n], m.recv.at[k % 2, n], m.e_s.at[k, n], m.e_r.at[k, n], partner)
+        return rdma(sender(k).at[n], m.recv.at[k % 2, n], m.e_s.at[k, n], m.e_r.at[k, n], partner)
 
     def exchange(k, n, value):
-        m.send[n] = value.astype(B16).reshape(T, Q, CHUNK)
+        sender(k)[n] = value.astype(B16)
         x_copy(k, n).start()
 
     def exchange_wait(k):
@@ -269,7 +331,8 @@
             x_copy(k, n).wait_send()
 
     def both(k, t):
-        parts = [m.send[n, t].astype(F32) + m.recv[k % 2, n, t].astype(F32) for n in range(NCH)]
+        rows = pl.ds(pl.multiple_of(t * Q, 16), Q)
+        parts = [sender(k)[n, rows, :].astype(F32) + m.recv[k % 2, n, rows, :].astype(F32) for n in range(NCH)]
         return jnp.concatenate(parts, axis=-1)
 
     def wz(z, lo, n):
@@ -355,9 +418,79 @@
         part = wall.at[(lax.rem(me_z + off, T),) + mine + (every, cols(pc))]
         return rdma(part, m.zb.at[off - 1, :, cols(pc)], m.rz_s.at[j, off - 1], m.rz_r.at[j, off - 1], z_dev(off))
 
+    def rz_special(j):
+        pc = dm.sums_order[j]
+        far = T - 1 - me_z
+        part = wall.at[(far,) + mine + (every, cols(pc))]
+        return rdma(part, m.zx.at[:, cols(pc)], m.rx.at[j, 0], m.rx.at[j, 1], tag_z((dpi, jnp.where(me_z == 0, 1, T - 2))))
+
+    ends_here = jnp.logical_not(inner)
+
+    def rz_begin(j):
+        @pl.when(ends_here)
+        def _():
+            rz_special(j).start()
+            rz_copy(j, 2).start()
+
+        for off, allowed in line_sends[1:]:
+            @pl.when(allowed)
+            def _():
+                rz_copy(j, off).start()
+
+    def rz_middle(j):
+        pc = dm.sums_order[j]
+
+        @pl.when(inner)
+        def _():
+            got = m.zx.at[:, cols(pc)]
+            rdma(got, got, m.rx.at[j, 0], m.rx.at[j, 1], tag_z((dpi, me_z))).wait_recv()
+            where = (lax.rem(me_z + 2, T),) + mine + (every, cols(pc))
+            wall[where] = (wall[where].astype(F32) + m.zx[:, cols(pc)].astype(F32)).astype(B16)
+            rz_copy(j, 2).start()
+
+    def rz_wait(j):
+        rz_copy(j, 2).wait_recv()
+        for off, came in ((1, me_z > 0), (3, me_z < T - 1)):
+            @pl.when(came)
+            def _():
+                rz_copy(j, off).wait_recv()
+
+    def rz_sent(j):
+        rz_copy(j, 2).wait_send()
+        for off, allowed in line_sends[1:]:
+            @pl.when(allowed)
+            def _():
+                rz_copy(j, off).wait_send()
+
+        @pl.when(ends_here)
+        def _():
+            rz_special(j).wait_send()
+
+    def final(pc, c):
+        if pc < 3:
+            return m.g_qkv, (pc, every, lanes_of(c * hq, hq))
+        if pc == 3:
+            return m.g_proj, (pl.ds(pl.multiple_of(c * hq, hq), hq), every)
+        at = c * fu + (pc - 4) // 2 * half
+        if pc % 2 == 0:
+            return m.g_up, (every, lanes_of(at, half))
+        return m.g_down, (pl.ds(pl.multiple_of(at, half), half), every)
+
+    def turned(pc):
+        return pc in (3, 5, 7)
+
+    def fin_from(j):
+        pc = dm.sums_order[j]
+        width = dm.pieces[pc][1]
+        if turned(pc):
+            return m.fturn, (j // 2 % 2, pl.ds(0, width))
+        return m.fbuf, (j % FINS, every, pl.ds(0, width))
+
     def fin_copy(j):
         pc = dm.sums_order[j]
-        return rdma(m.fbuf.at[:, cols(pc)], m.fin.at[core, :, cols(pc)], m.f_s.at[j], m.f_r.at[j], partner)
+        ref, at = fin_from(j)
+        out, place_ = final(pc, core)
+        return rdma(ref.at[at], out.at[place_], m.f_s.at[j], m.f_r.at[j], partner)
 
     def rs_event(j, s):
         pc = dm.sums_order[j]
@@ -367,11 +500,12 @@
                 if s < NB:
                     rs_start(j, s, h)
             if s == NB:
-                for off in range(1, T):
-                    rz_copy(j, off).start()
+                rz_begin(j)
             return
-        for off in range(1, T):
-            rz_copy(j, off).wait_recv()
+        if s == NB + 1:
+            rz_middle(j)
+            return
+        rz_wait(j)
 
         def total(rows):
             acc = wall[(me_z,) + mine + (rows, cols(pc))].astype(F32)
@@ -379,17 +513,27 @@
                 acc = acc + m.zb[off - 1, rows, cols(pc)].astype(F32)
             return acc
 
-        m.fbuf[:, cols(pc)] = total(core_rows(1 - core))
+        if j >= FINS:
+            fin_copy(j - FINS).wait_send()
+        ref, at = fin_from(j)
+        out, place_ = final(pc, core)
+        away, kept = total(core_rows(1 - core)), total(core_rows(core))
+        ref[at] = away.T if turned(pc) else away
         fin_copy(j).start()
-        m.fin[core, :, cols(pc)] = total(core_rows(core))
-
-    events = sorted(((j, s) for j in range(NP) for s in range(1, NB + 2)), key=lambda e: (e[0] + 1.5 * e[1], e[0]))
+        out[place_] = kept.T if turned(pc) else kept
+
+    events = sorted(((j, s) for j in range(NP) for s in range(1, NB + 3)), key=lambda e: (e[0] + LEAN * e[1], e[0]))
     begun = set()
 
     def pump(count):
         while count and events and (events[0][0], 1) in begun:
             rs_event(*events.pop(0))
             count -= 1
+
+    stops = list(PUMPS)
+
+    def stop():
+        pump(stops.pop(0) if stops else 0)
 
     def rs_begin(pc, h):
         j = place_of[pc]
@@ -403,20 +547,23 @@
             for step in range(NB):
                 for h in range(2):
                     rs_copy(j, step, h).wait_send()
-            for off in range(1, T):
-                rz_copy(j, off).wait_send()
-            fin_copy(j).wait()
+            rz_sent(j)
+            fin_copy(j).wait_recv()
+            if j + FINS >= NP:
+                fin_copy(j).wait_send()
 
     def small(src, dst, k, dev):
         return rdma(src, dst, m.s_s.at[k], m.s_r.at[k], dev)
 
-    def sum_step(acc, got, i, base, sign):
+    def sum_step(acc, got, i, base, sign, rows=None):
         dev = partner if i < sign else bit_dev(i - sign)
-        return small(acc.at[i], got.at[i], base + i, dev)
-
-    def sum_finish(acc, got, i, base, sign):
-        sum_step(acc, got, i, base, sign).wait_recv()
-        acc[i + 1] = acc[i] + got[i]
+        n = acc.shape[1] if rows is None else rows
+        return small(acc.at[i, pl.ds(0, n)], got.at[i, pl.ds(0, n)], base + i, dev)
+
+    def sum_finish(acc, got, i, base, sign, rows=None):
+        sum_step(acc, got, i, base, sign, rows).wait_recv()
+        n = acc.shape[1] if rows is None else rows
+        acc[i + 1, 0:n] = acc[i, 0:n] + got[i, 0:n]
 
     S_SID = 0
     S_M1 = 1
@@ -436,13 +583,19 @@
     if dm.inside:
         m.macc[0] = m.m1[...]
         sum_step(m.macc, m.mrec, 0, S_M1, 1).start()
-    core_copy(0).start()
-    core_local(0).start()
-    tok_start(0, m.xb, xs)
-    for pc in range(1, NP):
+    for pc in (0, 1, 2, 4, 6):
         core_copy(pc).start()
         core_local(pc).start()
-    gather_tick()
+    gather_to(-1.0)
+    transpose_own()
+    for pc in (3, 5, 7):
+        core_copy(pc).start()
+        core_local(pc).start()
+    for z, slot in ((0, 0), (T - 1, T - 2)):
+        @pl.when(me_z == z)
+        def _():
+            m.zb[slot] = jnp.zeros(m.zb.shape[1:], B16)
+
     sums[...] = jnp.zeros_like(sums)
     hsum[...] = jnp.zeros_like(hsum)
     fsum[...] = jnp.zeros_like(fsum)
@@ -465,7 +618,8 @@
         for off in range(1, T):
             small(m.m2s.at[lax.rem(me_z + off, T)], m.m2r.at[off - 1], S_M2 + off - 1, z_dev(off)).start()
 
-    gather_tick()
+    gather_to(1.85)
+    tok_start(0, m.xb, xs)
 
     if dm.inside:
         for off in range(1, T):
@@ -474,10 +628,7 @@
         own = m.m3c.at[core, chip]
         for k in range(1, NC):
             small(own, own, S_M3 + k - 1, chip_dev(k)).start()
-        for k in range(1, NC):
-            got = m.m3c.at[core, lax.rem(chip - k + NC, NC)]
-            small(got, got, S_M3 + k - 1, chip_dev(k)).wait_recv()
-        small(m.m3c.at[core], m.m3c.at[core], S_M4, partner).start()
+        gather_to(2.15)
         for off in range(1, T):
             got = m.sm.at[lax.rem(me_z - off + T, T)]
             small(got, got, S_SM + off - 1, z_dev(off)).wait_recv()
@@ -487,6 +638,20 @@
                 hp[z, r : r + 1, :] = m.sm[z, r + 1 : r + 2, head_cols]
             hp[z, 3:4, :] = 1.0 / hp[z, 2:3, :]
             hb[z, 0:1, :] = m.sm[z, 0:1, pl.ds(pl.multiple_of(core * fu, fu), fu)]
+        for k in range(1, NC):
+            got = m.m3c.at[core, lax.rem(chip - k + NC, NC)]
+            small(got, got, S_M3 + k - 1, chip_dev(k)).wait_recv()
+        small(m.m3c.at[core], m.m3c.at[core], S_M4, partner).start()
+
+    got = small(m.sidr, m.sidr, S_SID, partner)
+    got.wait_recv()
+    pick = lax.rem(me_z, 2)
+    ids = jnp.where(owner, m.sid[pl.ds(pick, 1), :], m.sidr[pl.ds(pick, 1), :])
+    lanes = lax.broadcasted_iota(jnp.int32, (128, 1), 0).astype(F32)
+    m.psi[...] = jnp.where(lanes > ids, FAR, 0.0).astype(B16).T
+    m.phi[...] = jnp.where(lanes == ids, -1.0, 0.0).astype(B16).T
+
+    if dm.inside:
         got = m.m3c.at[1 - core]
         small(got, got, S_M4, partner).wait_recv()
         for c in range(2):
@@ -496,13 +661,7 @@
                 for j in range(8):
                     mods[j : j + 1, d * R : (d + 1) * R] = row[:, j * R : (j + 1) * R]
 
-    got = small(m.sidr, m.sidr, S_SID, partner)
-    got.wait_recv()
-    pick = lax.rem(me_z, 2)
-    ids = jnp.where(owner, m.sid[pl.ds(pick, 1), :], m.sidr[pl.ds(pick, 1), :])
-    lanes = lax.broadcasted_iota(jnp.int32, (128, 1), 0).astype(F32)
-    m.psi[...] = jnp.where(lanes > ids, FAR, 0.0).astype(B16).T
-    m.phi[...] = jnp.where(lanes == ids, -1.0, 0.0).astype(B16).T
+    gather_to(4.1)
     tok_wait(0, m.xb, xs)
 
     def ln(rows):
@@ -516,7 +675,10 @@
         return carry
 
     lax.fori_loop(0, T, first_norm, 0)
-    tok_start(1, m.dyb, dys)
+    gather_to(4.96)
+    if dm.inside:
+        for i in range(NB + 1):
+            sum_step(m.macc, m.mrec, i, S_M1, 1).wait_send()
     gather_until(2)
 
     lane = lax.broadcasted_iota(jnp.int32, (1, hq), 1)
@@ -561,25 +723,20 @@
             inverse = inv if inverse is None else jnp.where(halves[k], inv, inverse)
         m.o[z] = mixed.astype(B16)
         m.ol[z] = (mixed - mixed.astype(B16).astype(F32)).astype(B16)
-        m.linv[z] = inverse
+        m.do[z] = inverse.astype(B16)
         return carry
 
-    lax.fori_loop(0, TH, attend, 0)
+    gather_to(5.0)
+    for z in range(T):
+        lax.fori_loop(z, z + 1, attend, 0)
+        if z == 1:
+            gather_to(5.9)
+            tok_start(1, m.dyb, dys)
+
     gather_until(3)
-    lax.fori_loop(TH, T, attend, 0)
-
     o_all = all_z(m.o)
     for n in range(NCH):
         exchange(0, n, dot_nt(o_all, wrows_all(n, 3 * hq, hq)))
-    tok_wait(1, m.dyb, dys)
-
-    def out_grad(t, carry):
-        d = (mod(1) * dys[t].astype(F32)).astype(B16)
-        m.df[t] = d
-        sums[7:8, :] += row_sum(d.astype(F32))
-        return carry
-
-    lax.fori_loop(0, T, out_grad, 0)
     exchange_wait(0)
 
     def second_norm(t, carry):
@@ -592,10 +749,15 @@
         return carry
 
     lax.fori_loop(0, T, second_norm, 0)
+    gather_to(7.05)
     exchange_sent(0)
-    gather_until(4)
     transpose_into(m.xt, h2)
-    transpose_into(m.xt2, m.df)
+
+    def out_grad(t, carry):
+        d = (mod(1) * dys[t].astype(F32)).astype(B16)
+        m.df[t] = d
+        sums[7:8, :] += row_sum(d.astype(F32))
+        return carry
 
     root = 0.7978845608028654
 
@@ -617,7 +779,13 @@
             fsum[z, 0:1, k * half : (k + 1) * half] = row_sum(du.astype(F32))
             return carry
 
+        gather_until(4 + 2 * k)
         lax.fori_loop(0, T, up, 0)
+        if k == 0:
+            gather_to(7.15)
+            tok_wait(1, m.dyb, dys)
+            lax.fori_loop(0, T, out_grad, 0)
+            transpose_into(m.xt2, m.df)
         gather_until(5 + 2 * k)
         lax.fori_loop(0, T, down, 0)
 
@@ -635,20 +803,19 @@
         for pc, body in ((5 + 2 * k, down_grad), (4 + 2 * k, up_grad)):
             for h in range(2):
                 lax.fori_loop(h * TH, (h + 1) * TH, body, 0)
-                if begin:
+                if pc in begin:
                     rs_begin(pc, h)
 
+    for pc in range(NP):
+        core_copy(pc).wait_send()
     hidden(0)
     du_all, g_all = all_z(m.duk), all_z(m.gk)
     for n in range(NCH):
         m.dacc[n] = dot_nt(du_all, wrows_all(n, dm.up, half))
         m.facc[n] = dot_nt(g_all, wrows_all(n, dm.down, half))
     gather_sent((4, 5))
-    grads(0, False)
-    gather_until(6)
-    for pc in (5, 4):
-        for h in range(2):
-            rs_begin(pc, h)
+    gather_to(99.0)
+    grads(0, (5, 4))
     hidden(1)
     du_all, g_all = all_z(m.duk), all_z(m.gk)
     for n in range(NCH):
@@ -656,10 +823,14 @@
     for n in range(NCH):
         m.facc[n] = m.facc[n] + dot_nt(g_all, wrows_all(n, dm.down + half, half))
     gather_sent((0, 1, 2, 3, 6, 7))
-    grads(1, True)
+    grads(1, (7,))
+    stop()
     transpose_into(m.xt, h1)
     tok_sent(1, m.dyb, dys)
     exchange_wait(1)
+    if sender(2) is not m.send:
+        for n in range(NCH):
+            exchange(2, n, m.facc[n])
 
     def ln_back(e, normed, inv):
         return (e - jnp.mean(e, axis=-1, keepdims=True) - normed * jnp.mean(e * normed, axis=-1, keepdims=True)) * inv
@@ -679,38 +850,43 @@
         return carry
 
     lax.fori_loop(0, T, mid_back, 0)
+    pl.semaphore_signal(m.took, inc=1, device_id=partner, device_id_type=MESH)
+    stop()
+    for h in range(2):
+        rs_begin(6, h)
     exchange_sent(1)
-    for n in range(NCH):
-        exchange(2, n, m.facc[n])
+    if sender(2) is m.send:
+        for n in range(NCH):
+            exchange(2, n, m.facc[n])
+
+    def last(t, carry):
+        f = both(2, t) + mod(7)
+        m.n2[t] = (mod(0) * m.ab[t].astype(F32) + mod(1) * f).astype(B16)
+        sums[1:2, :] += row_sum(dys[t].astype(F32) * f)
+        return carry
+
+    exchange_wait(2)
+    lax.fori_loop(0, T, last, 0)
+    exchange_sent(2)
+    back_start(0, m.outd)
 
     w_proj = jnp.concatenate([wz(z, 3 * hq, hq) for z in range(T)], axis=-1)
     do_all = dot(whole(m.df), w_proj).astype(B16)
     for z in range(T):
-        m.do[z] = do_all[:, z * hq : (z + 1) * hq]
+        m.do[z] = (do_all[:, z * hq : (z + 1) * hq].astype(F32) * m.do[z].astype(F32)).astype(B16)
     transpose_into(m.xt2, m.df)
     dw = dot(m.xt2[...], all_z(m.o))
     for z in range(T):
         wstore(z, 3 * hq, hq, dw[:, z * hq : (z + 1) * hq])
     for h in range(2):
         rs_begin(3, h)
-    pump(1)
-    exchange_wait(2)
-
-    def last(t, carry):
-        f = both(2, t) + mod(7)
-        m.n2[t] = (mod(0) * m.ab[t].astype(F32) + mod(1) * f).astype(B16)
-        sums[1:2, :] += row_sum(dys[t].astype(F32) * f)
-        return carry
-
-    lax.fori_loop(0, T, last, 0)
-    exchange_sent(2)
-    back_start(0, m.outd)
+    stop()
 
     ends = jnp.where(lane < 2, -1.0, 0.0).astype(B16)
 
     def attend_back(z, carry):
         q_all, k_all, v_all = m.qs[z], m.ks[z], m.vs[z]
-        dob = (m.do[z].astype(F32) * m.linv[z]).astype(B16)
+        dob = m.do[z]
         prod = dob.astype(F32) * (m.o[z].astype(F32) + m.ol[z].astype(F32))
         v_ends = jnp.concatenate([v_all, jnp.broadcast_to(ends, (M, hq))], axis=1)
         dq = dk = dv = 0.0
@@ -742,6 +918,8 @@
 
     for z in range(T):
         lax.fori_loop(z, z + 1, attend_back, 0)
+        if z == T - 1:
+            pl.semaphore_wait(m.took, 1)
         d_one_z = m.dqkv[...]
         for n in range(NCH):
             part = dot_nt(d_one_z, wrows(z, n, 0, 3 * hq))
@@ -750,18 +928,15 @@
             else:
                 m.facc[n] = part if z == 0 else m.facc[n] + part
         wstore(z, 0, 3 * hq, dot(m.xt[...], d_one_z))
-        if z % TH == TH - 1:
-            for pc in (2, 1, 0):
-                rs_begin(pc, z // TH)
-        else:
-            pump(2)
+        for pc, h in BEGIN[z]:
+            rs_begin(pc, h)
+        stop()
 
     if dm.inside:
         for z in range(T):
             m.pks[z] = jnp.concatenate([hsum[z], fsum[z], sums[...]], axis=-1)
         for off in range(1, T):
             small(m.pks.at[lax.rem(me_z + off, T)], m.pkr.at[off - 1], S_PZ + off - 1, z_dev(off)).start()
-    pump(2)
     exchange_wait(3)
 
     def first_back(t, carry):
@@ -772,9 +947,13 @@
         m.ab[t] = (h2[t].astype(F32) + ln_back(dh * (1.0 + mod(2)), normed, inv)).astype(B16)
         return carry
 
-    lax.fori_loop(0, T, first_back, 0)
+    for t in range(T):
+        lax.fori_loop(t, t + 1, first_back, 0)
+        if t % 2:
+            stop()
     exchange_sent(3)
-    back_start(1, m.gind)
+    if not dm.inside:
+        back_start(1, m.gind)
 
     if dm.inside:
         for p in range(NC):
@@ -783,11 +962,8 @@
             m.b1s[p] = jnp.broadcast_to(jnp.concatenate(rows, axis=-1), (8, 8 * R))
         for k in range(1, NC):
             small(m.b1s.at[lax.rem(chip + k, NC)], m.b1r.at[k - 1], S_B1 + k - 1, chip_dev(k)).start()
-        for off in range(1, T):
-            small(m.pks.at[0], m.pkr.at[off - 1], S_PZ + off - 1, z_dev(off)).wait_recv()
-        m.pka[0] = m.pks[me_z] + sum(m.pkr[k] for k in range(T - 1))
-        if NB:
-            sum_step(m.pka, m.pkb, 0, S_PB, 0).start()
+        stop()
+        stop()
         for k in range(1, NC):
             small(m.b1s.at[0], m.b1r.at[k - 1], S_B1 + k - 1, chip_dev(k)).wait_recv()
         row8 = lax.broadcasted_iota(jnp.int32, (8, 1), 0)
@@ -797,7 +973,13 @@
         m.dmodf[me_z] = packed
         for off in range(1, T):
             small(m.dmodf.at[me_z], m.dmodf.at[me_z], S_B2 + off - 1, z_dev(off)).start()
-        pump(1)
+        back_start(1, m.gind)
+        stop()
+        for off in range(1, T):
+            small(m.pks.at[0], m.pkr.at[off - 1], S_PZ + off - 1, z_dev(off)).wait_recv()
+        m.pka[0] = m.pks[me_z] + sum(m.pkr[k] for k in range(T - 1))
+        if NB:
+            sum_step(m.pka, m.pkb, 0, S_PB, 0).start()
         for off in range(1, T):
             got = m.dmodf.at[lax.rem(me_z - off + T, T)]
             small(got, got, S_B2 + off - 1, z_dev(off)).wait_recv()
@@ -806,8 +988,8 @@
             acc = 0.0
             for j in range(6):
                 acc = acc + dot_nt(m.dmodf[zz, :, j * R : (j + 1) * R].astype(B16), m.wada[j])
-            m.bacc[0, :, zz * width : (zz + 1) * width] = acc
-        sum_step(m.bacc, m.brec, 0, S_B3, 1).start()
+            m.macc[0, 0:8, zz * width : (zz + 1) * width] = acc
+        sum_step(m.macc, m.mrec, 0, S_B3, 1, 8).start()
         for i in range(NB + 1):
             if i < NB:
                 sum_finish(m.pka, m.pkb, i, S_PB, 0)
@@ -816,11 +998,11 @@
             if i == NB:
                 m.pk[core] = m.pka[NB]
                 small(m.pka.at[NB], m.pk.at[core], S_PC, partner).start()
-            sum_finish(m.bacc, m.brec, i, S_B3, 1)
+            sum_finish(m.macc, m.mrec, i, S_B3, 1, 8)
             if i < NB:
-                sum_step(m.bacc, m.brec, i + 1, S_B3, 1).start()
-            pump(1)
-        m.dsil[...] = m.bacc[NB + 1]
+                sum_step(m.macc, m.mrec, i + 1, S_B3, 1, 8).start()
+            stop()
+        m.dsil[...] = m.macc[NB + 1, 0:8]
     pump(len(events))
     assert not events
     rs_end()
@@ -830,8 +1012,7 @@
     sid_copy.wait_send()
     if dm.inside:
         for i in range(NB + 1):
-            sum_step(m.macc, m.mrec, i, S_M1, 1).wait_send()
-            sum_step(m.bacc, m.brec, i, S_B3, 1).wait_send()
+            sum_step(m.macc, m.mrec, i, S_B3, 1, 8).wait_send()
         for i in range(NB):
             sum_step(m.pka, m.pkb, i, S_PB, 0).wait_send()
         for off in range(1, T):
@@ -849,7 +1030,7 @@
         small(got, got, S_PC, partner).wait_recv()
 
 
-def block_call(dm, ws, xb, dyb, sid, extra):
+def block_call(dm, weights, xb, dyb, sid, extra):
     T, NC, NB, Q, M, D, R, C, W = dm.T, dm.NC, dm.bits, dm.Q, dm.M, dm.D, dm.R, dm.C, dm.W
     hq, fu, NCH, half = dm.hq, dm.fu, dm.NCH, dm.half
     TH, NP = T // 2, len(dm.pieces)
@@ -859,8 +1040,8 @@
     any_, vm = pl.BlockSpec(memory_space=pl.ANY), pl.BlockSpec(memory_space=pltpu.VMEM)
     s = jax.ShapeDtypeStruct
     tok, heads, acc = (T, Q, D), (T, M, hq), (NCH, M, CHUNK)
-    ins = {"ws": ws, "xb": xb, "dyb": dyb, "sid": sid, **extra}
-    outs = {"fin": s((2, R, C), F32), "outd": s((2, Q, D), B16), "gind": s((2, Q, D), B16)}
+    ins = {**weights, "xb": xb, "dyb": dyb, "sid": sid, **extra}
+    outs = {"g_qkv": s((3, R, 2 * hq), F32), "g_proj": s((2 * hq, R), F32), "g_up": s((R, 2 * fu), F32), "g_down": s((2 * fu, R), F32), "outd": s((2, Q, D), B16), "gind": s((2, Q, D), B16)}
     totals = {"sums": (8, D), "hsum": (T, 8, hq), "fsum": (T, 8, fu)}
     scratch = {"wall": v((T,) + two + (2 * R, C), B16)}
     for name in "xs dys h1 h2 ab n2 df".split():
@@ -868,11 +1049,11 @@
     for name in "qs ks vs rq rk o ol do".split():
         scratch[name] = v(heads, B16)
     scratch.update(
-        linv=v(heads, F32), r2=v((T, Q, 128), F32), psi=v((M, 128), B16), phi=v((M, 128), B16), sidr=v((8, M), F32),
+        r2=v((T, Q, 128), F32), psi=v((M, 128), B16), phi=v((M, 128), B16), sidr=v((8, M), F32),
         gk=v((T, M, half), B16), duk=v((T, M, half), B16), facc=v(acc, F32), dacc=v(acc, F32),
-        send=v((NCH, T, Q, CHUNK), B16), recv=v((2, NCH, T, Q, CHUNK), B16),
+        send=v((NCH, M, CHUNK), B16), recv=v((2, NCH, M, CHUNK), B16),
         xt=v((D, M), B16), xt2=v((D, M), B16), dqkv=v((M, 3 * hq), B16),
-        zb=v((T - 1, 2 * R, C), B16), fbuf=v((R, C), F32),
+        zb=v((T - 1, 2 * R, C), B16), zx=v((2 * R, C), B16), fbuf=v((FINS, R, half), F32), fturn=v((2, half, R), F32),
     )
     for k in range(NB):
         scratch[f"rb{k}"] = v((SLOTS, 2, TH) + (2,) * (NB - 1 - k) + (2 * R, half), B16)
@@ -884,7 +1065,6 @@
             macc=v((NB + 2, 16, D), F32), mrec=v((NB + 1, 16, D), F32), sm=v((T, 8, D), F32),
             m2s=v((T, 8, 8 * R), F32), m2r=v((T - 1, 8, 8 * R), F32), m3c=v((2, NC, 8, 8 * R), F32),
             b1s=v((NC, 8, 8 * R), F32), b1r=v((NC, 8, 8 * R), F32),
-            bacc=v((NB + 2, 8, D), F32), brec=v((NB + 1, 8, D), F32),
             pks=v((T, 8, W), F32), pkr=v((T - 1, 8, W), F32), pka=v((NB + 1, 8, W), F32), pkb=v((max(NB, 1), 8, W), F32),
         )
     else:
@@ -894,15 +1074,15 @@
     scratch.update(
         c_s=dma((NP,)), c_r=dma((NP,)), c_l=dma((NP,)), z_s=dma((NP, T - 1)), z_r=dma((NP, T - 1)),
         p_s=dma((NP, NB, 2)), p_r=dma((NP, NB, 2)), x_s=dma((2, 2)), x_r=dma((2, T)), x_l=dma((2,)), x_f=dma((2, 2)),
-        e_s=dma((4, NCH)), e_r=dma((4, NCH)), rs_s=dma((NP, NB, 2)), rs_r=dma((NP, NB, 2)), free=reg((NB, 2)),
-        rz_s=dma((NP, T - 1)), rz_r=dma((NP, T - 1)), f_s=dma((NP,)), f_r=dma((NP,)),
+        e_s=dma((4, NCH)), e_r=dma((4, NCH)), rs_s=dma((NP, NB, 2)), rs_r=dma((NP, NB, 2)), free=reg((NB, 2)), took=reg,
+        rz_s=dma((NP, T - 1)), rz_r=dma((NP, T - 1)), f_s=dma((NP,)), f_r=dma((NP,)), z_f=dma((NP,)), rx=dma((NP, 2)),
         o_s=dma((2, T)), o_r=dma((2, 2)), o_l=dma((2,)), s_s=dma((small,)), s_r=dma((small,)),
     )
     names = tuple(ins) + tuple(outs) + tuple(scratch)
     got = pl.pallas_call(
         functools.partial(block_kernel, dm, names),
         out_shape=tuple(outs.values()),
-        in_specs=[any_ if name in ("ws", "xb", "dyb") else vm for name in ins],
+        in_specs=[any_ if name in ("wqkv", "wup", "xb", "dyb") else vm for name in ins],
         out_specs=tuple(any_ if name in ("outd", "gind") else vm for name in outs),
         scratch_shapes=list(scratch.values()),
         compiler_params=pltpu.CompilerParams(
@@ -981,31 +1161,18 @@
 
         extra = {"mods": mods, "hp": hp, "hb": hb}
 
-    def halves(w):
-        return jnp.moveaxis(w.reshape(w.shape[:-1] + (2, w.shape[-1] // 2)), -2, 0)
-
-    qkv_half = halves(query_key_value_weight)
-    ws = jnp.concatenate(
-        [qkv_half[:, 0], qkv_half[:, 1], qkv_half[:, 2], halves(output_projection.T), halves(up_weight), halves(down_weight.T)],
-        axis=-1,
-    )
+    weights = {"wqkv": query_key_value_weight, "wup": up_weight, "wproj": output_projection, "wdown": down_weight}
     pad = ((0, 0), (0, rows - quarter), (0, 0))
     xb = jnp.pad(block_input.astype(B16), pad)
     dyb = jnp.pad(cotangent.astype(B16), pad)
 
-    got = block_call(dm, ws, xb, dyb, sid, extra)
-    fin, outd, gind = got["fin"], got["outd"], got["gind"]
+    got = block_call(dm, weights, xb, dyb, sid, extra)
+    outd, gind = got["outd"], got["gind"]
 
     block_output = block_input + outd[:, :quarter].astype(F32)
     input_grad = cotangent + gind[:, :quarter].astype(F32)
 
-    def joined(lo, n):
-        return jnp.moveaxis(fin[:, :, lo : lo + n], 0, 1).reshape(R, 2 * n)
-
-    w_qkv_grad = jnp.stack([joined(k * hq, hq) for k in range(3)])
-    w_proj_grad = joined(3 * hq, hq).T
-    w_fc1_grad = joined(dm.up, fu)
-    w_fc2_grad = joined(dm.down, fu).T
+    w_qkv_grad, w_proj_grad, w_fc1_grad, w_fc2_grad = (got[name] for name in ("g_qkv", "g_proj", "g_up", "g_down"))
 
     if dm.inside:
         cond = got["cond"][:NC].reshape(total, -1)

time: 366 us -> 301 us (0.82)
  Pallas kernels: 317 us -> 267 us
  local copies, waits for them, and re-layouts: 31.5 us -> 17.5 us
    pallas_call x1, Pallas kernels: 317 us -> 267 us  [block_call(): pl.pallas_call(functools.partial(block_kernel, dm, names), out_shape=tupl...]
    transpose x8 -> x0, local copies, waits for them, and re-layouts: 5.41 us -> none  [joined(): return jnp.moveaxis(fin[:, :, lo:lo + n], 0, 1).reshape(R, 2 * n)]
    unnamed x29 -> x44, local copies, waits for them, and re-layouts: 12.7 us -> 8.63 us
where the time goes in v3:
time: 301 us; the launch traced here: 296 us
  Pallas kernels  267 us (89%)
  local copies, waits for them, and re-layouts  17.5 us (6%)
  other arithmetic  7.51 us (2%)
    pallas_call x1, Pallas kernels, block_call(): pl.pallas_call(functools.partial(block_kernel, dm, names), out_shape=tupl...  267 us
    unnamed x44, local copies, waits for them, and re-layouts  8.63 us

profile of v3, /device:TPU:24, one launch (start us, length us, event | category | flops | bytes accessed | tf_op | source)
XLA Modules:
  0.0 295.9 jit_solution(12737911134097203906)
XLA Ops:
  0.6 1.8 convert_element_type.78
  2.5 0.0 copy-start
  2.5 0.2 copy.47
  2.7 0.9 pad.35.refs_4_
  3.6 0.5 copy-done
  4.1 0.5 convert_element_type.79
  4.6 0.0 copy-start.7
  4.6 0.0 copy-start.12
  4.6 0.0 copy-start.17
  4.6 0.0 copy-start.11
  4.6 0.0 copy-start.8
  4.6 0.0 copy-start.9
  4.6 0.0 copy-start.10
  4.6 0.0 copy-start.16
  4.7 0.2 copy.48
  4.8 0.9 pad.36.refs_5_
  5.8 0.0 copy-done.7
  5.8 0.1 reshape.127
  5.9 0.1 reshape.128
  6.0 0.6 pad.38.refs_6_
  6.6 0.0 copy-done.12
  6.6 0.0 copy-done.17
  6.6 0.0 copy-start.14
  6.6 0.2 fusion.13
  6.8 0.0 copy-done.11
  6.8 0.1 broadcast_select_fusion.1
  6.9 0.1 convert_element_type.82
  7.0 0.0 copy-done.8
  7.0 0.1 broadcast_in_dim.81
  7.1 0.1 broadcast_in_dim.77
  7.2 0.0 copy-done.14
  7.2 0.1 broadcast_in_dim.78
  7.3 0.1 copy.49
  7.4 0.1 broadcast_select_fusion
  7.5 0.1 convert_element_type.81
  7.6 0.6 select_maximum_fusion.refs_7_
  8.3 0.0 copy-done.10
  8.3 0.6 maximum_convert_fusion
  8.9 267.4 %shard_map.246 = (f32[3,128,256]{2,1,0:T(8,128)}, f32[256,128]{1,0:T(8,128)}, f32[128,1024]{1,0:T(8,128)}, f32[1024,128]{1,0:T(8,128)}, bf16[2,176,1024]{2,1,0:T...) custom-call(bf16[3,128,256]{2,1,0:T(8,128)(2,1)} %refs_0_.1, ...), custom_call_target="tpu_custom_call" | custom-call | flops 30000001024 | bytes 10000000 | tf_op jit(solution)/shard_map/pallas_call | solution.py:1082
  276.3 3.2 %copy_add_fusion = (f32[2,170,1024]{2,1,0:T(8,128)S(1)}, f32[2,170,1024]{2,1,0:T(8,128)S(1)}) fusion(f32[2,170,1024]{2,0,1:T(2,128)} %param.16, bf16[2,176,1024]{2,1,0:T(8,128)(2,1)} %get-tuple-element.24, bf16[2,176,1024]{2,1,0:T(8,128)(2,1)} %get-tuple-element.23, f32[2,170,1024]{2,0,1:T(2,128)} %param.15), kind=kLoop, calls=%fused_computation | loop fusion | flops 1392640 | bytes 6963200 | tf_op jit(solution)/shard_map/add | solution.py:1173
  279.4 2.2 copy.56
  281.6 2.2 copy.57
  283.9 0.0 copy-done.13
  283.9 0.0 copy-done.15
  283.9 1.0 fusion.5
  284.9 0.9 fusion
  285.8 0.0 copy-start.1
  285.8 1.2 fusion.1
  287.0 0.6 convert_reduce_fusion
  287.6 0.7 slice_bitcast_fusion
  288.3 0.1 reshape.133
  288.4 0.7 constant_dynamic-slice_fusion
  289.1 0.6 dynamic-slice_bitcast_fusion
  289.7 0.8 slice_reduce_fusion
  290.5 0.1 reshape_squeeze.3
  290.6 0.1 constant_dynamic-slice_fusion.1
  290.7 0.7 copy.59
  291.3 0.8 slice.45
  292.1 0.6 dynamic-slice_bitcast_fusion.1
  292.7 0.0 copy-done.3
  292.7 0.7 copy.69
  293.4 0.7 copy.70
  294.1 0.8 copy.71
  294.9 0.8 copy.72
  (30 shorter events, 0.2 us)
Async XLA Ops:
  2.5 1.6 copy-start
  4.6 1.2 copy-start.7
  4.6 2.0 copy-start.12
  4.6 2.0 copy-start.17
  4.6 2.2 copy-start.11
  4.6 2.4 copy-start.8
  4.6 2.7 copy-start.9
  4.6 3.6 %copy-start.10 = (bf16[6,128]{1,0:T(8,128)(2,1)S(1)}, bf16[6,128]{1,0:T(8,128)(2,1)}, u32[]{:S(2)}) copy-start(bf16[6,128]{1,0:T(8,128)(2,1)} %param.21) | copy-start | bytes 4612
  4.6 3.6 %copy-start.16 = (bf16[2,128]{1,0:T(2,128)(2,1)S(1)}, bf16[2,128]{1,0:T(2,128)(2,1)}, u32[]{:S(2)}) copy-start(bf16[2,128]{1,0:T(2,128)(2,1)} %param.29) | copy-start | bytes 1540
  6.6 0.6 copy-start.14
  281.6 2.2 copy-start.6
  281.6 2.2 copy-start.5
  281.6 2.3 copy-start.13
  281.6 2.3 copy-start.15
  283.8 8.9 %copy-start.3 = (f32[3,128,256]{2,1,0:T(8,128)S(1)}, f32[3,128,256]{2,1,0:T(8,128)}, u32[]{:S(2)}) copy-start(f32[3,128,256]{2,1,0:T(8,128)} %get-tuple-element.92) | copy-start | bytes 1179652
  283.8 9.6 %copy-start.4 = (f32[256,128]{1,0:T(8,128)S(1)}, f32[256,128]{1,0:T(8,128)}, u32[]{:S(2)}) copy-start(f32[256,128]{1,0:T(8,128)} %get-tuple-element.95) | copy-start | bytes 393220
  283.8 10.3 %copy-start.2 = (f32[128,1024]{1,0:T(8,128)S(1)}, f32[128,1024]{1,0:T(8,128)}, u32[]{:S(2)}) copy-start(f32[128,1024]{1,0:T(8,128)} %get-tuple-element.96) | copy-start | bytes 1572868
  285.8 9.0 %copy-start.1 = (f32[1024,128]{1,0:T(8,128)S(1)}, f32[1024,128]{1,0:T(8,128)}, u32[]{:S(2)}) copy-start(f32[1024,128]{1,0:T(8,128)} %get-tuple-element.98) | copy-start | bytes 1572868

commit v4 on v3

--- a/solution.py
+++ b/solution.py
@@ -4,6 +4,7 @@
 import jax.numpy as jnp
 from jax import lax
 from jax.experimental import pallas as pl
+from jax.experimental.layout import Layout, with_layout_constraint
 from jax.experimental.pallas import tpu as pltpu
 from jax.sharding import PartitionSpec as P
 
@@ -11,9 +12,9 @@
 F32, B16 = jnp.float32, jnp.bfloat16
 FINS = 3
 SLOTS = 3
-PUMPS = (0, 0, 0, 1, 2, 3, 3, 2, 2, 2, 2, 2, 2, 2)
+PUMPS = (1, 0, 0, 0, 1, 1, 4, 0, 3, 2, 4, 5, 2, 1)
 BEGIN = ((), ((2, 0),), ((1, 0),), ((2, 1), (1, 1), (0, 0), (0, 1)))
-LEAN = 1.5
+LEAN = 2.0
 CHUNK = 256
 EPS = 1e-06
 FAR = 256.0
@@ -55,7 +56,7 @@
         self.R = width // dp
         self.C = 4 * self.hq + 2 * self.fu
         self.NCH = width // CHUNK
-        self.inside = self.R % 128 == 0 and self.NC <= 8 and hidden // tensor <= width
+        self.inside = self.R % 128 == 0 and self.NC <= tensor and hidden // tensor <= width
         self.W = self.hq + self.fu + width
         hq, fu, half = self.hq, self.fu, self.fu // 2
         up, down = 4 * hq, 4 * hq + fu
@@ -72,8 +73,8 @@
 def block_kernel(dm, names, *refs):
     m = Refs()
     for name, ref in zip(names, refs):
-        if name.startswith("rb"):
-            m.rb = getattr(m, "rb", []) + [ref]
+        if name[:2] in ("rb", "rf"):
+            setattr(m, name[:2], getattr(m, name[:2], []) + [ref])
         else:
             setattr(m, name, ref)
     T, NC, NB, Q, M, D, R, C = dm.T, dm.NC, dm.bits, dm.Q, dm.M, dm.D, dm.R, dm.C
@@ -377,15 +378,30 @@
             fixed[b] = 1 - mybit[b]
         return b, fixed
 
+    FIRST = 1 if dm.inside else 0
+
+    def rf_copy(step, h):
+        lo, width = dm.pieces[dm.sums_order[0]]
+        b, fixed = rs_fixed(step, h, True)
+        part = wall.at[(me_z,) + place(fixed) + (every, pl.ds(lo + h * (width // 2), width // 2))]
+        return rdma(part, m.rf[step].at[h], m.rs_s.at[0, step, h], m.rs_r.at[0, step, h], bit_dev(b))
+
+    def rf_add(step, h):
+        rf_copy(step, h).wait_recv()
+        lo, width = dm.pieces[dm.sums_order[0]]
+        b, fixed = rs_fixed(step, h, False)
+        where = (me_z,) + place(fixed) + (every, pl.ds(lo + h * (width // 2), width // 2))
+        wall[where] = (wall[where].astype(F32) + m.rf[step][h].astype(F32)).astype(B16)
+
     def rs_copy(j, step, h):
         pc = dm.sums_order[j]
         b, fixed = rs_fixed(step, h, True)
         part = wall.at[(half_z(h),) + place(fixed) + (every, cols(pc))]
-        buf = m.rb[step].at[(j % SLOTS, h) + (every,) * (NB - step) + (every, pl.ds(0, dm.pieces[pc][1]))]
+        buf = m.rb[step].at[((j - FIRST) % SLOTS, h) + (every,) * (NB - step) + (every, pl.ds(0, dm.pieces[pc][1]))]
         return rdma(part, buf, m.rs_s.at[j, step, h], m.rs_r.at[j, step, h], bit_dev(b))
 
     def rs_start(j, step, h):
-        if j >= SLOTS:
+        if j - FIRST >= SLOTS:
             pl.semaphore_wait(m.free.at[step, h], 1)
         rs_copy(j, step, h).start()
 
@@ -394,7 +410,7 @@
         rs_copy(j, step, h).wait_recv()
         b, fixed = rs_fixed(step, h, False)
         rest = [k for k in reversed(range(NB)) if k not in fixed]
-        slot, width = j % SLOTS, dm.pieces[pc][1]
+        slot, width = (j - FIRST) % SLOTS, dm.pieces[pc][1]
 
         def one(i, carry):
             zz, r = i // (1 << len(rest)), lax.rem(i, 1 << len(rest))
@@ -413,58 +429,77 @@
         if j + SLOTS < NP:
             pl.semaphore_signal(m.free.at[step, h], inc=1, device_id=bit_dev(b), device_id_type=MESH)
 
-    def rz_copy(j, off):
+    def rz_blocks(j):
         pc = dm.sums_order[j]
-        part = wall.at[(lax.rem(me_z + off, T),) + mine + (every, cols(pc))]
-        return rdma(part, m.zb.at[off - 1, :, cols(pc)], m.rz_s.at[j, off - 1], m.rz_r.at[j, off - 1], z_dev(off))
-
-    def rz_special(j):
-        pc = dm.sums_order[j]
-        far = T - 1 - me_z
-        part = wall.at[(far,) + mine + (every, cols(pc))]
-        return rdma(part, m.zx.at[:, cols(pc)], m.rx.at[j, 0], m.rx.at[j, 1], tag_z((dpi, jnp.where(me_z == 0, 1, T - 2))))
+        if j >= FIRST:
+            return [(mine, cols(pc))]
+        width = dm.pieces[pc][1]
+        return [(place({b: (p >> b) & 1 for b in range(NB)}), pl.ds(p * width, width)) for p in range(NC)]
 
     ends_here = jnp.logical_not(inner)
 
+    def rz_copies(j, off):
+        pc, out = dm.sums_order[j], []
+        for i, (chip_at, at) in enumerate(rz_blocks(j)):
+            part = wall.at[(lax.rem(me_z + off, T),) + chip_at + (every, cols(pc))]
+            sems = m.rz_s.at[j, off - 1, i], m.rz_r.at[j, off - 1, i]
+            out.append(rdma(part, m.zb.at[off - 1, :, at], *sems, z_dev(off)))
+        return out
+
+    def rz_specials(j):
+        pc, out = dm.sums_order[j], []
+        dev = tag_z((dpi, jnp.where(me_z == 0, 1, T - 2)))
+        for i, (chip_at, at) in enumerate(rz_blocks(j)):
+            part = wall.at[(T - 1 - me_z,) + chip_at + (every, cols(pc))]
+            out.append(rdma(part, m.zx.at[:, at], m.rx_s.at[j, i], m.rx_r.at[j, i], dev))
+        return out
+
+    def each(copies, do):
+        for copy in copies:
+            getattr(copy, do)()
+
     def rz_begin(j):
+        if j == FIRST and FIRST:
+            pl.semaphore_wait(m.zfree, T - 1)
+
         @pl.when(ends_here)
         def _():
-            rz_special(j).start()
-            rz_copy(j, 2).start()
+            each(rz_specials(j), "start")
+            each(rz_copies(j, 2), "start")
 
         for off, allowed in line_sends[1:]:
             @pl.when(allowed)
             def _():
-                rz_copy(j, off).start()
+                each(rz_copies(j, off), "start")
 
     def rz_middle(j):
         pc = dm.sums_order[j]
 
         @pl.when(inner)
         def _():
-            got = m.zx.at[:, cols(pc)]
-            rdma(got, got, m.rx.at[j, 0], m.rx.at[j, 1], tag_z((dpi, me_z))).wait_recv()
-            where = (lax.rem(me_z + 2, T),) + mine + (every, cols(pc))
-            wall[where] = (wall[where].astype(F32) + m.zx[:, cols(pc)].astype(F32)).astype(B16)
-            rz_copy(j, 2).start()
+            each(rz_specials(j), "wait_recv")
+            for chip_at, at in rz_blocks(j):
+                where = (lax.rem(me_z + 2, T),) + chip_at + (every, cols(pc))
+                wall[where] = (wall[where].astype(F32) + m.zx[:, at].astype(F32)).astype(B16)
+            each(rz_copies(j, 2), "start")
 
     def rz_wait(j):
-        rz_copy(j, 2).wait_recv()
+        each(rz_copies(j, 2), "wait_recv")
         for off, came in ((1, me_z > 0), (3, me_z < T - 1)):
             @pl.when(came)
             def _():
-                rz_copy(j, off).wait_recv()
+                each(rz_copies(j, off), "wait_recv")
 
     def rz_sent(j):
-        rz_copy(j, 2).wait_send()
+        each(rz_copies(j, 2), "wait_send")
         for off, allowed in line_sends[1:]:
             @pl.when(allowed)
             def _():
-                rz_copy(j, off).wait_send()
+                each(rz_copies(j, off), "wait_send")
 
         @pl.when(ends_here)
         def _():
-            rz_special(j).wait_send()
+            each(rz_specials(j), "wait_send")
 
     def final(pc, c):
         if pc < 3:
@@ -492,8 +527,43 @@
         out, place_ = final(pc, core)
         return rdma(ref.at[at], out.at[place_], m.f_s.at[j], m.f_r.at[j], partner)
 
+    def rz_sum(j, chip_at, at, rows):
+        acc = wall[(me_z,) + chip_at + (rows, cols(dm.sums_order[j]))].astype(F32)
+        for off in range(1, T):
+            acc = acc + m.zb[off - 1, rows, at].astype(F32)
+        return acc
+
+    def finish(j, total):
+        pc = dm.sums_order[j]
+        if j >= FINS:
+            fin_copy(j - FINS).wait_send()
+        ref, at = fin_from(j)
+        out, place_ = final(pc, core)
+        away, kept = total(core_rows(1 - core)), total(core_rows(core))
+        ref[at] = away.T if turned(pc) else away
+        fin_copy(j).start()
+        out[place_] = kept.T if turned(pc) else kept
+
     def rs_event(j, s):
         pc = dm.sums_order[j]
+        if j < FIRST:
+            if s == 1:
+                rz_middle(j)
+            elif s == 2:
+                rz_wait(j)
+                for chip_at, at in rz_blocks(j):
+                    wall[(me_z,) + chip_at + (every, cols(pc))] = rz_sum(j, chip_at, at, every).astype(B16)
+                for off in range(1, T):
+                    pl.semaphore_signal(m.zfree, inc=1, device_id=z_dev(off), device_id_type=MESH)
+            if s > 2:
+                for h in range(2):
+                    rf_add(s - 3, h)
+            if 2 <= s < NB + 2:
+                for h in range(2):
+                    rf_copy(s - 2, h).start()
+            if s == NB + 2:
+                finish(j, lambda rows: wall[(me_z,) + mine + (rows, cols(pc))].astype(F32))
+            return
         if s <= NB:
             for h in range(2):
                 rs_add(j, s - 1, h)
@@ -506,21 +576,7 @@
             rz_middle(j)
             return
         rz_wait(j)
-
-        def total(rows):
-            acc = wall[(me_z,) + mine + (rows, cols(pc))].astype(F32)
-            for off in range(1, T):
-                acc = acc + m.zb[off - 1, rows, cols(pc)].astype(F32)
-            return acc
-
-        if j >= FINS:
-            fin_copy(j - FINS).wait_send()
-        ref, at = fin_from(j)
-        out, place_ = final(pc, core)
-        away, kept = total(core_rows(1 - core)), total(core_rows(core))
-        ref[at] = away.T if turned(pc) else away
-        fin_copy(j).start()
-        out[place_] = kept.T if turned(pc) else kept
+        finish(j, lambda rows: rz_sum(j, mine, cols(pc), rows))
 
     events = sorted(((j, s) for j in range(NP) for s in range(1, NB + 3)), key=lambda e: (e[0] + LEAN * e[1], e[0]))
     begun = set()
@@ -537,16 +593,19 @@
 
     def rs_begin(pc, h):
         j = place_of[pc]
-        while (j - SLOTS, 1) in events:
+        while j - SLOTS >= FIRST and (j - SLOTS, 1) in events:
             pump(1)
-        rs_start(j, 0, h)
+        if j >= FIRST:
+            rs_start(j, 0, h)
+        elif h == 1:
+            rz_begin(j)
         begun.add((j, h))
 
     def rs_end():
         for j in range(NP):
             for step in range(NB):
                 for h in range(2):
-                    rs_copy(j, step, h).wait_send()
+                    (rs_copy(j, step, h) if j >= FIRST else rf_copy(step, h)).wait_send()
             rz_sent(j)
             fin_copy(j).wait_recv()
             if j + FINS >= NP:
@@ -956,24 +1015,26 @@
         back_start(1, m.gind)
 
     if dm.inside:
+        for off in range(1, T):
+            zt = lax.rem(me_z + off, T)
+            small(m.m2s.at[zt], m.m2r.at[off - 1], S_M2 + off - 1, z_dev(off)).wait_send()
         for p in range(NC):
             d = pl.multiple_of((2 * p + core) * R, R)
             rows = [sums[j : j + 1, pl.ds(d, R)] for j in range(8)]
-            m.b1s[p] = jnp.broadcast_to(jnp.concatenate(rows, axis=-1), (8, 8 * R))
+            m.m2s[p] = jnp.broadcast_to(jnp.concatenate(rows, axis=-1), (8, 8 * R))
         for k in range(1, NC):
-            small(m.b1s.at[lax.rem(chip + k, NC)], m.b1r.at[k - 1], S_B1 + k - 1, chip_dev(k)).start()
+            small(m.m2s.at[lax.rem(chip + k, NC)], m.b1r.at[k - 1], S_B1 + k - 1, chip_dev(k)).start()
         stop()
         stop()
         for k in range(1, NC):
-            small(m.b1s.at[0], m.b1r.at[k - 1], S_B1 + k - 1, chip_dev(k)).wait_recv()
+            small(m.m2s.at[0], m.b1r.at[k - 1], S_B1 + k - 1, chip_dev(k)).wait_recv()
         row8 = lax.broadcasted_iota(jnp.int32, (8, 1), 0)
-        packed = jnp.where(row8 == chip, m.b1s[chip], 0.0)
+        packed = jnp.where(row8 == chip, m.m2s[chip], 0.0)
         for k in range(1, NC):
             packed = jnp.where(row8 == lax.rem(chip - k + NC, NC), m.b1r[k - 1], packed)
         m.dmodf[me_z] = packed
         for off in range(1, T):
             small(m.dmodf.at[me_z], m.dmodf.at[me_z], S_B2 + off - 1, z_dev(off)).start()
-        back_start(1, m.gind)
         stop()
         for off in range(1, T):
             small(m.pks.at[0], m.pkr.at[off - 1], S_PZ + off - 1, z_dev(off)).wait_recv()
@@ -1003,6 +1064,10 @@
                 sum_step(m.macc, m.mrec, i + 1, S_B3, 1, 8).start()
             stop()
         m.dsil[...] = m.macc[NB + 1, 0:8]
+    while (NP - 1, NB) in events:
+        pump(1)
+    if dm.inside:
+        back_start(1, m.gind)
     pump(len(events))
     assert not events
     rs_end()
@@ -1018,12 +1083,11 @@
         for off in range(1, T):
             zt = lax.rem(me_z + off, T)
             small(m.sm.at[me_z], m.sm.at[me_z], S_SM + off - 1, z_dev(off)).wait_send()
-            small(m.m2s.at[zt], m.m2r.at[off - 1], S_M2 + off - 1, z_dev(off)).wait_send()
             small(m.pks.at[zt], m.pkr.at[off - 1], S_PZ + off - 1, z_dev(off)).wait_send()
             small(m.dmodf.at[me_z], m.dmodf.at[me_z], S_B2 + off - 1, z_dev(off)).wait_send()
         for k in range(1, NC):
             small(m.m3c.at[core, chip], m.m3c.at[core, chip], S_M3 + k - 1, chip_dev(k)).wait_send()
-            small(m.b1s.at[lax.rem(chip + k, NC)], m.b1r.at[k - 1], S_B1 + k - 1, chip_dev(k)).wait_send()
+            small(m.m2s.at[lax.rem(chip + k, NC)], m.b1r.at[k - 1], S_B1 + k - 1, chip_dev(k)).wait_send()
         small(m.m3c.at[core], m.m3c.at[core], S_M4, partner).wait_send()
         small(m.pka.at[NB], m.pk.at[core], S_PC, partner).wait_send()
         got = m.pk.at[1 - core]
@@ -1056,6 +1120,7 @@
         zb=v((T - 1, 2 * R, C), B16), zx=v((2 * R, C), B16), fbuf=v((FINS, R, half), F32), fturn=v((2, half, R), F32),
     )
     for k in range(NB):
+        scratch[f"rf{k}"] = v((2,) + (2,) * (NB - 1 - k) + (2 * R, half // 2), B16)
         scratch[f"rb{k}"] = v((SLOTS, 2, TH) + (2,) * (NB - 1 - k) + (2 * R, half), B16)
     if dm.inside:
         outs.update(dmodf=s((T, 8, 8 * R), F32), cond=s((8, D), F32), dsil=s((8, D), F32), pk=s((2, 8, W), F32))
@@ -1064,7 +1129,7 @@
             mods=v((8, D), F32), hp=v((T, 8, hq), F32), hb=v((T, 8, fu), F32),
             macc=v((NB + 2, 16, D), F32), mrec=v((NB + 1, 16, D), F32), sm=v((T, 8, D), F32),
             m2s=v((T, 8, 8 * R), F32), m2r=v((T - 1, 8, 8 * R), F32), m3c=v((2, NC, 8, 8 * R), F32),
-            b1s=v((NC, 8, 8 * R), F32), b1r=v((NC, 8, 8 * R), F32),
+            b1r=v((max(NC - 1, 1), 8, 8 * R), F32),
             pks=v((T, 8, W), F32), pkr=v((T - 1, 8, W), F32), pka=v((NB + 1, 8, W), F32), pkb=v((max(NB, 1), 8, W), F32),
         )
     else:
@@ -1075,7 +1140,7 @@
         c_s=dma((NP,)), c_r=dma((NP,)), c_l=dma((NP,)), z_s=dma((NP, T - 1)), z_r=dma((NP, T - 1)),
         p_s=dma((NP, NB, 2)), p_r=dma((NP, NB, 2)), x_s=dma((2, 2)), x_r=dma((2, T)), x_l=dma((2,)), x_f=dma((2, 2)),
         e_s=dma((4, NCH)), e_r=dma((4, NCH)), rs_s=dma((NP, NB, 2)), rs_r=dma((NP, NB, 2)), free=reg((NB, 2)), took=reg,
-        rz_s=dma((NP, T - 1)), rz_r=dma((NP, T - 1)), f_s=dma((NP,)), f_r=dma((NP,)), z_f=dma((NP,)), rx=dma((NP, 2)),
+        rz_s=dma((NP, T - 1, NC)), rz_r=dma((NP, T - 1, NC)), rx_s=dma((NP, NC)), rx_r=dma((NP, NC)), zfree=reg, f_s=dma((NP,)), f_r=dma((NP,)), z_f=dma((NP,)),
         o_s=dma((2, T)), o_r=dma((2, 2)), o_l=dma((2,)), s_s=dma((small,)), s_r=dma((small,)),
     )
     names = tuple(ins) + tuple(outs) + tuple(scratch)
@@ -1169,8 +1234,14 @@
     got = block_call(dm, weights, xb, dyb, sid, extra)
     outd, gind = got["outd"], got["gind"]
 
-    block_output = block_input + outd[:, :quarter].astype(F32)
-    input_grad = cotangent + gind[:, :quarter].astype(F32)
+    outermost = Layout(major_to_minor=(0, 1, 2))
+
+    def added(base, step):
+        step = with_layout_constraint(jnp.swapaxes(step, 0, 1), outermost)
+        out = with_layout_constraint(jnp.swapaxes(base, 0, 1) + step[:quarter].astype(F32), outermost)
+        return jnp.swapaxes(out, 0, 1)
+
+    block_output, input_grad = added(block_input, outd), added(cotangent, gind)
 
     w_qkv_grad, w_proj_grad, w_fc1_grad, w_fc2_grad = (got[name] for name in ("g_qkv", "g_proj", "g_up", "g_down"))
 

time: 301 us -> 291 us (0.967)
  Pallas kernels: 267 us -> 258 us
    pallas_call x1, Pallas kernels: 267 us -> 258 us  [block_call(): pl.pallas_call(functools.partial(block_kernel, dm, names), out_shape=tupl...]
    unnamed x44 -> x46, local copies, waits for them, and re-layouts: 8.63 us -> 4.33 us
    transpose x0 -> x2, other arithmetic: none -> 3.6 us  [added(): return jnp.swapaxes(out, 0, 1)]
    add x1 -> x0, other arithmetic: 3.16 us -> none  [local(): input_grad = cotangent + gind[:, :quarter].astype(F32)]
where the time goes in v4:
time: 291 us; the launch traced here: 285 us
  Pallas kernels  258 us (89%)
  local copies, waits for them, and re-layouts  16.1 us (6%)
  other arithmetic  7.95 us (3%)
    pallas_call x1, Pallas kernels, block_call(): pl.pallas_call(functools.partial(block_kernel, dm, names), out_shape=tupl...  258 us

profile of v4, /device:TPU:24, one launch (start us, length us, event | category | flops | bytes accessed | tf_op | source)
XLA Modules:
  0.0 285.5 jit_solution(1383761085407786967)
XLA Ops:
  0.6 1.8 convert_element_type.78
  2.5 0.0 copy-start.1
  2.5 0.2 copy.43
  2.7 0.9 pad.35.refs_4_
  3.6 0.5 copy-done.1
  4.1 0.5 convert_element_type.79
  4.6 0.0 copy-start.9
  4.6 0.0 copy-start.14
  4.6 0.0 copy-start.19
  4.6 0.0 copy-start.13
  4.6 0.0 copy-start.10
  4.6 0.0 copy-start.11
  4.6 0.0 copy-start.12
  4.6 0.0 copy-start.18
  4.7 0.2 copy.44
  4.8 0.9 pad.36.refs_5_
  5.8 0.0 copy-done.9
  5.8 0.1 reshape.127
  5.9 0.1 reshape.128
  6.0 0.6 pad.38.refs_6_
  6.6 0.0 copy-done.14
  6.6 0.0 copy-done.19
  6.6 0.0 copy-start.16
  6.6 0.2 fusion.15
  6.8 0.1 broadcast_select_fusion.1
  6.9 0.1 convert_element_type.82
  7.0 0.1 broadcast_in_dim.81
  7.1 0.1 broadcast_in_dim.77
  7.2 0.0 copy-done.16
  7.2 0.1 broadcast_in_dim.78
  7.3 0.1 copy.45
  7.4 0.1 broadcast_select_fusion
  7.5 0.1 convert_element_type.81
  7.6 0.6 select_maximum_fusion.refs_7_
  8.3 0.0 copy-done.18
  8.3 0.6 maximum_convert_fusion
  8.9 257.7 %shard_map.246 = (f32[3,128,256]{2,1,0:T(8,128)}, f32[256,128]{1,0:T(8,128)}, f32[128,1024]{1,0:T(8,128)}, f32[1024,128]{1,0:T(8,128)}, bf16[2,176,1024]{2,1,0:T...) custom-call(bf16[3,128,256]{2,1,0:T(8,128)(2,1)} %refs_0_.1, ...), custom_call_target="tpu_custom_call" | custom-call | flops 30000001024 | bytes 10000000 | tf_op jit(solution)/shard_map/pallas_call | solution.py:1147
  266.6 0.0 copy-start
  266.6 2.9 %copy_bitcast_fusion = (bf16[176,2,1024]{2,1,0:T(2,128)(2,1)S(1)}, bf16[176,2,1024]{2,1,0:T(2,128)(2,1)S(1)}) fusion(bf16[2,176,1024]{2,1,0:T(8,128)(2,1)} %get-tuple-element.24, bf16[2,176,1024]{2,1,0:T(8,128)(2,1)} %get-tuple-element.23), kind=kLoop, calls=%fused_computation.4 | loop fusion | bytes 2883584 | tf_op jit(solution)/shard_map/transpose | solution.py:1240
  269.5 0.0 copy-start.2
  269.5 1.8 fusion.1
  271.3 0.0 copy-done.2
  271.3 0.0 copy-start.17
  271.3 1.8 fusion
  273.2 1.0 fusion.7
  274.2 0.9 fusion.2
  275.2 1.2 fusion.3
  276.4 0.6 convert_reduce_fusion
  277.0 0.7 slice_bitcast_fusion
  277.7 0.1 reshape.133
  277.8 0.7 constant_dynamic-slice_fusion
  278.5 0.6 dynamic-slice_bitcast_fusion
  279.1 0.8 slice_reduce_fusion
  279.9 0.1 reshape_squeeze.3
  280.0 0.1 constant_dynamic-slice_fusion.1
  280.0 0.7 copy.53
  280.7 0.8 slice.45
  281.5 0.6 dynamic-slice_bitcast_fusion.1
  282.0 0.0 copy-done.5
  282.0 0.7 copy.63
  282.8 0.7 copy.64
  283.4 0.8 copy.65
  284.2 0.0 copy-done.3
  284.2 0.8 copy.66
  (34 shorter events, 0.2 us)
Async XLA Ops:
  2.5 1.6 copy-start.1
  4.6 1.2 copy-start.9
  4.6 2.0 copy-start.14
  4.6 2.0 copy-start.19
  4.6 2.2 copy-start.13
  4.6 2.4 copy-start.10
  4.6 2.7 copy-start.11
  4.6 3.6 %copy-start.12 = (bf16[6,128]{1,0:T(8,128)(2,1)S(1)}, bf16[6,128]{1,0:T(8,128)(2,1)}, u32[]{:S(2)}) copy-start(bf16[6,128]{1,0:T(8,128)(2,1)} %param.21) | copy-start | bytes 4612
  4.6 3.6 %copy-start.18 = (bf16[2,128]{1,0:T(2,128)(2,1)S(1)}, bf16[2,128]{1,0:T(2,128)(2,1)}, u32[]{:S(2)}) copy-start(bf16[2,128]{1,0:T(2,128)(2,1)} %param.29) | copy-start | bytes 1540
  6.6 0.6 copy-start.16
  266.6 2.9 %copy-start = (f32[2,170,1024]{2,0,1:T(2,128)S(1)}, f32[2,170,1024]{2,0,1:T(2,128)}, u32[]{:S(2)}) copy-start(f32[2,170,1024]{2,0,1:T(2,128)} %param.15) | copy-start | bytes 4177924
  269.5 1.8 copy-start.2
  271.3 1.8 copy-start.8
  271.3 1.9 copy-start.7
  271.3 1.9 copy-start.15
  271.3 1.9 copy-start.17
  273.1 8.9 %copy-start.5 = (f32[3,128,256]{2,1,0:T(8,128)S(1)}, f32[3,128,256]{2,1,0:T(8,128)}, u32[]{:S(2)}) copy-start(f32[3,128,256]{2,1,0:T(8,128)} %get-tuple-element.53) | copy-start | bytes 1179652
  273.1 9.6 %copy-start.6 = (f32[256,128]{1,0:T(8,128)S(1)}, f32[256,128]{1,0:T(8,128)}, u32[]{:S(2)}) copy-start(f32[256,128]{1,0:T(8,128)} %get-tuple-element.56) | copy-start | bytes 393220
  273.1 10.3 %copy-start.4 = (f32[128,1024]{1,0:T(8,128)S(1)}, f32[128,1024]{1,0:T(8,128)}, u32[]{:S(2)}) copy-start(f32[128,1024]{1,0:T(8,128)} %get-tuple-element.57) | copy-start | bytes 1572868
  275.2 9.0 %copy-start.3 = (f32[1024,128]{1,0:T(8,128)S(1)}, f32[1024,128]{1,0:T(8,128)}, u32[]{:S(2)}) copy-start(f32[1024,128]{1,0:T(8,128)} %get-tuple-element.59) | copy-start | bytes 1572868

commit v5 on v4

--- a/solution.py
+++ b/solution.py
@@ -10,7 +10,7 @@
 
 MESH = pl.DeviceIdType.MESH
 F32, B16 = jnp.float32, jnp.bfloat16
-FINS = 3
+FINS = 2
 SLOTS = 3
 PUMPS = (1, 0, 0, 0, 1, 1, 4, 0, 3, 2, 4, 5, 2, 1)
 BEGIN = ((), ((2, 0),), ((1, 0),), ((2, 1), (1, 1), (0, 0), (0, 1)))
@@ -667,10 +667,10 @@
         m.sm[me_z] = m.macc[NB + 1, 8:16, :]
         for off in range(1, T):
             small(m.sm.at[me_z], m.sm.at[me_z], S_SM + off - 1, z_dev(off)).start()
-        m.cond[...] = m.macc[NB + 1, 0:8, :]
         width = D // T
         for zz in range(T):
-            c = m.cond[:, zz * width : (zz + 1) * width]
+            c = m.macc[NB + 1, 0:8, zz * width : (zz + 1) * width]
+            m.cond[8 * zz : 8 * zz + 8, :] = c
             low = (c / (1.0 + jnp.exp(-c))).astype(B16)
             rows = [dot(low, m.wada[j]) for j in range(6)] + [jnp.zeros((8, 2 * R), F32)]
             m.m2s[zz] = jnp.concatenate(rows, axis=-1)
@@ -763,11 +763,11 @@
     lax.fori_loop(0, T, qkv, 0)
     zero16 = jnp.zeros((), B16)
 
-    def expo(z, k, q_all, k_all):
-        q_one = jnp.where(halves[k], q_all, zero16)
-        left = jnp.concatenate([q_one, m.psi[...]], axis=1)
+    def expo(z, k, q_all, k_all, rows=slice(None)):
+        q_one = jnp.where(halves[k], q_all[rows], zero16)
+        left = jnp.concatenate([q_one, m.psi[rows, :]], axis=1)
         right = jnp.concatenate([k_all, m.phi[...]], axis=1)
-        return q_one, jnp.exp(dot_nt(left, right)).astype(B16)
+        return q_one, jnp.exp(dot_nt(left, right))
 
     def attend(z, carry):
         q_all, k_all, v_all = m.qs[z], m.ks[z], m.vs[z]
@@ -775,7 +775,7 @@
         mixed = inverse = None
         for k in range(hq // dm.hd):
             _, e = expo(z, k, q_all, k_all)
-            both_ = dot(e, v_ones)
+            both_ = dot(e.astype(B16), v_ones)
             inv = 1.0 / both_[:, hq:]
             one = both_[:, :hq] * inv
             mixed = one if mixed is None else jnp.where(halves[k], one, mixed)
@@ -950,18 +950,23 @@
         v_ends = jnp.concatenate([v_all, jnp.broadcast_to(ends, (M, hq))], axis=1)
         dq = dk = dv = 0.0
         for k in range(hq // dm.hd):
-            q_one, e = expo(z, k, q_all, k_all)
             to_all = (bi == k).astype(B16)
             total = split_dot(prod, to_all)
             high = total.astype(B16)
             low = (total - high.astype(F32)).astype(B16)
             extra = jnp.where(lane == 0, high, jnp.where(lane == 1, low, zero16))
             d_one = jnp.where(halves[k], dob, zero16)
-            dp = dot_nt(jnp.concatenate([d_one, extra], axis=1), v_ends)
-            ds = (e.astype(F32) * dp).astype(B16)
-            dq = dq + dot(ds, jnp.where(halves[k], k_all, zero16))
-            dk = dk + dot_tn(ds, q_one)
-            dv = dv + dot_tn(e, d_one)
+            d_ext = jnp.concatenate([d_one, extra], axis=1)
+            k_one = jnp.where(halves[k], k_all, zero16)
+            dq_rows = []
+            for rows in (slice(0, 256), slice(256, M)):
+                q_one, e = expo(z, k, q_all, k_all, rows)
+                dp = dot_nt(d_ext[rows], v_ends)
+                ds = (e * dp).astype(B16)
+                dq_rows.append(dot(ds, k_one))
+                dk = dk + dot_tn(ds, q_one)
+                dv = dv + dot_tn(e.astype(B16), d_one[rows])
+            dq = dq + jnp.concatenate(dq_rows, axis=0)
         gain = hp[z, 2:3, :]
         q_hat = q_all.astype(F32) * hp[z, 3:4, :]
         k_hat = k_all.astype(F32)
@@ -1047,6 +1052,8 @@
         width = D // T
         for zz in range(T):
             acc = 0.0
+            for j in range(8):
+                m.dmod[j, 8 * zz : 8 * zz + 8, :] = m.dmodf[zz, :, j * R : (j + 1) * R]
             for j in range(6):
                 acc = acc + dot_nt(m.dmodf[zz, :, j * R : (j + 1) * R].astype(B16), m.wada[j])
             m.macc[0, 0:8, zz * width : (zz + 1) * width] = acc
@@ -1063,7 +1070,8 @@
             if i < NB:
                 sum_step(m.macc, m.mrec, i + 1, S_B3, 1, 8).start()
             stop()
-        m.dsil[...] = m.macc[NB + 1, 0:8]
+        for zz in range(T):
+            m.dsil[8 * zz : 8 * zz + 8, :] = m.macc[NB + 1, 0:8, zz * width : (zz + 1) * width]
     while (NP - 1, NB) in events:
         pump(1)
     if dm.inside:
@@ -1123,10 +1131,10 @@
         scratch[f"rf{k}"] = v((2,) + (2,) * (NB - 1 - k) + (2 * R, half // 2), B16)
         scratch[f"rb{k}"] = v((SLOTS, 2, TH) + (2,) * (NB - 1 - k) + (2 * R, half), B16)
     if dm.inside:
-        outs.update(dmodf=s((T, 8, 8 * R), F32), cond=s((8, D), F32), dsil=s((8, D), F32), pk=s((2, 8, W), F32))
+        outs.update(dmod=s((8, 8 * T, R), F32), cond=s((8 * T, D // T), F32), dsil=s((8 * T, D // T), F32), pk=s((2, 8, W), F32))
         scratch.update({name: v(shape, F32) for name, shape in totals.items()})
         scratch.update(
-            mods=v((8, D), F32), hp=v((T, 8, hq), F32), hb=v((T, 8, fu), F32),
+            dmodf=v((T, 8, 8 * R), F32), mods=v((8, D), F32), hp=v((T, 8, hq), F32), hb=v((T, 8, fu), F32),
             macc=v((NB + 2, 16, D), F32), mrec=v((NB + 1, 16, D), F32), sm=v((T, 8, D), F32),
             m2s=v((T, 8, 8 * R), F32), m2r=v((T - 1, 8, 8 * R), F32), m3c=v((2, NC, 8, 8 * R), F32),
             b1r=v((max(NC - 1, 1), 8, 8 * R), F32),
@@ -1246,12 +1254,13 @@
     w_qkv_grad, w_proj_grad, w_fc1_grad, w_fc2_grad = (got[name] for name in ("g_qkv", "g_proj", "g_up", "g_down"))
 
     if dm.inside:
-        cond = got["cond"][:NC].reshape(total, -1)
-        silu, silu_back = jax.vjp(jax.nn.silu, cond)
-        dmod = jnp.swapaxes(got["dmodf"][:, :NC], 0, 1).reshape(total, 8, R)[:, :6].astype(B16)
-        b_ada_grad = jnp.sum(dmod.astype(F32), axis=0)
-        w_ada_grad = jnp.einsum("sc,sjd->cjd", silu.astype(B16), dmod, preferred_element_type=F32)
-        (d_cond,) = silu_back(got["dsil"][:NC].reshape(total, -1))
+        silu, silu_back = jax.vjp(jax.nn.silu, got["cond"])
+        dmod = got["dmod"][:6].astype(B16)
+        b_ada_grad = jnp.sum(dmod.astype(F32), axis=1)
+        w_ada_grad = jnp.einsum("sc,jsd->cjd", silu.astype(B16), dmod, preferred_element_type=F32)
+        (d_cond,) = silu_back(got["dsil"])
+        ids = jnp.pad(class_ids.reshape(NC, T).T, ((0, 0), (0, 8 - NC)), constant_values=-1).reshape(-1)
+        hot = ids[:, None] == my_ids[None, :]
         pk = got["pk"]
 
         def own(w, n):
@@ -1260,7 +1269,7 @@
         heads = own(jnp.swapaxes(pk[:, :3, :hq], 0, 1).reshape(3, -1, head), head // dp)
         qv_bias_grad, q_gain_grad = heads[:2], heads[2]
         b_fc1_grad = own(pk[:, 0, hq : hq + fu].reshape(hidden_bias.shape[0], -1), hidden_bias.shape[1])
-        b_out_grad = own(pk[0, 6:8, hq + fu :], R)
+        b_out_grad = lax.dynamic_slice(pk, (0, 6, hq + fu + di * R), (1, 2, R))[0]
     else:
         sums, hsum, fsum = got["sums"], got["hsum"], got["fsum"]
         dmod = sums[:6].reshape(6, dp, R).astype(B16)

time: 291 us -> 288 us (0.990)
  no operation moved by 1% of the time
where the time goes in v5:
time: 288 us; the launch traced here: 284 us
  Pallas kernels  258 us (90%)
  local copies, waits for them, and re-layouts  15.3 us (5%)
  other arithmetic  7.95 us (3%)
    pallas_call x1, Pallas kernels, block_call(): pl.pallas_call(functools.partial(block_kernel, dm, names), out_shape=tupl...  258 us

profile of v5, /device:TPU:24, one launch (start us, length us, event | category | flops | bytes accessed | tf_op | source)
XLA Modules:
  0.0 284.4 jit_solution(16989433796211910450)
XLA Ops:
  0.6 1.8 convert_element_type.78
  2.5 0.0 copy-start.1
  2.5 0.2 copy.43
  2.7 0.9 pad.39.refs_4_
  3.6 0.5 copy-done.1
  4.1 0.5 convert_element_type.79
  4.6 0.0 copy-start.9
  4.6 0.0 copy-start.14
  4.6 0.0 copy-start.17
  4.6 0.0 copy-start.13
  4.6 0.0 copy-start.10
  4.6 0.0 copy-start.11
  4.6 0.0 copy-start.12
  4.6 0.0 copy-start.16
  4.7 0.2 copy.44
  4.8 0.9 pad.40.refs_5_
  5.8 0.0 copy-done.9
  5.8 0.1 reshape.120
  5.9 0.1 reshape.121
  6.0 0.6 pad.42.refs_6_
  6.6 0.0 copy-done.14
  6.6 0.0 copy-start.19
  6.6 0.2 fusion.19
  6.8 0.1 broadcast_select_fusion.1
  6.9 0.1 convert_element_type.82
  7.0 0.1 broadcast_in_dim.82
  7.1 0.1 broadcast_in_dim.78
  7.2 0.0 copy-done.19
  7.2 0.1 broadcast_in_dim.79
  7.3 0.1 copy.45
  7.4 0.1 broadcast_select_fusion
  7.5 0.1 convert_element_type.81
  7.6 0.6 select_maximum_fusion.refs_7_
  8.3 0.6 maximum_convert_fusion
  8.9 257.7 %shard_map.246 = (f32[3,128,256]{2,1,0:T(8,128)}, f32[256,128]{1,0:T(8,128)}, f32[128,1024]{1,0:T(8,128)}, f32[1024,128]{1,0:T(8,128)}, bf16[2,176,1024]{2,1,0:T...) custom-call(bf16[3,128,256]{2,1,0:T(8,128)(2,1)} %refs_0_.1, ...), custom_call_target="tpu_custom_call" | custom-call | flops 30000001024 | bytes 10000000 | tf_op jit(solution)/shard_map/pallas_call | solution.py:1155
  266.6 0.0 copy-start
  266.6 2.9 %copy_bitcast_fusion = (bf16[176,2,1024]{2,1,0:T(2,128)(2,1)S(1)}, bf16[176,2,1024]{2,1,0:T(2,128)(2,1)S(1)}) fusion(bf16[2,176,1024]{2,1,0:T(8,128)(2,1)} %get-tuple-element.24, bf16[2,176,1024]{2,1,0:T(8,128)(2,1)} %get-tuple-element.23), kind=kLoop, calls=%fused_computation.4 | loop fusion | bytes 2883584 | tf_op jit(solution)/shard_map/transpose | solution.py:1248
  269.5 0.0 copy-done
  269.5 0.0 copy-start.2
  269.5 1.8 fusion.1
  271.3 0.0 copy-start.20
  271.3 1.8 fusion
  273.2 0.1 reshape.123
  273.2 0.1 copy.52
  273.3 0.1 eq.39
  273.4 0.0 copy-done.20
  273.4 1.0 fusion.4
  274.4 0.0 copy-done.6
  274.4 1.2 fusion.8
  275.6 0.6 convert_reduce_fusion
  276.2 0.7 slice_bitcast_fusion
  276.9 0.1 reshape.124
  277.0 0.7 constant_dynamic-slice_fusion
  277.7 0.6 dynamic-slice_bitcast_fusion
  278.3 0.8 slice_reduce_fusion
  279.1 0.1 reshape_squeeze.3
  279.2 0.1 constant_dynamic-slice_fusion.1
  279.3 0.7 copy.51
  279.9 1.3 dynamic-slice_bitcast_fusion.1
  281.2 0.7 copy.59
  282.0 0.7 copy.60
  282.6 0.8 copy.61
  283.4 0.0 copy-done.3
  283.4 0.8 copy.62
  (32 shorter events, 0.1 us)
Async XLA Ops:
  2.5 1.6 copy-start.1
  4.6 1.2 copy-start.9
  4.6 2.0 copy-start.14
  4.6 2.0 copy-start.17
  4.6 2.2 copy-start.13
  4.6 2.4 copy-start.10
  4.6 2.7 copy-start.11
  4.6 3.6 %copy-start.12 = (bf16[6,128]{1,0:T(8,128)(2,1)S(1)}, bf16[6,128]{1,0:T(8,128)(2,1)}, u32[]{:S(2)}) copy-start(bf16[6,128]{1,0:T(8,128)(2,1)} %param.21) | copy-start | bytes 4612
  4.6 3.6 %copy-start.16 = (bf16[2,128]{1,0:T(2,128)(2,1)S(1)}, bf16[2,128]{1,0:T(2,128)(2,1)}, u32[]{:S(2)}) copy-start(bf16[2,128]{1,0:T(2,128)(2,1)} %param.29) | copy-start | bytes 1540
  6.6 0.6 copy-start.19
  266.6 2.9 %copy-start = (f32[2,170,1024]{2,0,1:T(2,128)S(1)}, f32[2,170,1024]{2,0,1:T(2,128)}, u32[]{:S(2)}) copy-start(f32[2,170,1024]{2,0,1:T(2,128)} %param.15) | copy-start | bytes 4177924
  269.5 1.8 copy-start.2
  271.3 1.8 copy-start.15
  271.3 2.1 copy-start.8
  271.3 2.1 copy-start.18
  271.3 2.1 copy-start.20
  271.3 3.1 %copy-start.6 = (f32[8,32,128]{2,1,0:T(8,128)S(1)}, f32[8,32,128]{2,1,0:T(8,128)}, u32[]{:S(2)}) copy-start(f32[8,32,128]{2,1,0:T(8,128)} %get-tuple-element.27) | copy-start | bytes 393220
  273.1 8.1 %copy-start.5 = (f32[3,128,256]{2,1,0:T(8,128)S(1)}, f32[3,128,256]{2,1,0:T(8,128)}, u32[]{:S(2)}) copy-start(f32[3,128,256]{2,1,0:T(8,128)} %get-tuple-element.53) | copy-start | bytes 1179652
  273.1 8.8 %copy-start.7 = (f32[256,128]{1,0:T(8,128)S(1)}, f32[256,128]{1,0:T(8,128)}, u32[]{:S(2)}) copy-start(f32[256,128]{1,0:T(8,128)} %get-tuple-element.56) | copy-start | bytes 393220
  273.1 9.5 %copy-start.4 = (f32[128,1024]{1,0:T(8,128)S(1)}, f32[128,1024]{1,0:T(8,128)}, u32[]{:S(2)}) copy-start(f32[128,1024]{1,0:T(8,128)} %get-tuple-element.57) | copy-start | bytes 1572868
  274.4 9.0 %copy-start.3 = (f32[1024,128]{1,0:T(8,128)S(1)}, f32[1024,128]{1,0:T(8,128)}, u32[]{:S(2)}) copy-start(f32[1024,128]{1,0:T(8,128)} %get-tuple-element.59) | copy-start | bytes 1572868

commit v6 on v5

--- a/solution.py
+++ b/solution.py
@@ -153,23 +153,39 @@
         dst = wall.at[(me_z,) + mine + (core_rows(core), cols(pc))]
         return pltpu.make_async_copy(own_weight(pc, core), dst, m.c_l.at[pc])
 
-    def z_copy(pc, off):
-        part = wall.at[(me_z,) + mine + (every, cols(pc))]
-        return rdma(part, part, m.z_s.at[pc, off - 1], m.z_r.at[pc, off - 1], z_dev(off))
+    mixed = (NP - 1,) if dm.inside and NB == 2 else ()
+
+    def half_rows(h):
+        return pl.ds(h * R, R)
+
+    def z_parts(pc, z):
+        if pc not in mixed:
+            return [wall.at[(z,) + mine + (every, cols(pc))]]
+        known = [place({order[h][1]: mybit[order[h][1]]}) for h in range(2)]
+        return [wall.at[(z,) + known[h] + (half_rows(h), cols(pc))] for h in range(2)]
+
+    def z_copies(pc, off):
+        parts = z_parts(pc, me_z)
+        return [rdma(p, p, m.z_s.at[pc, off - 1, i], m.z_r.at[pc, off - 1, i], z_dev(off)) for i, p in enumerate(parts)]
+
+    def all_do(copies, do):
+        for copy in copies:
+            getattr(copy, do)()
+
+    order = [list(range(NB)), list(reversed(range(NB)))]
 
     inner = jnp.logical_and(me_z > 0, me_z < T - 1)
     line_sends = ((2, me_z >= 0), (1, me_z < T - 1), (3, me_z > 0))
 
     def z_landed(pc, off):
-        part = wall.at[(lax.rem(me_z - off + T, T),) + mine + (every, cols(pc))]
-        rdma(part, part, m.z_s.at[pc, off - 1], m.z_r.at[pc, off - 1], z_dev(off)).wait_recv()
+        for i, p in enumerate(z_parts(pc, lax.rem(me_z - off + T, T))):
+            rdma(p, p, m.z_s.at[pc, off - 1, i], m.z_r.at[pc, off - 1, i], z_dev(off)).wait_recv()
 
     def z_forward(pc):
-        part = wall.at[(lax.rem(me_z + 2, T),) + mine + (every, cols(pc))]
         up = lax.rem(me_z + 1, 2)
-        return rdma(part, part, m.z_f.at[pc], m.z_r.at[pc, 2 * up], tag_z((dpi, me_z + 2 * up - 1)))
-
-    order = [list(range(NB)), list(reversed(range(NB)))]
+        dev = tag_z((dpi, me_z + 2 * up - 1))
+        parts = z_parts(pc, lax.rem(me_z + 2, T))
+        return [rdma(p, p, m.z_f.at[pc, i], m.z_r.at[pc, 2 * up, i], dev) for i, p in enumerate(parts)]
 
     def half_z(h):
         return pl.ds(h * TH, TH)
@@ -179,8 +195,23 @@
         fixed = {k: mybit[k] for k in order[h][step:]}
         if landing:
             fixed[b] = 1 - mybit[b]
-        part = wall.at[(half_z(h),) + place(fixed) + (every, cols(pc))]
+        if pc in mixed:
+            part = wall.at[(every if step else me_z,) + place(fixed) + (half_rows(h), cols(pc))]
+        else:
+            part = wall.at[(half_z(h),) + place(fixed) + (every, cols(pc))]
         return rdma(part, part, m.p_s.at[pc, step, h], m.p_r.at[pc, step, h], bit_dev(b))
+
+    def z_begin(pc):
+        for off, allowed in line_sends:
+            @pl.when(allowed)
+            def _():
+                all_do(z_copies(pc, off), "start")
+
+    def z_pass(pc):
+        @pl.when(inner)
+        def _():
+            z_landed(pc, 2)
+            all_do(z_forward(pc), "start")
 
     def gather_stage(pc, s):
         if not 0 <= pc < NP:
@@ -189,24 +220,35 @@
             core_local(pc).wait()
             other = wall.at[(me_z,) + mine + (core_rows(1 - core), cols(pc))]
             rdma(other, other, m.c_s.at[pc], m.c_r.at[pc], partner).wait_recv()
-            for off, allowed in line_sends:
-                @pl.when(allowed)
-                def _():
-                    z_copy(pc, off).start()
+            if pc in mixed:
+                for h in range(2):
+                    p_copy(pc, 0, h, False).start()
+            else:
+                z_begin(pc)
+            return
+        if pc in mixed and s < NB:
+            if s == -1:
+                for h in range(2):
+                    p_copy(pc, 0, h, True).wait_recv()
+                z_begin(pc)
+            else:
+                z_pass(pc)
             return
         if s == -1:
-            @pl.when(inner)
-            def _():
-                z_landed(pc, 2)
-                z_forward(pc).start()
+            z_pass(pc)
             return
-        if s == 1:
+        if s == (NB if pc in mixed else 1):
             z_landed(pc, 1)
             z_landed(pc, 3)
 
             @pl.when(jnp.logical_not(inner))
             def _():
                 z_landed(pc, 2)
+
+            if pc in mixed:
+                for h in range(2):
+                    p_copy(pc, 1, h, False).start()
+                return
         for h in range(2):
             if s > 1:
                 p_copy(pc, s - 2, h, True).wait_recv()
@@ -217,6 +259,8 @@
     starts += [(pc + 1.1 * (s - 1), pc, s) for pc in range(NP) for s in range(1, NB + 1)]
     if NB == 2:
         starts[starts.index((4 + 1.1, 4, 2))] = (4.95, 4, 2)
+    keys = {0: -3.2, -1: -2.2, 1: 0.06, 2: 1.05}
+    starts = [(pc + keys[s], pc, s) if pc in mixed else (key, pc, s) for key, pc, s in starts]
     starts.sort()
 
     here = [0]
@@ -236,11 +280,11 @@
             for off, allowed in line_sends:
                 @pl.when(allowed)
                 def _():
-                    z_copy(pc, off).wait_send()
+                    all_do(z_copies(pc, off), "wait_send")
 
             @pl.when(inner)
             def _():
-                z_forward(pc).wait_send()
+                all_do(z_forward(pc), "wait_send")
 
             for step in range(NB):
                 for h in range(2):
@@ -1145,10 +1189,10 @@
     small = 4 * NB + 6 * T + 2 * NC + 8
     reg = pltpu.SemaphoreType.REGULAR
     scratch.update(
-        c_s=dma((NP,)), c_r=dma((NP,)), c_l=dma((NP,)), z_s=dma((NP, T - 1)), z_r=dma((NP, T - 1)),
+        c_s=dma((NP,)), c_r=dma((NP,)), c_l=dma((NP,)), z_s=dma((NP, T - 1, 2)), z_r=dma((NP, T - 1, 2)),
         p_s=dma((NP, NB, 2)), p_r=dma((NP, NB, 2)), x_s=dma((2, 2)), x_r=dma((2, T)), x_l=dma((2,)), x_f=dma((2, 2)),
         e_s=dma((4, NCH)), e_r=dma((4, NCH)), rs_s=dma((NP, NB, 2)), rs_r=dma((NP, NB, 2)), free=reg((NB, 2)), took=reg,
-        rz_s=dma((NP, T - 1, NC)), rz_r=dma((NP, T - 1, NC)), rx_s=dma((NP, NC)), rx_r=dma((NP, NC)), zfree=reg, f_s=dma((NP,)), f_r=dma((NP,)), z_f=dma((NP,)),
+        rz_s=dma((NP, T - 1, NC)), rz_r=dma((NP, T - 1, NC)), rx_s=dma((NP, NC)), rx_r=dma((NP, NC)), zfree=reg, f_s=dma((NP,)), f_r=dma((NP,)), z_f=dma((NP, 2)),
         o_s=dma((2, T)), o_r=dma((2, 2)), o_l=dma((2,)), s_s=dma((small,)), s_r=dma((small,)),
     )
     names = tuple(ins) + tuple(outs) + tuple(scratch)

time: 288 us -> 287 us (level)
  no operation moved by 1% of the time
where the time goes in v6:
time: 287 us; the launch traced here: 284 us
  Pallas kernels  258 us (90%)
  local copies, waits for them, and re-layouts  15.3 us (5%)
  other arithmetic  7.95 us (3%)
    pallas_call x1, Pallas kernels, block_call(): pl.pallas_call(functools.partial(block_kernel, dm, names), out_shape=tupl...  258 us

profile of v6, /device:TPU:24, one launch (start us, length us, event | category | flops | bytes accessed | tf_op | source)
XLA Modules:
  0.0 284.5 jit_solution(5462576853073994620)
XLA Ops:
  0.6 1.8 convert_element_type.78
  2.5 0.0 copy-start.1
  2.5 0.2 copy.43
  2.7 0.9 pad.39.refs_4_
  3.6 0.5 copy-done.1
  4.1 0.5 convert_element_type.79
  4.6 0.0 copy-start.9
  4.6 0.0 copy-start.14
  4.6 0.0 copy-start.17
  4.6 0.0 copy-start.13
  4.6 0.0 copy-start.10
  4.6 0.0 copy-start.11
  4.6 0.0 copy-start.12
  4.6 0.0 copy-start.16
  4.7 0.2 copy.44
  4.8 0.9 pad.40.refs_5_
  5.8 0.1 reshape.120
  5.9 0.1 reshape.121
  6.0 0.6 pad.42.refs_6_
  6.6 0.0 copy-done.14
  6.6 0.0 copy-start.19
  6.6 0.2 fusion.19
  6.8 0.1 broadcast_select_fusion.1
  6.9 0.1 convert_element_type.82
  7.0 0.0 copy-done.10
  7.0 0.1 broadcast_in_dim.82
  7.1 0.1 broadcast_in_dim.78
  7.2 0.1 broadcast_in_dim.79
  7.3 0.1 copy.45
  7.4 0.1 broadcast_select_fusion
  7.5 0.1 convert_element_type.81
  7.6 0.6 select_maximum_fusion.refs_7_
  8.3 0.6 maximum_convert_fusion
  8.9 257.7 %shard_map.246 = (f32[3,128,256]{2,1,0:T(8,128)}, f32[256,128]{1,0:T(8,128)}, f32[128,1024]{1,0:T(8,128)}, f32[1024,128]{1,0:T(8,128)}, bf16[2,176,1024]{2,1,0:T...) custom-call(bf16[3,128,256]{2,1,0:T(8,128)(2,1)} %refs_0_.1, ...), custom_call_target="tpu_custom_call" | custom-call | flops 30000001024 | bytes 10000000 | tf_op jit(solution)/shard_map/pallas_call | solution.py:1199
  266.6 0.0 copy-start
  266.6 2.9 %copy_bitcast_fusion = (bf16[176,2,1024]{2,1,0:T(2,128)(2,1)S(1)}, bf16[176,2,1024]{2,1,0:T(2,128)(2,1)S(1)}) fusion(bf16[2,176,1024]{2,1,0:T(8,128)(2,1)} %get-tuple-element.24, bf16[2,176,1024]{2,1,0:T(8,128)(2,1)} %get-tuple-element.23), kind=kLoop, calls=%fused_computation.4 | loop fusion | bytes 2883584 | tf_op jit(solution)/shard_map/transpose | solution.py:1292
  269.6 0.0 copy-start.2
  269.6 1.8 fusion.1
  271.4 0.0 copy-done.2
  271.4 0.0 copy-start.20
  271.4 1.8 fusion
  273.2 0.1 reshape.123
  273.3 0.1 copy.52
  273.4 0.1 eq.39
  273.5 0.0 copy-done.18
  273.5 1.0 fusion.4
  274.5 1.2 fusion.8
  275.7 0.6 convert_reduce_fusion
  276.3 0.7 slice_bitcast_fusion
  277.0 0.1 reshape.124
  277.1 0.7 constant_dynamic-slice_fusion
  277.8 0.6 dynamic-slice_bitcast_fusion
  278.4 0.8 slice_reduce_fusion
  279.2 0.1 reshape_squeeze.3
  279.3 0.1 constant_dynamic-slice_fusion.1
  279.3 0.7 copy.51
  280.0 1.3 dynamic-slice_bitcast_fusion.1
  281.3 0.7 copy.59
  282.0 0.0 copy-done.7
  282.0 0.7 copy.60
  282.7 0.0 copy-done.4
  282.7 0.8 copy.61
  283.5 0.0 copy-done.3
  283.5 0.8 copy.62
  (32 shorter events, 0.1 us)
Async XLA Ops:
  2.5 1.6 copy-start.1
  4.6 1.2 copy-start.9
  4.6 2.0 copy-start.14
  4.6 2.0 copy-start.17
  4.6 2.2 copy-start.13
  4.6 2.4 copy-start.10
  4.6 2.7 copy-start.11
  4.6 3.6 %copy-start.12 = (bf16[6,128]{1,0:T(8,128)(2,1)S(1)}, bf16[6,128]{1,0:T(8,128)(2,1)}, u32[]{:S(2)}) copy-start(bf16[6,128]{1,0:T(8,128)(2,1)} %param.21) | copy-start | bytes 4612
  4.6 3.6 %copy-start.16 = (bf16[2,128]{1,0:T(2,128)(2,1)S(1)}, bf16[2,128]{1,0:T(2,128)(2,1)}, u32[]{:S(2)}) copy-start(bf16[2,128]{1,0:T(2,128)(2,1)} %param.29) | copy-start | bytes 1540
  6.6 0.6 copy-start.19
  266.6 2.9 %copy-start = (f32[2,170,1024]{2,0,1:T(2,128)S(1)}, f32[2,170,1024]{2,0,1:T(2,128)}, u32[]{:S(2)}) copy-start(f32[2,170,1024]{2,0,1:T(2,128)} %param.15) | copy-start | bytes 4177924
  269.6 1.8 copy-start.2
  271.4 1.8 copy-start.15
  271.4 2.1 copy-start.8
  271.4 2.1 copy-start.18
  271.4 2.1 copy-start.20
  271.4 3.1 %copy-start.6 = (f32[8,32,128]{2,1,0:T(8,128)S(1)}, f32[8,32,128]{2,1,0:T(8,128)}, u32[]{:S(2)}) copy-start(f32[8,32,128]{2,1,0:T(8,128)} %get-tuple-element.27) | copy-start | bytes 393220
  273.2 8.1 %copy-start.5 = (f32[3,128,256]{2,1,0:T(8,128)S(1)}, f32[3,128,256]{2,1,0:T(8,128)}, u32[]{:S(2)}) copy-start(f32[3,128,256]{2,1,0:T(8,128)} %get-tuple-element.53) | copy-start | bytes 1179652
  273.2 8.8 %copy-start.7 = (f32[256,128]{1,0:T(8,128)S(1)}, f32[256,128]{1,0:T(8,128)}, u32[]{:S(2)}) copy-start(f32[256,128]{1,0:T(8,128)} %get-tuple-element.56) | copy-start | bytes 393220
  273.2 9.5 %copy-start.4 = (f32[128,1024]{1,0:T(8,128)S(1)}, f32[128,1024]{1,0:T(8,128)}, u32[]{:S(2)}) copy-start(f32[128,1024]{1,0:T(8,128)} %get-tuple-element.57) | copy-start | bytes 1572868
  274.5 9.0 %copy-start.3 = (f32[1024,128]{1,0:T(8,128)S(1)}, f32[1024,128]{1,0:T(8,128)}, u32[]{:S(2)}) copy-start(f32[1024,128]{1,0:T(8,128)} %get-tuple-element.59) | copy-start | bytes 1572868
